TPU v7x, 128 devices: a whole 4x4x4 slice. The times are simulated.
128 devices in a mesh: ctx: 8 (over x, z_lo), rows: 16 (over z_hi, y, core).
Axes of the slice: x: 4, y: 4, z: 4 (z_hi: 2, z_lo: 2; z = z_hi * 2 + z_lo), core: 2. Of those that a mesh axis runs over, the one named last changes fastest.
Arguments:
- queries: bfloat16 [16384, 4096], P('ctx', 'rows'), as said below
- keys: bfloat16 [16384, 1024], P('ctx'), as said below
- values: bfloat16 [16384, 1024], P('ctx'), may hold values from -6 to 6
- verticals: int32 [32, 8], P('rows'), may hold values from 0 to 127
- slashes: int32 [32, 16], P('rows'), may hold values from 1 to 127
- destination: int32 [16384], P('ctx'), may hold values from 0 to 16383, as said below
Outputs:
- remapped: bfloat16 [16384, 4096], P(('ctx', 'rows'))
Inputs may be any that keep to these rules, and one draw needn't show every extreme that they name: queries lie within -9 to 9. keys lie within -4 to 4. destination is a permutation of the 16384 rows; within each aligned block of 128 output rows the tokens stand in ascending order; of the 2048 tokens of one aligned token shard at most 32 go to one such block, and in every draw some shard sends exactly 32 to some block.
All inputs are finite; a program needn't handle non-finite values.
Results may differ from a plain program's by a relative error of at most 0.018.
Values may be sent and summed in bfloat16 or wider, within the bound.
No kernel may reach another device: no remote copies, remote signals or barrier semaphores. Data moves between devices by JAX's collectives and lax.ppermute only.
A program may use at most 320 MiB of HBM per device.

v0:
```python
import jax
import jax.numpy as jnp
from jax import lax
from jax.sharding import PartitionSpec as P

HEADS = 32
KV_HEADS = 8
DH = 128
BLOCK = 128


NEG = -1e30
row_ceiling = 1 << 30


def sparse_visit(carry, query_rows, key_rows, value_rows, query_start, verticals, slashes):
    out_sum, row_max, row_total = carry
    count = query_rows.shape[0]
    heads = verticals.shape[0]
    width = key_rows.shape[1]
    query_nblk = count // BLOCK
    key_nblk = key_rows.shape[0] // BLOCK
    query_blocks = query_start // BLOCK + jnp.arange(query_nblk, dtype=jnp.int32)
    diagonal = jnp.broadcast_to(query_blocks[None, :, None], (heads, query_nblk, 1))
    vertical = jnp.broadcast_to(verticals[:, None, :], (heads, query_nblk, verticals.shape[1]))
    slash = query_blocks[None, :, None] - slashes[:, None, :]
    candidate = jnp.concatenate([diagonal, vertical, slash], axis=2)
    slots = candidate.shape[2]
    inside = (candidate >= 0) & (candidate < key_nblk)
    order = jnp.arange(slots, dtype=jnp.int32)
    earlier = order[None, :] < order[:, None]
    repeated = jnp.any(
        (candidate[:, :, :, None] == candidate[:, :, None, :]) & earlier[None, None], axis=3
    )
    valid = inside & jnp.logical_not(repeated)
    index = jnp.clip(candidate, 0, key_nblk - 1)
    key_blocks = key_rows.reshape(key_nblk, BLOCK, width)
    value_blocks = value_rows.reshape(key_nblk, BLOCK, width)
    query_heads = jnp.transpose(query_rows.reshape(query_nblk, BLOCK, heads, width), (2, 0, 1, 3))
    query_pos = (query_start + jnp.arange(count, dtype=jnp.int32)).reshape(query_nblk, BLOCK)
    within = jnp.arange(BLOCK, dtype=jnp.int32)
    old_out = jnp.transpose(out_sum.reshape(count, heads, width), (1, 0, 2))

    def per_head(inputs):
        query_head_slot, head_index, head_valid, head_cand, head_max, head_total, head_out = inputs
        collected_keys = key_blocks[head_index]
        gathered_values = value_blocks[head_index]
        scores = jnp.einsum(
            "hxt,hawt->hxaw", query_head_slot, collected_keys, preferred_element_type=jnp.float32
        ) * width ** (-0.5)
        key_pos = head_cand[:, :, None] * BLOCK + within[None, None, :]
        allowed = head_valid[:, None, :, None] & (
            key_pos[:, None, :, :] <= query_pos[:, :, None, None]
        )
        masked = jnp.where(allowed, scores, NEG)
        block_score_max = jnp.max(masked, axis=(2, 3)).reshape(count)
        new_max = jnp.maximum(head_max, block_score_max)
        shaped_max = new_max.reshape(query_nblk, BLOCK, 1, 1)
        weights = jnp.where(allowed, jnp.exp(scores - shaped_max), 0.0)
        factor = jnp.exp(head_max - new_max)
        new_total = factor * head_total + jnp.sum(weights, axis=(2, 3)).reshape(count)
        mixed = jnp.einsum(
            "rylo,rlox->ryx",
            weights.astype(jnp.bfloat16),
            gathered_values,
            preferred_element_type=jnp.float32,
        ).reshape(count, width)
        return (head_out * factor[:, None] + mixed, new_max, new_total)

    new_out, new_max, new_total = lax.map(
        per_head, (query_heads, index, valid, candidate, row_max, row_total, old_out)
    )
    return (jnp.transpose(new_out, (1, 0, 2)).reshape(count, heads * width), new_max, new_total)


def visit(carry, query_rows, key_rows, value_rows, query_start, verticals, slashes):
    return sparse_visit(carry, query_rows, key_rows, value_rows, query_start, verticals, slashes)


def body(queries, keys, values, verticals, slashes, destination):
    cycle = lax.axis_size("ctx")
    groups = lax.axis_size("rows")
    place = lax.axis_index("ctx")
    group = lax.axis_index("rows")
    rows_here = queries.shape[0]
    heads = verticals.shape[0]
    width = DH
    share = HEADS // KV_HEADS
    kv_index = group * heads // share
    own_keys = lax.dynamic_slice_in_dim(keys, kv_index * width, width, 1)
    own_values = lax.dynamic_slice_in_dim(values, kv_index * width, width, 1)
    initial = (
        jnp.zeros((rows_here, heads * width), jnp.float32),
        jnp.full((heads, rows_here), NEG, jnp.float32),
        jnp.zeros((heads, rows_here), jnp.float32),
    )
    my_start = place * rows_here
    carry = visit(
        initial,
        queries,
        lax.all_gather(own_keys, "ctx", axis=0, tiled=True),
        lax.all_gather(own_values, "ctx", axis=0, tiled=True),
        my_start,
        verticals,
        slashes,
    )
    out_sum, row_max, row_total = carry
    normalized_output = out_sum.reshape(rows_here, heads, width) / row_total.T[:, :, None]
    attended = normalized_output.reshape(rows_here, heads * width).astype(jnp.bfloat16)
    devices = cycle * groups
    own_rows = rows_here // groups
    capacity = 2 * rows_here // devices
    owner_self = place * groups + group
    owner = destination // own_rows
    slots = jnp.arange(devices, dtype=jnp.int32)
    member = owner[:, None] == slots[None, :]
    first_row = jnp.min(jnp.where(member, destination[:, None], row_ceiling), axis=0)
    counts = jnp.sum(member.astype(jnp.int32), axis=0)
    token_first = jnp.sum(jnp.where(member, first_row[None, :], 0), axis=1)
    position = destination - token_first
    outgoing = (
        jnp.zeros((devices, capacity, attended.shape[1]), jnp.bfloat16)
        .at[owner, position]
        .set(attended)
    )
    incoming = lax.all_to_all(outgoing, ("ctx", "rows"), split_axis=0, concat_axis=0, tiled=True)
    shard_counts = lax.all_gather(counts[None, :], "ctx", axis=0, tiled=True)
    mine = lax.dynamic_index_in_dim(shard_counts, owner_self, 1, keepdims=False)
    start_offsets = jnp.cumsum(mine) - mine
    ends = start_offsets + mine
    local_rows = jnp.arange(own_rows, dtype=jnp.int32)
    source_shard = jnp.sum((local_rows[:, None] >= ends[None, :]).astype(jnp.int32), axis=1)
    shard_pick = source_shard[:, None] == jnp.arange(cycle, dtype=jnp.int32)[None, :]
    offset_rows = local_rows - jnp.sum(jnp.where(shard_pick, start_offsets[None, :], 0), axis=1)
    arranged = incoming.reshape(cycle, groups, capacity, attended.shape[1])[
        source_shard, :, offset_rows, :
    ]
    return arranged.reshape(own_rows, groups * attended.shape[1])


def solution(mesh):
    placed = (
        P("ctx", "rows"),
        P("ctx", None),
        P("ctx", None),
        P("rows", None),
        P("rows", None),
        P("ctx"),
    )
    return jax.shard_map(
        body, mesh=mesh, in_specs=placed, out_specs=P(("ctx", "rows"), None), check_vma=False
    )
```

profile of v0, /device:TPU:1, one launch (start us, length us, event | category | flops | bytes accessed | tf_op | source)
XLA Modules:
  0.0 416.3 jit_solution(17746267828694992741)
XLA Ops:
  6.5 0.0 all-gather.5.cloned.1.call-start
  6.5 1.9 constant_dynamic-slice_fusion.1
  8.4 0.0 all-gather.5.cloned.1.call-update
  8.4 0.0 all-gather.7.cloned.1.call-start
  8.5 1.9 constant_dynamic-slice_fusion
  10.4 0.0 all-gather.7.cloned.1.call-update
  10.4 0.8 broadcast_subtract_fusion
  11.2 0.7 broadcast_in_dim.75
  12.0 0.1 copy.25
  12.0 1.1 and_reduce_fusion
  13.1 0.1 copy.27
  13.2 0.1 copy.30
  13.3 1.3 reshape.287
  14.7 0.2 copy.43
  14.9 0.7 compare_select_fusion.2
  15.6 3.1 convert_reduce_fusion
  18.7 0.6 select_reduce_fusion.1
  19.4 0.7 compare_select_fusion.1
  20.1 0.7 multiply_reduce_fusion
  20.8 0.8 and_reduce_fusion.1
  21.6 0.6 broadcast_select_fusion
  22.2 79.9 %all-gather.5.cloned.1.call-done = bf16[16384,128]{1,0:T(8,128)(2,1)} async-done(((bf16[2048,128]{1,0:T(8,128)(2,1)}), bf16[16384,128]{1,0:T(8,128)(2,1)}) %all-gather.5.cloned.1.call-update) | async-done | bytes 4194320 | tf_op jit(solution)/shard_map/all_gather | solution.py:101
  102.1 94.0 %all-gather.7.cloned.1.call-done = bf16[16384,128]{1,0:T(8,128)(2,1)} async-done(((bf16[2048,128]{1,0:T(8,128)(2,1)}), bf16[16384,128]{1,0:T(8,128)(2,1)}) %all-gather.7.cloned.1.call-update) | async-done | bytes 4194320 | tf_op jit(solution)/shard_map/all_gather | solution.py:102
  196.0 148.2 %while.13 = (s32[]{:T(128)}, f32[2,2048,128]{1,2,0:T(8,128)}, f32[2,2048]{1,0:T(2,128)S(1)}, pred[2,16,25]{2,1,0:T(8,128)(4,1)S(1)}, s32[2,16,25]{2,1,0:T(8,128)...) while((s32[]{:T(128)}, f32[2,2048,128]{1,2,0:T(8,128)}, ...), condition=%wide.region_6.7_spmd.clone, body=%wide.region_3.6_spmd.clone.sunk | while | flops 3467178496 | bytes 271048544 | solution.py:70
  196.0 0.1 reshape.301
  196.1 14.6 %gather_fusion.1 = bf16[400,128,128]{2,1,0:T(8,128)(2,1)} fusion(bf16[128,128,128]{2,1,0:T(8,128)(2,1)} %get-tuple-element.259, s32[1024]{0:T(1024)S(1)} %pad_clamp_fusion.2), kind=kCustom, calls=%fused_computation.clone.clone.1 | custom fusion | bytes 26216000 | tf_op jit(solution)/shard_map/while/body/eval_jaxpr/gather | solution.py:46
  210.8 0.1 iota_add_fusion.3
  210.9 10.9 %select_reduce_fusion.5 = (f32[16,128]{1,0:T(8,128)S(1)}, f32[16,128,25,128]{1,3,2,0:T(8,128)S(1)}) fusion(s32[16,128]{1,0:T(8,128)S(1)} %add_bitcast_fusion.2, s32[16,25,128]{2,1,0:T(8,128)S(1)} %iota_add_fusion.3, pred[16,25]{1,0:T(8,128)(4,1)S(1)} %dynamic-slice_bitcast_fusion.2, bf16[16,25,128,128]{3,2,1,0:T(8,128)(2,1)} %bitcast.91, ...), kind=kOutput, calls=%fused_computation.7.clone.2 | convolution fusion | flops 1710487552 | bytes 40126468 | tf_op jit(solution)/shard_map/while/body/eval_jaxpr/hxt,hawt->hxaw/dot_general | solution.py:48
  221.8 0.0 copy-start
  221.8 12.0 %fusion.44 = f32[16,128]{1,0:T(8,128)S(1)} fusion(f32[16,128,25,128]{1,3,2,0:T(8,128)S(1)} %get-tuple-element.224, f32[16,128]{1,0:T(8,128)S(1)} %broadcast_maximum_fusion.2, s32[16,128]{1,0:T(8,128)S(1)} %add_bitcast_fusion.2, s32[16,25,128]{2,1,0:T(8,128)S(1)} %iota_add_fusion.3, pred[16,25]{1,0:T(8,128)(4,1)S(1)} %dynamic-slice_bitcast_fusion.2), kind=kLoop, calls=%fused_computation.9.clone.1 | loop fusion | flops 39319552 | bytes 26444176 | tf_op jit(solution)/shard_map/while/body/eval_jaxpr/reduce_sum | solution.py:61
  233.8 0.0 copy-done
  233.8 14.6 %gather_fusion = bf16[400,128,128]{2,1,0:T(8,128)(2,1)} fusion(bf16[128,128,128]{2,1,0:T(8,128)(2,1)} %get-tuple-element.260, s32[1024]{0:T(1024)S(1)} %pad_clamp_fusion.2), kind=kCustom, calls=%fused_computation.1.clone.clone.1 | custom fusion | bytes 26216000 | tf_op jit(solution)/shard_map/while/body/eval_jaxpr/gather | solution.py:47
  248.5 19.8 %fusion.43 = f32[16,128,128,1]{2,1,3,0:T(8,128)S(1)} fusion(bf16[16,25,128,128]{3,2,1,0:T(8,128)(2,1)} %bitcast.92, f32[16,128,25,128]{1,3,2,0:T(8,128)} %copy-done, f32[16,128]{1,0:T(8,128)S(1)} %broadcast_maximum_fusion.2, s32[16,128]{1,0:T(8,128)S(1)} %add_bitcast_fusion.2, s32[16,25,128]{2,1,0:T(8,128)S(1)} %iota_add_fusion.3, ...), kind=kOutput, calls=%fused_computation.11.clone.2 | convolution fusion | flops 1717043200 | bytes 40591760 | tf_op jit(solution)/shard_map/while/body/eval_jaxpr/rylo,rlox->ryx/dot_general | solution.py:62
  268.3 0.3 broadcast_add_fusion.2
  268.6 0.3 copy.45
  269.0 1.1 constant_dynamic-update-slice_fusion.2
  270.0 0.1 dynamic_update_slice.14
  270.1 0.1 reshape.301
  270.2 14.6 %gather_fusion.1 = bf16[400,128,128]{2,1,0:T(8,128)(2,1)} fusion(bf16[128,128,128]{2,1,0:T(8,128)(2,1)} %get-tuple-element.259, s32[1024]{0:T(1024)S(1)} %pad_clamp_fusion.2), kind=kCustom, calls=%fused_computation.clone.clone.1 | custom fusion | bytes 26216000 | tf_op jit(solution)/shard_map/while/body/eval_jaxpr/gather | solution.py:46
  284.9 0.1 iota_add_fusion.3
  285.0 10.9 %select_reduce_fusion.5 = (f32[16,128]{1,0:T(8,128)S(1)}, f32[16,128,25,128]{1,3,2,0:T(8,128)S(1)}) fusion(s32[16,128]{1,0:T(8,128)S(1)} %add_bitcast_fusion.2, s32[16,25,128]{2,1,0:T(8,128)S(1)} %iota_add_fusion.3, pred[16,25]{1,0:T(8,128)(4,1)S(1)} %dynamic-slice_bitcast_fusion.2, bf16[16,25,128,128]{3,2,1,0:T(8,128)(2,1)} %bitcast.91, ...), kind=kOutput, calls=%fused_computation.7.clone.2 | convolution fusion | flops 1710487552 | bytes 40126468 | tf_op jit(solution)/shard_map/while/body/eval_jaxpr/hxt,hawt->hxaw/dot_general | solution.py:48
  295.9 0.0 copy-start
  295.9 12.0 %fusion.44 = f32[16,128]{1,0:T(8,128)S(1)} fusion(f32[16,128,25,128]{1,3,2,0:T(8,128)S(1)} %get-tuple-element.224, f32[16,128]{1,0:T(8,128)S(1)} %broadcast_maximum_fusion.2, s32[16,128]{1,0:T(8,128)S(1)} %add_bitcast_fusion.2, s32[16,25,128]{2,1,0:T(8,128)S(1)} %iota_add_fusion.3, pred[16,25]{1,0:T(8,128)(4,1)S(1)} %dynamic-slice_bitcast_fusion.2), kind=kLoop, calls=%fused_computation.9.clone.1 | loop fusion | flops 39319552 | bytes 26444176 | tf_op jit(solution)/shard_map/while/body/eval_jaxpr/reduce_sum | solution.py:61
  307.9 0.0 copy-done
  308.0 14.7 %gather_fusion = bf16[400,128,128]{2,1,0:T(8,128)(2,1)} fusion(bf16[128,128,128]{2,1,0:T(8,128)(2,1)} %get-tuple-element.260, s32[1024]{0:T(1024)S(1)} %pad_clamp_fusion.2), kind=kCustom, calls=%fused_computation.1.clone.clone.1 | custom fusion | bytes 26216000 | tf_op jit(solution)/shard_map/while/body/eval_jaxpr/gather | solution.py:47
  322.6 19.8 %fusion.43 = f32[16,128,128,1]{2,1,3,0:T(8,128)S(1)} fusion(bf16[16,25,128,128]{3,2,1,0:T(8,128)(2,1)} %bitcast.92, f32[16,128,25,128]{1,3,2,0:T(8,128)} %copy-done, f32[16,128]{1,0:T(8,128)S(1)} %broadcast_maximum_fusion.2, s32[16,128]{1,0:T(8,128)S(1)} %add_bitcast_fusion.2, s32[16,25,128]{2,1,0:T(8,128)S(1)} %iota_add_fusion.3, ...), kind=kOutput, calls=%fused_computation.11.clone.2 | convolution fusion | flops 1717043200 | bytes 40591760 | tf_op jit(solution)/shard_map/while/body/eval_jaxpr/rylo,rlox->ryx/dot_general | solution.py:62
  342.4 0.3 broadcast_add_fusion.2
  342.8 0.3 copy.45
  343.1 1.1 constant_dynamic-update-slice_fusion.2
  344.2 0.1 dynamic_update_slice.14
  344.2 1.8 fusion.17
  346.0 0.5 copy.32
  346.5 11.2 %scatter_custom_fusion = bf16[4096,256]{1,0:T(8,128)(2,1)} fusion(s32[2048]{0:T(1024)} %broadcast_select_fusion, bf16[2048,256]{1,0:T(8,128)(2,1)S(1)} %copy.32, bf16[]{:T(256)} %constant.68.clone.1), kind=kCustom, calls=%fused_computation.34 | custom fusion | bytes 2097664
  357.8 12.1 %all-to-all-start = ((bf16[128,32,256]{2,1,0:T(8,128)(2,1)}), bf16[128,32,256]{2,1,0:T(8,128)(2,1)S(1)}, u32[]{:S(2)}, u32[]{:S(2)}) async-start(bf16[128,32,256]{2,1,0:T(8,128)(2,1)} %bitcast.95), calls=%async_computation | async-start | bytes 4194304 | tf_op jit(solution)/shard_map/all_to_all | solution.py:126
  369.9 0.0 copy-done.1
  369.9 32.4 %all-gather.1 = s32[8,1,128]{2,1,0:T(1,128)S(1)} all-gather(s32[1,1,128]{2,1,0:T(1,128)S(1)} %bitcast.105), channel_id=2, replica_groups=mesh['ctx'=8,'rows'=16] {'ctx'}, dimensions={0}, use_global_device_ids=true | all-gather | bytes 4608 | tf_op jit(solution)/shard_map/all_gather | solution.py:127
  402.3 0.3 dynamic-slice_reduce_fusion
  402.6 0.2 reduce-window.7
  402.8 0.1 convert_reduce_fusion.1
  402.9 0.1 select_reduce_fusion.3
  403.0 0.0 all-to-all-done
  403.0 2.6 copy.33
  405.6 2.4 gather_fusion.2
  408.1 1.4 copy.41
  (24 shorter events, 0.2 us)
Async XLA Ops:
  6.5 95.5 %all-gather.5.cloned.1.call-start = ((), (), s32[]{:S(2)}) async-start(), calls=%async_computation.1 | async-start | bytes 4718592 | tf_op jit(solution)/shard_map/all_gather | solution.py:101
  8.4 187.6 %all-gather.7.cloned.1.call-start = ((), (), s32[]{:S(2)}) async-start(), calls=%async_computation.2 | async-start | bytes 4718592 | tf_op jit(solution)/shard_map/all_gather | solution.py:102
  196.0 173.9 %copy-start.1 = (s32[128]{0:T(128)S(1)}, s32[128]{0:T(128)}, u32[]{:S(2)}) copy-start(s32[128]{0:T(128)} %get-tuple-element.129) | copy-start | bytes 1540
  221.8 12.0 %copy-start = (f32[16,128,25,128]{1,3,2,0:T(8,128)}, f32[16,128,25,128]{1,3,2,0:T(8,128)S(1)}, u32[]{:S(2)}) copy-start(f32[16,128,25,128]{1,3,2,0:T(8,128)S(1)} %get-tuple-element.224) | copy-start | bytes 78643200 | tf_op jit(solution)/shard_map/while
  295.9 12.0 %copy-start = (f32[16,128,25,128]{1,3,2,0:T(8,128)}, f32[16,128,25,128]{1,3,2,0:T(8,128)S(1)}, u32[]{:S(2)}) copy-start(f32[16,128,25,128]{1,3,2,0:T(8,128)S(1)} %get-tuple-element.224) | copy-start | bytes 78643200 | tf_op jit(solution)/shard_map/while
  357.8 45.2 %all-to-all-start = ((bf16[128,32,256]{2,1,0:T(8,128)(2,1)}), bf16[128,32,256]{2,1,0:T(8,128)(2,1)S(1)}, u32[]{:S(2)}, u32[]{:S(2)}) async-start(bf16[128,32,256]{2,1,0:T(8,128)(2,1)} %bitcast.95), calls=%async_computation | async-start | bytes 4194304 | tf_op jit(solution)/shard_map/all_to_all | solution.py:126
Sparse Core Ops, SparseCore 0:
  9.0 93.0 all-gather.4
  103.7 92.2 all-gather.6
where the time goes:
time: 419 us; the launch traced here: 416 us
  waiting for transfers between devices  174 us (42%)
  local copies, waits for them, and re-layouts  86.5 us (21%)
  matrix products  61.3 us (15%)
  other arithmetic  36.3 us (9%)
  blocking collectives  32.4 us (8%)
  between operations  13.6 us (3%)
  starting transfers between devices  12.2 us (3%)
    all_gather x1, waiting for transfers between devices, body(): lax.all_gather(own_values, 'ctx', axis=0, tiled=True)  94 us
    all_gather x1, waiting for transfers between devices, body(): lax.all_gather(own_keys, 'ctx', axis=0, tiled=True)  79.9 us
    dot_general x2, matrix products, per_head(): jnp.einsum('rylo,rlox->ryx', weights.astype(jnp.bfloat16), gathered_value...  39.6 us
    all_gather x1, blocking collectives, body(): shard_counts = lax.all_gather(counts[None, :], 'ctx', axis=0, tiled=True)  32.4 us
    gather x2, local copies, waits for them, and re-layouts, per_head(): gathered_values = value_blocks[head_index]  29.3 us
    gather x2, local copies, waits for them, and re-layouts, per_head(): collected_keys = key_blocks[head_index]  29.2 us
    reduce_sum x2, other arithmetic, per_head(): jnp.sum(weights, axis=(2, 3)).reshape(count)  24 us
    dot_general x2, matrix products, per_head(): jnp.einsum('hxt,hawt->hxaw', query_head_slot, collected_keys, preferred_e...  21.7 us
  transfers between devices with their start and end apart: 3, of which 2 were waited for; matrix products, arithmetic and copies ran while one was open for 3% of the time, Pallas kernels for 0%

commit v1 on v0

v1 whole, which is shorter than its diff:
```python
import functools

import jax
import jax.numpy as jnp
from jax import lax
from jax.experimental import pallas as pl
from jax.experimental.pallas import tpu as pltpu
from jax.sharding import PartitionSpec as P

HEADS = 32
KV_HEADS = 8
DH = 128
BLOCK = 128
NEG = -1e30
ROW_CEILING = 1 << 30
EMPTY = 1048576.0
SCALE2 = DH**-0.5 * 1.4426950408889634
GROUP = 4
PIECE = {(0, 0): 0, (3, 0): 1, (1, 0): 2, (0, 1): 3, (2, 0): 4, (1, 1): 5, (3, 1): 6, (2, 1): 7}
ANY = pl.BlockSpec(memory_space=pl.ANY)
SMEM = pl.BlockSpec(memory_space=pltpu.SMEM)
VMEM = pl.BlockSpec(memory_space=pltpu.VMEM)


def dot_t(a, b):
    return lax.dot_general(a, b, (((1,), (1,)), ((), ())), preferred_element_type=jnp.float32)


def attend_kernel(pieces, slots, heads, meta, lists, counts, first_row, sent, q_ref, dest_ref, keys, values, *rest):
    mine, other = rest[: pieces - 1], rest[pieces - 1 : 2 * pieces - 2]
    out_ref, k_s, v_s, att, sem = rest[2 * pieces - 2 :]
    shard = q_ref.shape[0]
    nblk = shard // BLOCK
    core, kv = meta[0], meta[1]
    column = pl.ds(pl.multiple_of(kv * DH, DH), DH)

    def spot(ref, p):
        return ref.at[pl.ds(p * shard, shard)]

    pltpu.make_async_copy(keys.at[:, column], spot(k_s, 0), sem.at[0]).start()
    pltpu.make_async_copy(values.at[:, column], spot(v_s, 0), sem.at[pieces]).start()
    for p in range(1, pieces):

        @pl.when(core == 0)
        def _():
            pltpu.make_async_copy(mine[p - 1], spot(k_s, p), sem.at[p]).start()
            pltpu.make_async_copy(other[p - 1], spot(v_s, p), sem.at[pieces + p]).start()

        @pl.when(core != 0)
        def _():
            pltpu.make_async_copy(other[p - 1], spot(k_s, p), sem.at[p]).start()
            pltpu.make_async_copy(mine[p - 1], spot(v_s, p), sem.at[pieces + p]).start()

    pltpu.make_async_copy(keys.at[:, column], spot(k_s, 0), sem.at[0]).wait()
    pltpu.make_async_copy(values.at[:, column], spot(v_s, 0), sem.at[pieces]).wait()
    for p in range(1, pieces):
        pltpu.make_async_copy(mine[p - 1], spot(k_s, p), sem.at[p]).wait()
        pltpu.make_async_copy(mine[p - 1], spot(v_s, p), sem.at[pieces + p]).wait()

    def block_of(ref, index):
        return ref[pl.ds(pl.multiple_of(index * BLOCK, BLOCK), BLOCK), :]

    def per_block(qb, _):
        at = pl.ds(pl.multiple_of(qb * BLOCK, BLOCK), BLOCK)
        tri = lax.broadcasted_iota(jnp.int32, (BLOCK, BLOCK), 1) <= lax.broadcasted_iota(
            jnp.int32, (BLOCK, BLOCK), 0
        )
        for h in range(heads):
            query = q_ref[at, h * DH : (h + 1) * DH]
            row = h * nblk + qb
            count = counts[row]
            index = [lists[row, s] for s in range(slots)]
            parts = [jnp.where(tri, dot_t(query, block_of(k_s, qb)), NEG)]
            for base in range(0, slots, GROUP):
                block = jnp.concatenate([block_of(k_s, index[base + u]) for u in range(GROUP)], axis=0)
                scores = dot_t(query, block)
                for u in range(GROUP):
                    parts.append(
                        jnp.where(base + u < count, scores[:, u * BLOCK : (u + 1) * BLOCK], NEG)
                    )
            top = functools.reduce(jnp.maximum, parts)
            top = jnp.max(top, axis=1, keepdims=True)
            weights = jnp.exp2((parts[0] - top) * SCALE2)
            total = weights
            mixed = jnp.dot(
                weights.astype(jnp.bfloat16), block_of(v_s, qb), preferred_element_type=jnp.float32
            )
            for base in range(0, slots, GROUP):
                block = jnp.concatenate([block_of(v_s, index[base + u]) for u in range(GROUP)], axis=0)
                low = []
                for u in range(GROUP):
                    weights = jnp.exp2((parts[1 + base + u] - top) * SCALE2)
                    total = total + weights
                    low.append(weights.astype(jnp.bfloat16))
                mixed = mixed + jnp.dot(
                    jnp.concatenate(low, axis=1), block, preferred_element_type=jnp.float32
                )
            attended = mixed / jnp.sum(total, axis=1, keepdims=True)
            att[at, h * DH : (h + 1) * DH] = attended.astype(jnp.bfloat16)
        return 0

    lax.fori_loop(0, nblk, per_block, 0)
    scatter_rows(first_row, sent, dest_ref, att, out_ref)


def scatter_rows(first_row, sent, dest_ref, att, out_ref):
    shard, width = att.shape
    owners = first_row.shape[0]
    capacity = out_ref.shape[0] // owners
    batch = 16

    def per_batch(step, _):
        goal = dest_ref[...]
        place = lax.broadcasted_iota(jnp.int32, (capacity, shard), 0)
        hot = [
            jnp.where(goal - first_row[step * batch + u] == place, 1.0, 0.0).astype(jnp.bfloat16)
            for u in range(batch)
        ]
        rows = jnp.dot(jnp.concatenate(hot, axis=0), att[...], preferred_element_type=jnp.float32)
        line = lax.broadcasted_iota(jnp.int32, (capacity, width), 0)
        for u in range(batch):
            owner = step * batch + u
            kept = jnp.where(line < sent[owner], rows[u * capacity : (u + 1) * capacity], EMPTY)
            out_ref[pl.ds(pl.multiple_of(owner * capacity, capacity), capacity), :] = kept.astype(jnp.bfloat16)
        return 0

    lax.fori_loop(0, owners // batch, per_batch, 0)


def arrange_kernel(in_ref, out_ref, pick):
    shards, _, capacity, width = in_ref.shape
    slots = shards * capacity
    rows = out_ref.shape[0]
    block = in_ref[...].reshape(slots, width)

    @pl.when(pl.program_id(0) == 0)
    def _():
        used = jnp.where(block[:, :rows].astype(jnp.float32) < EMPTY / 2, 1.0, 0.0).astype(jnp.bfloat16)
        one = lax.broadcasted_iota(jnp.int32, (slots, slots), 0)
        two = lax.broadcasted_iota(jnp.int32, (slots, slots), 1)
        contract = (((0,), (0,)), ((), ()))
        before = lax.dot_general(
            used,
            jnp.where(one < two, 1.0, 0.0).astype(jnp.bfloat16),
            contract,
            preferred_element_type=jnp.float32,
        )
        here = lax.dot_general(
            used,
            jnp.where(one == two, 1.0, 0.0).astype(jnp.bfloat16),
            contract,
            preferred_element_type=jnp.float32,
        )
        line = lax.broadcasted_iota(jnp.int32, (rows, slots), 0).astype(jnp.float32)
        pick[...] = jnp.where((before == line) & (here > 0.5), 1.0, 0.0).astype(jnp.bfloat16)

    out_ref[...] = jnp.dot(pick[...], block, preferred_element_type=jnp.float32).astype(jnp.bfloat16)


def block_lists(verticals, slashes, place, nblk, nshards):
    heads = verticals.shape[0]
    query_blocks = place * nblk + jnp.arange(nblk, dtype=jnp.int32)
    vertical = jnp.broadcast_to(verticals[:, None, :], (heads, nblk, verticals.shape[1]))
    slash = query_blocks[None, :, None] - slashes[:, None, :]
    cand = jnp.concatenate([vertical, slash], axis=2)
    slots = cand.shape[2]
    order = jnp.arange(slots, dtype=jnp.int32)
    earlier = order[None, :] < order[:, None]
    repeated = jnp.any((cand[:, :, :, None] == cand[:, :, None, :]) & earlier[None, None], axis=3)
    valid = (cand >= 0) & (cand < query_blocks[None, :, None]) & jnp.logical_not(repeated)
    source = cand // nblk
    dx = (source // 2 - place // 2) % (nshards // 2)
    dz = (source - place) % 2
    piece = jnp.zeros_like(cand)
    for (ox, oz), number in PIECE.items():
        piece = jnp.where((dx == ox) & (dz == oz), number, piece)
    local = jnp.clip(piece * nblk + cand % nblk, 0, nshards * nblk - 1)
    rank = jnp.sum((valid[:, :, None, :] & earlier[None, None]).astype(jnp.int32), axis=3)
    chosen = valid[:, :, :, None] & (rank[:, :, :, None] == order)
    lists = jnp.sum(jnp.where(chosen, local[:, :, :, None], 0), axis=2)
    return lists.reshape(heads * nblk, slots), jnp.sum(valid.astype(jnp.int32), axis=2).reshape(heads * nblk)


def body(queries, keys, values, verticals, slashes, destination):
    cycle = lax.axis_size("ctx")
    groups = lax.axis_size("rows")
    place = lax.axis_index("ctx")
    group = lax.axis_index("rows")
    rows_here = queries.shape[0]
    heads = verticals.shape[0]
    nblk = rows_here // BLOCK
    devices = cycle * groups
    own_rows = rows_here // groups
    capacity = 2 * rows_here // devices
    kv_index = group * heads // (HEADS // KV_HEADS)
    core = group % 2

    own = jnp.where(
        core == 0,
        lax.dynamic_slice_in_dim(keys, kv_index * DH, DH, 1),
        lax.dynamic_slice_in_dim(values, kv_index * DH, DH, 1),
    )

    def along_x(x, step):
        return lax.ppermute(x, "ctx", [(c, (c + 2 * step) % cycle) for c in range(cycle)])

    def along_z(x):
        return lax.ppermute(x, "ctx", [(c, c ^ 1) for c in range(cycle)])

    def swap(x):
        return lax.ppermute(x, "rows", [(r, r ^ 1) for r in range(groups)])

    half = rows_here // 2
    p1 = along_x(own, 1)
    p2 = along_x(own, -1)
    p3 = along_z(own)
    p4 = along_x(p1, 1)
    p5 = along_x(p3, -1)
    p6 = along_z(p1)
    p7 = jnp.concatenate([along_x(p6[:half], 1), along_x(p5[half:], -1)], axis=0)
    mine = (p1, p2, p3, p4, p5, p6, p7)
    other = tuple(swap(x) for x in mine)

    lists, counts = block_lists(verticals, slashes, place, nblk, cycle)
    owner = destination // own_rows
    member = owner[:, None] == jnp.arange(devices, dtype=jnp.int32)[None, :]
    first_row = jnp.min(jnp.where(member, destination[:, None], ROW_CEILING), axis=0)
    sent = jnp.sum(member.astype(jnp.int32), axis=0)
    meta = jnp.stack([core, kv_index]).astype(jnp.int32)

    slots = lists.shape[1]
    outgoing = pl.pallas_call(
        functools.partial(attend_kernel, cycle, slots, heads),
        out_shape=jax.ShapeDtypeStruct((devices * capacity, heads * DH), jnp.bfloat16),
        in_specs=[SMEM] * 5 + [VMEM] * 2 + [ANY] * (2 + 2 * (cycle - 1)),
        out_specs=VMEM,
        scratch_shapes=[
            pltpu.VMEM((cycle * rows_here, DH), jnp.bfloat16),
            pltpu.VMEM((cycle * rows_here, DH), jnp.bfloat16),
            pltpu.VMEM((rows_here, heads * DH), jnp.bfloat16),
            pltpu.SemaphoreType.DMA((2 * cycle,)),
        ],
        compiler_params=pltpu.CompilerParams(vmem_limit_bytes=48 * 1024 * 1024),
        name="attend",
    )(meta, lists, counts, first_row, sent, queries, destination.reshape(1, rows_here), keys, values, *mine, *other)

    incoming = lax.all_to_all(
        outgoing.reshape(devices, capacity, heads * DH), ("ctx", "rows"), split_axis=0, concat_axis=0, tiled=True
    )
    incoming = incoming.reshape(cycle, groups, capacity, heads * DH)
    return pl.pallas_call(
        arrange_kernel,
        grid=(groups,),
        out_shape=jax.ShapeDtypeStruct((own_rows, groups * heads * DH), jnp.bfloat16),
        in_specs=[pl.BlockSpec((cycle, 1, capacity, heads * DH), lambda g: (0, g, 0, 0))],
        out_specs=pl.BlockSpec((own_rows, heads * DH), lambda g: (0, g)),
        scratch_shapes=[pltpu.VMEM((own_rows, cycle * capacity), jnp.bfloat16)],
        compiler_params=pltpu.CompilerParams(vmem_limit_bytes=32 * 1024 * 1024),
        name="arrange",
    )(incoming)


def solution(mesh):
    placed = (
        P("ctx", "rows"),
        P("ctx", None),
        P("ctx", None),
        P("rows", None),
        P("rows", None),
        P("ctx"),
    )
    return jax.shard_map(
        body, mesh=mesh, in_specs=placed, out_specs=P(("ctx", "rows"), None), check_vma=False
    )
```

time: 419 us -> 137 us (0.33)
  waiting for transfers between devices: 174 us -> 26.3 us
  local copies, waits for them, and re-layouts: 86.5 us -> 5.21 us
  matrix products: 61.3 us -> 0 us
  Pallas kernels: 0 us -> 44.4 us
  other arithmetic: 36.3 us -> 7.6 us
  between operations: 13.6 us -> 0.16 us
  blocking collectives: 32.4 us -> 37.4 us
    all_gather x2 -> x0, waiting for transfers between devices: 174 us -> none  [the longest x1 94 us: body(): lax.all_gather(own_values, 'ctx', axis=0, tiled=True)]
    dot_general x4 -> x0, matrix products: 61.3 us -> none  [the longest x2 39.6 us: per_head(): jnp.einsum('rylo,rlox->ryx', weights.astype(jnp.bfloat16), gathered_value...]
    gather x5 -> x0, local copies, waits for them, and re-layouts: 61 us -> none  [the longest x2 29.3 us: per_head(): gathered_values = value_blocks[head_index]]
    pallas_call x0 -> x2, Pallas kernels: none -> 44.4 us  [the longest x1 37.5 us: body(): pl.pallas_call(functools.partial(attend_kernel, cycle, slots, heads), out...]
    all_to_all x0 -> x1, blocking collectives: none -> 37.4 us  [body(): lax.all_to_all(outgoing.reshape(devices, capacity, heads * DH), ('ctx', '...]
    all_gather x1 -> x0, blocking collectives: 32.4 us -> none  [body(): shard_counts = lax.all_gather(counts[None, :], 'ctx', axis=0, tiled=True)]
    ppermute x0 -> x15, waiting for transfers between devices: none -> 26.3 us  [the longest x6 17.3 us: along_x(): lax.ppermute(x, 'ctx', [(c, (c + 2 * step) % cycle) for c in range(cycle)])]
    reduce_sum x6 -> x4, other arithmetic: 27.9 us -> 3.87 us  [the longest x1 2.55 us: body(): sent = jnp.sum(member.astype(jnp.int32), axis=0)]
  transfers between devices with their start and end apart: 3 -> 15, of which waited for: 2 -> 3; matrix products, arithmetic and copies ran while one was open for 3% -> 5% of each run, Pallas kernels for 0% -> 0%
where the time goes in v1:
time: 137 us; the launch traced here: 136 us
  Pallas kernels  44.4 us (32%)
  blocking collectives  37.4 us (27%)
  waiting for transfers between devices  26.3 us (19%)
  starting transfers between devices  15.1 us (11%)
  other arithmetic  7.6 us (6%)
  local copies, waits for them, and re-layouts  5.21 us (4%)
    pallas_call x1, Pallas kernels, body(): pl.pallas_call(functools.partial(attend_kernel, cycle, slots, heads), out...  37.5 us
    all_to_all x1, blocking collectives, body(): lax.all_to_all(outgoing.reshape(devices, capacity, heads * DH), ('ctx', '...  37.4 us
    ppermute x6, waiting for transfers between devices, along_x(): lax.ppermute(x, 'ctx', [(c, (c + 2 * step) % cycle) for c in range(cycle)])  17.3 us
    ppermute x2, waiting for transfers between devices, along_z(): return lax.ppermute(x, 'ctx', [(c, c ^ 1) for c in range(cycle)])  8.95 us
    ppermute x6, starting transfers between devices, along_x(): lax.ppermute(x, 'ctx', [(c, (c + 2 * step) % cycle) for c in range(cycle)])  6.95 us
    pallas_call x1, Pallas kernels, body(): pl.pallas_call(arrange_kernel, grid=(groups,), out_shape=jax.ShapeDtypeSt...  6.9 us
    unnamed x11, local copies, waits for them, and re-layouts  4.37 us
    ppermute x7, starting transfers between devices, swap(): return lax.ppermute(x, 'rows', [(r, r ^ 1) for r in range(groups)])  4.31 us
  transfers between devices with their start and end apart: 15, of which 3 were waited for; matrix products, arithmetic and copies ran while one was open for 5% of the time, Pallas kernels for 0%

profile of v1, /device:TPU:1, one launch (start us, length us, event | category | flops | bytes accessed | tf_op | source)
XLA Modules:
  0.0 136.2 jit_solution(2671501145742992586)
XLA Ops:
  0.0 1.4 dynamic-slice_select_fusion
  1.4 2.5 %collective-permute-start.2 = (bf16[2048,128]{1,0:T(8,128)(2,1)S(1)}, bf16[2048,128]{1,0:T(8,128)(2,1)S(1)}, u32[]{:S(2)}, u32[]{:S(2)}) collective-permute-start(bf16[2048,128]{1,0:T(8,128)(2,1)S(1)} %dynamic-slice_select_fusion), channel_id=1, source_target_pairs={{0,16},{16,0},{32,48},{48,32},{64,80},{80,64},{96,112},{112,96},{1... | collective-permute-start | bytes 1572872 | tf_op jit(solution)/shard_map/ppermute | solution.py:208
  3.9 1.2 collective-permute-start
  5.1 1.5 %collective-permute-start.1 = (bf16[2048,128]{1,0:T(8,128)(2,1)S(1)}, bf16[2048,128]{1,0:T(8,128)(2,1)S(1)}, u32[]{:S(2)}, u32[]{:S(2)}) collective-permute-start(bf16[2048,128]{1,0:T(8,128)(2,1)S(1)} %dynamic-slice_select_fusion), channel_id=1, source_target_pairs={{0,96},{16,112},{32,0},{48,16},{64,32},{80,48},{96,64},{112,80},{1... | collective-permute-start | bytes 1572872 | tf_op jit(solution)/shard_map/ppermute | solution.py:205
  6.6 8.9 %collective-permute-done.2.rest_2_ = bf16[2048,128]{1,0:T(8,128)(2,1)S(1)} collective-permute-done((bf16[2048,128]{1,0:T(8,128)(2,1)S(1)}, bf16[2048,128]{1,0:T(8,128)(2,1)S(1)}, u32[]{:S(2)}, u32[]{:S(2)}) %collective-permute-start.2) | collective-permute-done | bytes 524320 | tf_op jit(solution)/shard_map/ppermute | solution.py:208
  15.5 2.4 %collective-permute-start.4 = (bf16[2048,128]{1,0:T(8,128)(2,1)S(1)}, bf16[2048,128]{1,0:T(8,128)(2,1)S(1)}, u32[]{:S(2)}, u32[]{:S(2)}) collective-permute-start(bf16[2048,128]{1,0:T(8,128)(2,1)S(1)} %collective-permute-done.2.rest_2_), channel_id=1, source_target_pairs={{0,96},{16,112},{32,0},{48,16},{64,32},{80,48},{96,64},{112,80},{1... | collective-permute-start | bytes 1572872 | tf_op jit(solution)/shard_map/ppermute | solution.py:205
  17.9 0.0 collective-permute-done.rest_0_
  17.9 1.3 collective-permute-start.5
  19.2 0.7 broadcast_subtract_fusion
  19.9 0.7 broadcast_in_dim.62
  20.6 0.1 pad_add_fusion
  20.7 0.8 and_reduce_fusion
  21.5 2.2 %collective-permute-start.10 = (bf16[2048,128]{1,0:T(8,128)(2,1)S(1)}, bf16[2048,128]{1,0:T(8,128)(2,1)S(1)}, u32[]{:S(2)}, u32[]{:S(2)}) collective-permute-start(bf16[2048,128]{1,0:T(8,128)(2,1)S(1)} %collective-permute-done.2.rest_2_), channel_id=1, source_target_pairs={{0,1},{1,0},{2,3},{3,2},{4,5},{5,4},{6,7},{7,6},{8,9},{9,8},{10,11... | collective-permute-start | bytes 1572872 | tf_op jit(solution)/shard_map/ppermute | solution.py:211
  23.6 0.0 collective-permute-start.3
  23.6 0.0 collective-permute-done.1.rest_1_
  23.6 0.2 collective-permute-start.9
  23.8 5.6 %collective-permute-done.4.rest_4_ = bf16[2048,128]{1,0:T(8,128)(2,1)S(1)} collective-permute-done((bf16[2048,128]{1,0:T(8,128)(2,1)S(1)}, bf16[2048,128]{1,0:T(8,128)(2,1)S(1)}, u32[]{:S(2)}, u32[]{:S(2)}) %collective-permute-start.4) | collective-permute-done | bytes 524320 | tf_op jit(solution)/shard_map/ppermute | solution.py:205
  29.5 1.8 %collective-permute-start.7 = (bf16[1024,128]{1,0:T(8,128)(2,1)S(1)}, bf16[1024,128]{1,0:T(8,128)(2,1)S(1)}, u32[]{:S(2)}, u32[]{:S(2)}) collective-permute-start(bf16[1024,128]{1,0:T(8,128)(2,1)S(1)} %slice.9), channel_id=1, source_target_pairs={{0,96},{16,112},{32,0},{48,16},{64,32},{80,48},{96,64},{112,80},{1... | collective-permute-start | bytes 786440 | tf_op jit(solution)/shard_map/ppermute | solution.py:205
  31.3 0.0 collective-permute-done.5.rest_5_
  31.3 0.1 collective-permute-start.6
  31.4 0.2 convert_reduce_fusion.2
  31.6 0.6 convert_reduce_fusion.1
  32.3 11.7 %collective-permute-done.6 = bf16[1024,128]{1,0:T(8,128)(2,1)S(1)} collective-permute-done((bf16[1024,128]{1,0:T(8,128)(2,1)S(1)}, bf16[1024,128]{1,0:T(8,128)(2,1)S(1)}, u32[]{:S(2)}, u32[]{:S(2)}) %collective-permute-start.6) | collective-permute-done | bytes 262176 | tf_op jit(solution)/shard_map/ppermute | solution.py:205
  44.0 0.9 collective-permute-start.8
  44.8 0.0 collective-permute-done.7
  44.9 0.1 collective-permute-start.12
  45.0 0.0 collective-permute-done.10.rest_9_
  45.0 0.0 copy-start
  45.0 0.8 copy-done
  45.8 0.5 collective-permute-start.13
  46.3 0.0 collective-permute-done.3.rest_3_
  46.3 0.0 collective-permute-start.11
  46.3 0.0 collective-permute-done.9.rest_8_
  46.3 0.0 copy-start.2
  46.3 0.8 copy-done.2
  47.1 0.5 collective-permute-start.14
  47.6 0.1 pad_add_fusion.1.meta
  47.7 0.1 reshape.224.counts
  47.8 0.5 select_reduce_fusion.1
  48.2 0.7 add_select_fusion.5
  48.9 2.5 %convert_reduce_fusion = (s32[128]{0:T(128)S(1)}, s32[128]{0:T(128)S(1)}) fusion(s32[2048]{0:T(1024)S(1)} %add_select_fusion.5, s32[2048]{0:T(1024)} %param.11), kind=kLoop, calls=%fused_computation | loop fusion | flops 1310464 | bytes 17408 | tf_op jit(solution)/shard_map/reduce_sum | solution.py:228
  51.5 0.0 collective-permute-done.8.rest_7_
  51.5 0.0 collective-permute-done.12.rest_11_
  51.5 0.0 collective-permute-done.13.rest_12_
  51.5 0.0 collective-permute-done.11.rest_10_
  51.5 0.0 collective-permute-done.14.rest_13_
  51.5 0.0 copy-start.1
  51.6 1.0 copy-done.1
  52.6 0.0 copy-start.3
  52.6 1.0 copy-done.3
  53.6 0.0 copy-start.4
  53.6 0.7 copy-done.4
  54.3 37.5 %attend.1 = bf16[4096,256]{1,0:T(8,128)(2,1)} custom-call(s32[2]{0:T(128)S(1)} %pad_add_fusion.1.meta, s32[32,24]{1,0:T(8,128)S(1)} %bitcast.8, s32[32]{0:T(128)S(1)} %reshape.224.counts, s32[128]{0:T(128)S(1)} %get-tuple-element.6.first_row, s32[128]{0:T(128)S(1)} %get-tuple-element.5.sent, bf16[2048,256]{1,0:T(8,128)(2,1)} %q_ref.1, ...), custom_call_target="tpu_custom_call" | custom-call | tf_op jit(solution)/shard_map/attend/pallas_call | solution.py:232
  91.9 37.4 %all_to_all.5 = bf16[128,32,256]{2,1,0:T(8,128)(2,1)S(1)} all-to-all(bf16[128,32,256]{2,1,0:T(8,128)(2,1)} %bitcast.9), channel_id=1, replica_groups=mesh['ctx'=8,'rows'=16] {'ctx','rows'}, dimensions={0} | all-to-all | bytes 4194304 | tf_op jit(solution)/shard_map/all_to_all | solution.py:247
  129.3 6.9 %arrange.1 = bf16[128,4096]{1,0:T(8,128)(2,1)} custom-call(bf16[8,16,32,256]{3,2,1,0:T(8,128)(2,1)S(1)} %bitcast.6), custom_call_target="tpu_custom_call" | custom-call | tf_op jit(solution)/shard_map/arrange/pallas_call | solution.py:251
  (6 shorter events, 0.1 us)
Async XLA Ops:
  1.4 14.2 %collective-permute-start.2 = (bf16[2048,128]{1,0:T(8,128)(2,1)S(1)}, bf16[2048,128]{1,0:T(8,128)(2,1)S(1)}, u32[]{:S(2)}, u32[]{:S(2)}) collective-permute-start(bf16[2048,128]{1,0:T(8,128)(2,1)S(1)} %dynamic-slice_select_fusion), channel_id=1, source_target_pairs={{0,16},{16,0},{32,48},{48,32},{64,80},{80,64},{96,112},{112,96},{1... | collective-permute-start | bytes 1572872 | tf_op jit(solution)/shard_map/ppermute | solution.py:208
  3.9 14.0 %collective-permute-start = (bf16[2048,128]{1,0:T(8,128)(2,1)S(1)}, bf16[2048,128]{1,0:T(8,128)(2,1)S(1)}, u32[]{:S(2)}, u32[]{:S(2)}) collective-permute-start(bf16[2048,128]{1,0:T(8,128)(2,1)S(1)} %dynamic-slice_select_fusion), channel_id=1, source_target_pairs={{0,32},{16,48},{32,64},{48,80},{64,96},{80,112},{96,0},{112,16},{1... | collective-permute-start | bytes 1572872 | tf_op jit(solution)/shard_map/ppermute | solution.py:205
  5.1 18.5 %collective-permute-start.1 = (bf16[2048,128]{1,0:T(8,128)(2,1)S(1)}, bf16[2048,128]{1,0:T(8,128)(2,1)S(1)}, u32[]{:S(2)}, u32[]{:S(2)}) collective-permute-start(bf16[2048,128]{1,0:T(8,128)(2,1)S(1)} %dynamic-slice_select_fusion), channel_id=1, source_target_pairs={{0,96},{16,112},{32,0},{48,16},{64,32},{80,48},{96,64},{112,80},{1... | collective-permute-start | bytes 1572872 | tf_op jit(solution)/shard_map/ppermute | solution.py:205
  15.5 13.9 %collective-permute-start.4 = (bf16[2048,128]{1,0:T(8,128)(2,1)S(1)}, bf16[2048,128]{1,0:T(8,128)(2,1)S(1)}, u32[]{:S(2)}, u32[]{:S(2)}) collective-permute-start(bf16[2048,128]{1,0:T(8,128)(2,1)S(1)} %collective-permute-done.2.rest_2_), channel_id=1, source_target_pairs={{0,96},{16,112},{32,0},{48,16},{64,32},{80,48},{96,64},{112,80},{1... | collective-permute-start | bytes 1572872 | tf_op jit(solution)/shard_map/ppermute | solution.py:205
  17.9 13.4 %collective-permute-start.5 = (bf16[2048,128]{1,0:T(8,128)(2,1)S(1)}, bf16[2048,128]{1,0:T(8,128)(2,1)S(1)}, u32[]{:S(2)}, u32[]{:S(2)}) collective-permute-start(bf16[2048,128]{1,0:T(8,128)(2,1)S(1)} %collective-permute-done.rest_0_), channel_id=1, source_target_pairs={{0,16},{16,0},{32,48},{48,32},{64,80},{80,64},{96,112},{112,96},{1... | collective-permute-start | bytes 1572872 | tf_op jit(solution)/shard_map/ppermute | solution.py:208
  21.5 23.5 %collective-permute-start.10 = (bf16[2048,128]{1,0:T(8,128)(2,1)S(1)}, bf16[2048,128]{1,0:T(8,128)(2,1)S(1)}, u32[]{:S(2)}, u32[]{:S(2)}) collective-permute-start(bf16[2048,128]{1,0:T(8,128)(2,1)S(1)} %collective-permute-done.2.rest_2_), channel_id=1, source_target_pairs={{0,1},{1,0},{2,3},{3,2},{4,5},{5,4},{6,7},{7,6},{8,9},{9,8},{10,11... | collective-permute-start | bytes 1572872 | tf_op jit(solution)/shard_map/ppermute | solution.py:211
  23.6 22.7 %collective-permute-start.3 = (bf16[2048,128]{1,0:T(8,128)(2,1)S(1)}, bf16[2048,128]{1,0:T(8,128)(2,1)}, u32[]{:S(2)}, u32[]{:S(2)}) collective-permute-start(bf16[2048,128]{1,0:T(8,128)(2,1)S(1)} %collective-permute-done.rest_0_), channel_id=1, source_target_pairs={{0,32},{16,48},{32,64},{48,80},{64,96},{80,112},{96,0},{112,16},{1... | collective-permute-start | bytes 1572872 | tf_op jit(solution)/shard_map/ppermute | solution.py:205
  23.6 22.7 %collective-permute-start.9 = (bf16[2048,128]{1,0:T(8,128)(2,1)S(1)}, bf16[2048,128]{1,0:T(8,128)(2,1)S(1)}, u32[]{:S(2)}, u32[]{:S(2)}) collective-permute-start(bf16[2048,128]{1,0:T(8,128)(2,1)S(1)} %collective-permute-done.1.rest_1_), channel_id=1, source_target_pairs={{0,1},{1,0},{2,3},{3,2},{4,5},{5,4},{6,7},{7,6},{8,9},{9,8},{10,11... | collective-permute-start | bytes 1572872 | tf_op jit(solution)/shard_map/ppermute | solution.py:211
  29.5 15.4 %collective-permute-start.7 = (bf16[1024,128]{1,0:T(8,128)(2,1)S(1)}, bf16[1024,128]{1,0:T(8,128)(2,1)S(1)}, u32[]{:S(2)}, u32[]{:S(2)}) collective-permute-start(bf16[1024,128]{1,0:T(8,128)(2,1)S(1)} %slice.9), channel_id=1, source_target_pairs={{0,96},{16,112},{32,0},{48,16},{64,32},{80,48},{96,64},{112,80},{1... | collective-permute-start | bytes 786440 | tf_op jit(solution)/shard_map/ppermute | solution.py:205
  31.3 12.7 %collective-permute-start.6 = (bf16[1024,128]{1,0:T(8,128)(2,1)S(1)}, bf16[1024,128]{1,0:T(8,128)(2,1)S(1)}, u32[]{:S(2)}, u32[]{:S(2)}) collective-permute-start(bf16[1024,128]{1,0:T(8,128)(2,1)S(1)} %slice.8), channel_id=1, source_target_pairs={{0,32},{16,48},{32,64},{48,80},{64,96},{80,112},{96,0},{112,16},{1... | collective-permute-start | bytes 786440 | tf_op jit(solution)/shard_map/ppermute | solution.py:205
  44.0 7.5 %collective-permute-start.8 = (bf16[2048,128]{1,0:T(8,128)(2,1)S(1)}, bf16[2048,128]{1,0:T(8,128)(2,1)}, u32[]{:S(2)}, u32[]{:S(2)}) collective-permute-start(bf16[2048,128]{1,0:T(8,128)(2,1)S(1)} %collective-permute-done.rest_0_), channel_id=1, source_target_pairs={{0,1},{1,0},{2,3},{3,2},{4,5},{5,4},{6,7},{7,6},{8,9},{9,8},{10,11... | collective-permute-start | bytes 1572872 | tf_op jit(solution)/shard_map/ppermute | solution.py:211
  44.9 6.7 %collective-permute-start.12 = (bf16[2048,128]{1,0:T(8,128)(2,1)S(1)}, bf16[2048,128]{1,0:T(8,128)(2,1)}, u32[]{:S(2)}, u32[]{:S(2)}) collective-permute-start(bf16[2048,128]{1,0:T(8,128)(2,1)S(1)} %collective-permute-done.4.rest_4_), channel_id=1, source_target_pairs={{0,1},{1,0},{2,3},{3,2},{4,5},{5,4},{6,7},{7,6},{8,9},{9,8},{10,11... | collective-permute-start | bytes 1572872 | tf_op jit(solution)/shard_map/ppermute | solution.py:211
  45.0 0.8 copy-start
  45.8 5.7 %collective-permute-start.13 = (bf16[2048,128]{1,0:T(8,128)(2,1)S(1)}, bf16[2048,128]{1,0:T(8,128)(2,1)}, u32[]{:S(2)}, u32[]{:S(2)}) collective-permute-start(bf16[2048,128]{1,0:T(8,128)(2,1)S(1)} %collective-permute-done.5.rest_5_), channel_id=1, source_target_pairs={{0,1},{1,0},{2,3},{3,2},{4,5},{5,4},{6,7},{7,6},{8,9},{9,8},{10,11... | collective-permute-start | bytes 1572872 | tf_op jit(solution)/shard_map/ppermute | solution.py:211
  46.3 5.2 %collective-permute-start.11 = (bf16[2048,128]{1,0:T(8,128)(2,1)}, bf16[2048,128]{1,0:T(8,128)(2,1)}, u32[]{:S(2)}, u32[]{:S(2)}) collective-permute-start(bf16[2048,128]{1,0:T(8,128)(2,1)} %collective-permute-done.3.rest_3_), channel_id=1, source_target_pairs={{0,1},{1,0},{2,3},{3,2},{4,5},{5,4},{6,7},{7,6},{8,9},{9,8},{10,11... | collective-permute-start | bytes 1572872 | tf_op jit(solution)/shard_map/ppermute | solution.py:211
  46.3 0.8 copy-start.2
  47.1 4.4 %collective-permute-start.14 = (bf16[2048,128]{1,0:T(8,128)(2,1)S(1)}, bf16[2048,128]{1,0:T(8,128)(2,1)}, u32[]{:S(2)}, u32[]{:S(2)}) collective-permute-start(bf16[2048,128]{1,0:T(8,128)(2,1)S(1)} %constant_dynamic-update-slice_fusion.rest_6_), channel_id=1, source_target_pairs={{0,1},{1,0},{2,3},{3,2},{4,5},{5,4},{6,7},{7,6},{8,9},{9,8},{10,11... | collective-permute-start | bytes 1572872 | tf_op jit(solution)/shard_map/ppermute | solution.py:211
  51.5 1.0 copy-start.1
  52.6 1.0 copy-start.3
  53.6 0.7 copy-start.4

commit v2 on v1

--- a/solution.py
+++ b/solution.py
@@ -16,6 +16,7 @@
 EMPTY = 1048576.0
 SCALE2 = DH**-0.5 * 1.4426950408889634
 GROUP = 4
+SLOT = 32
 PIECE = {(0, 0): 0, (3, 0): 1, (1, 0): 2, (0, 1): 3, (2, 0): 4, (1, 1): 5, (3, 1): 6, (2, 1): 7}
 ANY = pl.BlockSpec(memory_space=pl.ANY)
 SMEM = pl.BlockSpec(memory_space=pltpu.SMEM)
@@ -26,36 +27,39 @@
     return lax.dot_general(a, b, (((1,), (1,)), ((), ())), preferred_element_type=jnp.float32)
 
 
-def attend_kernel(pieces, slots, heads, meta, lists, counts, first_row, sent, q_ref, dest_ref, keys, values, *rest):
-    mine, other = rest[: pieces - 1], rest[pieces - 1 : 2 * pieces - 2]
-    out_ref, k_s, v_s, att, sem = rest[2 * pieces - 2 :]
+def attend_kernel(sizes, slots, heads, meta, lists, counts, first_row, sent, q_ref, dest_ref, keys, values, *rest):
+    pieces = len(sizes)
+    mine, other = rest[:pieces], rest[pieces : 2 * pieces]
+    out_ref, k_s, v_s, att, sem = rest[2 * pieces :]
     shard = q_ref.shape[0]
     nblk = shard // BLOCK
     core, kv = meta[0], meta[1]
     column = pl.ds(pl.multiple_of(kv * DH, DH), DH)
-
-    def spot(ref, p):
-        return ref.at[pl.ds(p * shard, shard)]
-
-    pltpu.make_async_copy(keys.at[:, column], spot(k_s, 0), sem.at[0]).start()
-    pltpu.make_async_copy(values.at[:, column], spot(v_s, 0), sem.at[pieces]).start()
-    for p in range(1, pieces):
+    copies = []
+    for ref, to in ((keys, k_s), (values, v_s)):
+        copy = pltpu.make_async_copy(ref.at[:, column], to.at[pl.ds(0, shard)], sem.at[len(copies)])
+        copy.start()
+        copies.append(copy)
+    begin = shard
+    for p in range(pieces):
+        spot = pl.ds(begin, sizes[p])
+        begin += sizes[p]
+        number = len(copies)
 
         @pl.when(core == 0)
         def _():
-            pltpu.make_async_copy(mine[p - 1], spot(k_s, p), sem.at[p]).start()
-            pltpu.make_async_copy(other[p - 1], spot(v_s, p), sem.at[pieces + p]).start()
+            pltpu.make_async_copy(mine[p], k_s.at[spot], sem.at[number]).start()
+            pltpu.make_async_copy(other[p], v_s.at[spot], sem.at[number + 1]).start()
 
         @pl.when(core != 0)
         def _():
-            pltpu.make_async_copy(other[p - 1], spot(k_s, p), sem.at[p]).start()
-            pltpu.make_async_copy(mine[p - 1], spot(v_s, p), sem.at[pieces + p]).start()
-
-    pltpu.make_async_copy(keys.at[:, column], spot(k_s, 0), sem.at[0]).wait()
-    pltpu.make_async_copy(values.at[:, column], spot(v_s, 0), sem.at[pieces]).wait()
-    for p in range(1, pieces):
-        pltpu.make_async_copy(mine[p - 1], spot(k_s, p), sem.at[p]).wait()
-        pltpu.make_async_copy(mine[p - 1], spot(v_s, p), sem.at[pieces + p]).wait()
+            pltpu.make_async_copy(other[p], k_s.at[spot], sem.at[number]).start()
+            pltpu.make_async_copy(mine[p], v_s.at[spot], sem.at[number + 1]).start()
+
+        copies.append(pltpu.make_async_copy(mine[p], k_s.at[spot], sem.at[number]))
+        copies.append(pltpu.make_async_copy(mine[p], v_s.at[spot], sem.at[number + 1]))
+    for copy in copies:
+        copy.wait()
 
     def block_of(ref, index):
         return ref[pl.ds(pl.multiple_of(index * BLOCK, BLOCK), BLOCK), :]
@@ -127,34 +131,28 @@
     lax.fori_loop(0, owners // batch, per_batch, 0)
 
 
-def arrange_kernel(in_ref, out_ref, pick):
-    shards, _, capacity, width = in_ref.shape
+def arrange_kernel(in_ref, out_ref):
+    shards, groups, capacity, width = in_ref.shape
     slots = shards * capacity
     rows = out_ref.shape[0]
-    block = in_ref[...].reshape(slots, width)
-
-    @pl.when(pl.program_id(0) == 0)
-    def _():
-        used = jnp.where(block[:, :rows].astype(jnp.float32) < EMPTY / 2, 1.0, 0.0).astype(jnp.bfloat16)
-        one = lax.broadcasted_iota(jnp.int32, (slots, slots), 0)
-        two = lax.broadcasted_iota(jnp.int32, (slots, slots), 1)
-        contract = (((0,), (0,)), ((), ()))
-        before = lax.dot_general(
-            used,
-            jnp.where(one < two, 1.0, 0.0).astype(jnp.bfloat16),
-            contract,
-            preferred_element_type=jnp.float32,
+    block = in_ref[:, 0].reshape(slots, width)
+    used = jnp.where(block[:, :rows].astype(jnp.float32) < EMPTY / 2, 1.0, 0.0).astype(jnp.bfloat16)
+    one = lax.broadcasted_iota(jnp.int32, (slots, slots), 0)
+    two = lax.broadcasted_iota(jnp.int32, (slots, slots), 1)
+    contract = (((0,), (0,)), ((), ()))
+    before = lax.dot_general(
+        used, jnp.where(one < two, 1.0, 0.0).astype(jnp.bfloat16), contract, preferred_element_type=jnp.float32
+    )
+    here = lax.dot_general(
+        used, jnp.where(one == two, 1.0, 0.0).astype(jnp.bfloat16), contract, preferred_element_type=jnp.float32
+    )
+    line = lax.broadcasted_iota(jnp.int32, (rows, slots), 0).astype(jnp.float32)
+    pick = jnp.where((before == line) & (here > 0.5), 1.0, 0.0).astype(jnp.bfloat16)
+    for g in range(groups):
+        block = in_ref[:, g].reshape(slots, width)
+        out_ref[:, g * width : (g + 1) * width] = jnp.dot(pick, block, preferred_element_type=jnp.float32).astype(
+            jnp.bfloat16
         )
-        here = lax.dot_general(
-            used,
-            jnp.where(one == two, 1.0, 0.0).astype(jnp.bfloat16),
-            contract,
-            preferred_element_type=jnp.float32,
-        )
-        line = lax.broadcasted_iota(jnp.int32, (rows, slots), 0).astype(jnp.float32)
-        pick[...] = jnp.where((before == line) & (here > 0.5), 1.0, 0.0).astype(jnp.bfloat16)
-
-    out_ref[...] = jnp.dot(pick[...], block, preferred_element_type=jnp.float32).astype(jnp.bfloat16)
 
 
 def block_lists(verticals, slashes, place, nblk, nshards):
@@ -191,7 +189,7 @@
     nblk = rows_here // BLOCK
     devices = cycle * groups
     own_rows = rows_here // groups
-    capacity = 2 * rows_here // devices
+    capacity = SLOT
     kv_index = group * heads // (HEADS // KV_HEADS)
     core = group % 2
 
@@ -217,8 +215,10 @@
     p4 = along_x(p1, 1)
     p5 = along_x(p3, -1)
     p6 = along_z(p1)
-    p7 = jnp.concatenate([along_x(p6[:half], 1), along_x(p5[half:], -1)], axis=0)
-    mine = (p1, p2, p3, p4, p5, p6, p7)
+    p1, p2, p3, p4, p5, p6 = lax.optimization_barrier((p1, p2, p3, p4, p5, p6))
+    p7 = along_x(p6[:half], 1)
+    p8 = along_x(p5[half:], -1)
+    mine = (p1, p2, p3, p4, p5, p6, p7, p8)
     other = tuple(swap(x) for x in mine)
 
     lists, counts = block_lists(verticals, slashes, place, nblk, cycle)
@@ -230,17 +230,17 @@
 
     slots = lists.shape[1]
     outgoing = pl.pallas_call(
-        functools.partial(attend_kernel, cycle, slots, heads),
+        functools.partial(attend_kernel, [x.shape[0] for x in mine], slots, heads),
         out_shape=jax.ShapeDtypeStruct((devices * capacity, heads * DH), jnp.bfloat16),
-        in_specs=[SMEM] * 5 + [VMEM] * 2 + [ANY] * (2 + 2 * (cycle - 1)),
+        in_specs=[SMEM] * 5 + [VMEM] * 2 + [ANY] * (2 + 2 * len(mine)),
         out_specs=VMEM,
         scratch_shapes=[
             pltpu.VMEM((cycle * rows_here, DH), jnp.bfloat16),
             pltpu.VMEM((cycle * rows_here, DH), jnp.bfloat16),
             pltpu.VMEM((rows_here, heads * DH), jnp.bfloat16),
-            pltpu.SemaphoreType.DMA((2 * cycle,)),
+            pltpu.SemaphoreType.DMA((2 + 2 * len(mine),)),
         ],
-        compiler_params=pltpu.CompilerParams(vmem_limit_bytes=48 * 1024 * 1024),
+        compiler_params=pltpu.CompilerParams(vmem_limit_bytes=60 * 1024 * 1024),
         name="attend",
     )(meta, lists, counts, first_row, sent, queries, destination.reshape(1, rows_here), keys, values, *mine, *other)
 
@@ -250,12 +250,10 @@
     incoming = incoming.reshape(cycle, groups, capacity, heads * DH)
     return pl.pallas_call(
         arrange_kernel,
-        grid=(groups,),
         out_shape=jax.ShapeDtypeStruct((own_rows, groups * heads * DH), jnp.bfloat16),
-        in_specs=[pl.BlockSpec((cycle, 1, capacity, heads * DH), lambda g: (0, g, 0, 0))],
-        out_specs=pl.BlockSpec((own_rows, heads * DH), lambda g: (0, g)),
-        scratch_shapes=[pltpu.VMEM((own_rows, cycle * capacity), jnp.bfloat16)],
-        compiler_params=pltpu.CompilerParams(vmem_limit_bytes=32 * 1024 * 1024),
+        in_specs=[VMEM],
+        out_specs=VMEM,
+        compiler_params=pltpu.CompilerParams(vmem_limit_bytes=60 * 1024 * 1024),
         name="arrange",
     )(incoming)
 

time: 137 us -> 138 us (level)
  blocking collectives: 37.4 us -> 39.7 us
  Pallas kernels: 44.4 us -> 42.1 us
  starting transfers between devices: 15.1 us -> 17 us
  other arithmetic: 7.6 us -> 9.29 us
    unnamed x11 -> x18, local copies, waits for them, and re-layouts: 4.37 us -> 1.27 us
    pallas_call x2, Pallas kernels: 44.4 us -> 42.1 us  [the longest x1 38.9 us: body(): pl.pallas_call(functools.partial(attend_kernel, [x.shape[0] for x in mine...]
    all_to_all x1, blocking collectives: 37.4 us -> 39.7 us  [body(): lax.all_to_all(outgoing.reshape(devices, capacity, heads * DH), ('ctx', '...]
    slice x2, local copies, waits for them, and re-layouts: 0.04 us -> 1.44 us  [the longest x1 0.72 us: body(): p7 = along_x(p6[:half], 1)]
    ppermute x7 -> x8, starting transfers between devices: 4.31 us -> 5.41 us  [swap(): return lax.ppermute(x, 'rows', [(r, r ^ 1) for r in range(groups)])]
  transfers between devices with their start and end apart: 15 -> 16, of which waited for: 3 -> 5; matrix products, arithmetic and copies ran while one was open for 5% -> 8% of each run, Pallas kernels for 0% -> 0%
where the time goes in v2:
time: 138 us
  Pallas kernels  42.1 us (31%)
  blocking collectives  39.7 us (29%)
  waiting for transfers between devices  25.8 us (19%)
  starting transfers between devices  17 us (12%)
  other arithmetic  9.29 us (7%)
  local copies, waits for them, and re-layouts  4.04 us (3%)
    all_to_all x1, blocking collectives, body(): lax.all_to_all(outgoing.reshape(devices, capacity, heads * DH), ('ctx', '...  39.7 us
    pallas_call x1, Pallas kernels, body(): pl.pallas_call(functools.partial(attend_kernel, [x.shape[0] for x in mine...  38.9 us
    ppermute x6, waiting for transfers between devices, along_x(): lax.ppermute(x, 'ctx', [(c, (c + 2 * step) % cycle) for c in range(cycle)])  16.4 us
    ppermute x2, waiting for transfers between devices, along_z(): return lax.ppermute(x, 'ctx', [(c, c ^ 1) for c in range(cycle)])  9.32 us
    ppermute x6, starting transfers between devices, along_x(): lax.ppermute(x, 'ctx', [(c, (c + 2 * step) % cycle) for c in range(cycle)])  7.73 us
    ppermute x8, starting transfers between devices, swap(): return lax.ppermute(x, 'rows', [(r, r ^ 1) for r in range(groups)])  5.41 us
    ppermute x2, starting transfers between devices, along_z(): return lax.ppermute(x, 'ctx', [(c, c ^ 1) for c in range(cycle)])  3.81 us
    pallas_call x1, Pallas kernels, body(): pl.pallas_call(arrange_kernel, out_shape=jax.ShapeDtypeStruct((own_rows,...  3.17 us
  transfers between devices with their start and end apart: 16, of which 5 were waited for; matrix products, arithmetic and copies ran while one was open for 8% of the time, Pallas kernels for 0%

profile of v2, /device:TPU:1, one launch (start us, length us, event | category | flops | bytes accessed | tf_op | source)
XLA Modules:
  0.0 138.0 jit_solution(11277042810360424231)
XLA Ops:
  0.0 1.4 dynamic-slice_select_fusion
  1.4 2.5 %collective-permute-start.2 = (bf16[2048,128]{1,0:T(8,128)(2,1)S(1)}, bf16[2048,128]{1,0:T(8,128)(2,1)S(1)}, u32[]{:S(2)}, u32[]{:S(2)}) collective-permute-start(bf16[2048,128]{1,0:T(8,128)(2,1)S(1)} %dynamic-slice_select_fusion), channel_id=1, source_target_pairs={{0,16},{16,0},{32,48},{48,32},{64,80},{80,64},{96,112},{112,96},{1... | collective-permute-start | bytes 1572872 | tf_op jit(solution)/shard_map/ppermute | solution.py:206
  3.9 1.2 collective-permute-start
  5.1 1.5 %collective-permute-start.1 = (bf16[2048,128]{1,0:T(8,128)(2,1)S(1)}, bf16[2048,128]{1,0:T(8,128)(2,1)S(1)}, u32[]{:S(2)}, u32[]{:S(2)}) collective-permute-start(bf16[2048,128]{1,0:T(8,128)(2,1)S(1)} %dynamic-slice_select_fusion), channel_id=1, source_target_pairs={{0,96},{16,112},{32,0},{48,16},{64,32},{80,48},{96,64},{112,80},{1... | collective-permute-start | bytes 1572872 | tf_op jit(solution)/shard_map/ppermute | solution.py:203
  6.6 9.0 %collective-permute-done.2.rest_2_ = bf16[2048,128]{1,0:T(8,128)(2,1)S(1)} collective-permute-done((bf16[2048,128]{1,0:T(8,128)(2,1)S(1)}, bf16[2048,128]{1,0:T(8,128)(2,1)S(1)}, u32[]{:S(2)}, u32[]{:S(2)}) %collective-permute-start.2) | collective-permute-done | bytes 524320 | tf_op jit(solution)/shard_map/ppermute | solution.py:206
  15.5 0.0 copy-start.2
  15.5 2.4 %collective-permute-start.4 = (bf16[2048,128]{1,0:T(8,128)(2,1)S(1)}, bf16[2048,128]{1,0:T(8,128)(2,1)S(1)}, u32[]{:S(2)}, u32[]{:S(2)}) collective-permute-start(bf16[2048,128]{1,0:T(8,128)(2,1)S(1)} %collective-permute-done.2.rest_2_), channel_id=1, source_target_pairs={{0,96},{16,112},{32,0},{48,16},{64,32},{80,48},{96,64},{112,80},{1... | collective-permute-start | bytes 1572872 | tf_op jit(solution)/shard_map/ppermute | solution.py:203
  17.9 0.0 collective-permute-done.rest_0_
  17.9 0.0 copy-start.3
  17.9 1.3 collective-permute-start.5
  19.2 0.0 collective-permute-start.3
  19.2 0.7 broadcast_subtract_fusion
  19.9 0.0 collective-permute-done.1.rest_1_
  19.9 0.0 copy-start.4
  19.9 9.5 %collective-permute-done.4.rest_4_ = bf16[2048,128]{1,0:T(8,128)(2,1)S(1)} collective-permute-done((bf16[2048,128]{1,0:T(8,128)(2,1)S(1)}, bf16[2048,128]{1,0:T(8,128)(2,1)S(1)}, u32[]{:S(2)}, u32[]{:S(2)}) %collective-permute-start.4) | collective-permute-done | bytes 524320 | tf_op jit(solution)/shard_map/ppermute | solution.py:203
  29.4 0.0 copy-start
  29.4 0.4 collective-permute-done.5.rest_5_
  29.8 0.0 copy-start.1
  29.8 2.0 %collective-permute-done.3.rest_3_ = bf16[2048,128]{1,0:T(8,128)(2,1)} collective-permute-done((bf16[2048,128]{1,0:T(8,128)(2,1)S(1)}, bf16[2048,128]{1,0:T(8,128)(2,1)}, u32[]{:S(2)}, u32[]{:S(2)}) %collective-permute-start.3) | collective-permute-done | bytes 524320 | tf_op jit(solution)/shard_map/ppermute | solution.py:203
  31.8 3.0 %collective-permute-start.8 = (bf16[2048,128]{1,0:T(8,128)(2,1)S(1)}, bf16[2048,128]{1,0:T(8,128)(2,1)S(1)}, u32[]{:S(2)}, u32[]{:S(2)}) collective-permute-start(bf16[2048,128]{1,0:T(8,128)(2,1)S(1)} %collective-permute-done.rest_0_), channel_id=1, source_target_pairs={{0,1},{1,0},{2,3},{3,2},{4,5},{5,4},{6,7},{7,6},{8,9},{9,8},{10,11... | collective-permute-start | bytes 1572872 | tf_op jit(solution)/shard_map/ppermute | solution.py:209
  34.8 0.7 broadcast_in_dim.62
  35.5 0.1 pad_add_fusion
  35.6 0.7 slice.7
  36.3 0.7 slice.6
  37.0 0.0 collective-permute-start.6
  37.0 2.7 %collective-permute-start.7 = (bf16[1024,128]{1,0:T(8,128)(2,1)}, bf16[1024,128]{1,0:T(8,128)(2,1)}, u32[]{:S(2)}, u32[]{:S(2)}) collective-permute-start(bf16[1024,128]{1,0:T(8,128)(2,1)} %slice.7), channel_id=1, source_target_pairs={{0,96},{16,112},{32,0},{48,16},{64,32},{80,48},{96,64},{112,80},{1... | collective-permute-start | bytes 786440 | tf_op jit(solution)/shard_map/ppermute | solution.py:203
  39.7 0.8 and_reduce_fusion
  40.5 0.6 collective-permute-start.9
  41.1 0.1 collective-permute-start.10
  41.2 0.2 convert_reduce_fusion.2
  41.5 4.9 %collective-permute-done.6.rest_6_ = bf16[1024,128]{1,0:T(8,128)(2,1)S(1)} collective-permute-done((bf16[1024,128]{1,0:T(8,128)(2,1)}, bf16[1024,128]{1,0:T(8,128)(2,1)S(1)}, u32[]{:S(2)}, u32[]{:S(2)}) %collective-permute-start.6) | collective-permute-done | bytes 262176 | tf_op jit(solution)/shard_map/ppermute | solution.py:203
  46.4 0.8 collective-permute-start.12
  47.2 0.0 collective-permute-done.7.rest_7_
  47.2 0.1 collective-permute-start.13
  47.3 0.0 collective-permute-done.8.rest_8_
  47.3 0.4 collective-permute-start.11
  47.7 0.7 add_select_fusion.5
  48.4 0.6 convert_reduce_fusion.1
  49.0 0.0 collective-permute-done.9.rest_9_
  49.0 0.0 copy-start.6
  49.1 0.2 collective-permute-start.14
  49.3 0.0 collective-permute-done.10.rest_10_
  49.3 0.6 copy-done.6
  49.8 0.1 collective-permute-start.15
  50.0 0.7 copy-done.7
  50.7 1.1 select_reduce_fusion.1
  51.7 0.7 reshape.224.counts
  52.4 0.6 pad_add_fusion.1.meta
  53.0 3.1 %convert_reduce_fusion = (s32[128]{0:T(128)}, s32[128]{0:T(128)}) fusion(s32[2048]{0:T(1024)S(1)} %add_select_fusion.5, s32[2048]{0:T(1024)} %param.11), kind=kLoop, calls=%fused_computation | loop fusion | flops 1310464 | bytes 17408 | tf_op jit(solution)/shard_map/reduce_sum | solution.py:228
  56.1 0.0 collective-permute-done.11.rest_11_
  56.1 0.0 collective-permute-done.12.rest_12_
  56.1 0.0 collective-permute-done.13.rest_13_
  56.1 0.0 collective-permute-done.14.rest_14_
  56.1 0.0 collective-permute-done.15.rest_15_
  56.1 0.0 copy-done.2
  56.1 0.0 copy-done.3
  56.2 0.0 copy-done.4
  56.2 0.0 copy-done
  56.2 0.0 copy-done.1
  56.2 0.0 copy-done.8
  56.2 0.0 copy-done.5
  56.2 38.9 %attend.1 = bf16[4096,256]{1,0:T(8,128)(2,1)} custom-call(s32[2]{0:T(128)} %pad_add_fusion.1.meta, s32[32,24]{1,0:T(8,128)} %bitcast.9, s32[32]{0:T(128)} %reshape.224.counts, s32[128]{0:T(128)} %get-tuple-element.18.first_row, s32[128]{0:T(128)} %get-tuple-element.17.sent, bf16[2048,256]{1,0:T(8,128)(2,1)} %q_ref.1, s32[1,2048]{1,0:T(1,128)} %bitcast.8, ...), custom_call_target="tpu_custom_call" | custom-call | tf_op jit(solution)/shard_map/attend/pallas_call | solution.py:232
  95.1 39.7 %all_to_all.5 = bf16[128,32,256]{2,1,0:T(8,128)(2,1)} all-to-all(bf16[128,32,256]{2,1,0:T(8,128)(2,1)} %bitcast.7), channel_id=1, replica_groups=mesh['ctx'=8,'rows'=16] {'ctx','rows'}, dimensions={0} | all-to-all | bytes 4194304 | tf_op jit(solution)/shard_map/all_to_all | solution.py:247
  134.8 3.2 %arrange.1 = bf16[128,4096]{1,0:T(8,128)(2,1)} custom-call(bf16[8,16,32,256]{3,2,1,0:T(8,128)(2,1)} %bitcast.6), custom_call_target="tpu_custom_call" | custom-call | tf_op jit(solution)/shard_map/arrange/pallas_call | solution.py:251
  (5 shorter events, 0.0 us)
Async XLA Ops:
  1.4 14.2 %collective-permute-start.2 = (bf16[2048,128]{1,0:T(8,128)(2,1)S(1)}, bf16[2048,128]{1,0:T(8,128)(2,1)S(1)}, u32[]{:S(2)}, u32[]{:S(2)}) collective-permute-start(bf16[2048,128]{1,0:T(8,128)(2,1)S(1)} %dynamic-slice_select_fusion), channel_id=1, source_target_pairs={{0,16},{16,0},{32,48},{48,32},{64,80},{80,64},{96,112},{112,96},{1... | collective-permute-start | bytes 1572872 | tf_op jit(solution)/shard_map/ppermute | solution.py:206
  3.9 14.0 %collective-permute-start = (bf16[2048,128]{1,0:T(8,128)(2,1)S(1)}, bf16[2048,128]{1,0:T(8,128)(2,1)S(1)}, u32[]{:S(2)}, u32[]{:S(2)}) collective-permute-start(bf16[2048,128]{1,0:T(8,128)(2,1)S(1)} %dynamic-slice_select_fusion), channel_id=1, source_target_pairs={{0,32},{16,48},{32,64},{48,80},{64,96},{80,112},{96,0},{112,16},{1... | collective-permute-start | bytes 1572872 | tf_op jit(solution)/shard_map/ppermute | solution.py:203
  5.1 14.8 %collective-permute-start.1 = (bf16[2048,128]{1,0:T(8,128)(2,1)S(1)}, bf16[2048,128]{1,0:T(8,128)(2,1)S(1)}, u32[]{:S(2)}, u32[]{:S(2)}) collective-permute-start(bf16[2048,128]{1,0:T(8,128)(2,1)S(1)} %dynamic-slice_select_fusion), channel_id=1, source_target_pairs={{0,96},{16,112},{32,0},{48,16},{64,32},{80,48},{96,64},{112,80},{1... | collective-permute-start | bytes 1572872 | tf_op jit(solution)/shard_map/ppermute | solution.py:203
  15.5 40.6 %copy-start.2 = (bf16[2048,128]{1,0:T(8,128)(2,1)}, bf16[2048,128]{1,0:T(8,128)(2,1)S(1)}, u32[]{:S(2)}) copy-start(bf16[2048,128]{1,0:T(8,128)(2,1)S(1)} %collective-permute-done.2.rest_2_) | copy-start | bytes 1572868
  15.5 13.9 %collective-permute-start.4 = (bf16[2048,128]{1,0:T(8,128)(2,1)S(1)}, bf16[2048,128]{1,0:T(8,128)(2,1)S(1)}, u32[]{:S(2)}, u32[]{:S(2)}) collective-permute-start(bf16[2048,128]{1,0:T(8,128)(2,1)S(1)} %collective-permute-done.2.rest_2_), channel_id=1, source_target_pairs={{0,96},{16,112},{32,0},{48,16},{64,32},{80,48},{96,64},{112,80},{1... | collective-permute-start | bytes 1572872 | tf_op jit(solution)/shard_map/ppermute | solution.py:203
  17.9 38.2 %copy-start.3 = (bf16[2048,128]{1,0:T(8,128)(2,1)}, bf16[2048,128]{1,0:T(8,128)(2,1)S(1)}, u32[]{:S(2)}) copy-start(bf16[2048,128]{1,0:T(8,128)(2,1)S(1)} %collective-permute-done.rest_0_) | copy-start | bytes 1572868
  17.9 11.9 %collective-permute-start.5 = (bf16[2048,128]{1,0:T(8,128)(2,1)S(1)}, bf16[2048,128]{1,0:T(8,128)(2,1)S(1)}, u32[]{:S(2)}, u32[]{:S(2)}) collective-permute-start(bf16[2048,128]{1,0:T(8,128)(2,1)S(1)} %collective-permute-done.rest_0_), channel_id=1, source_target_pairs={{0,16},{16,0},{32,48},{48,32},{64,80},{80,64},{96,112},{112,96},{1... | collective-permute-start | bytes 1572872 | tf_op jit(solution)/shard_map/ppermute | solution.py:206
  19.2 12.6 %collective-permute-start.3 = (bf16[2048,128]{1,0:T(8,128)(2,1)S(1)}, bf16[2048,128]{1,0:T(8,128)(2,1)}, u32[]{:S(2)}, u32[]{:S(2)}) collective-permute-start(bf16[2048,128]{1,0:T(8,128)(2,1)S(1)} %collective-permute-done.rest_0_), channel_id=1, source_target_pairs={{0,32},{16,48},{32,64},{48,80},{64,96},{80,112},{96,0},{112,16},{1... | collective-permute-start | bytes 1572872 | tf_op jit(solution)/shard_map/ppermute | solution.py:203
  19.9 36.2 %copy-start.4 = (bf16[2048,128]{1,0:T(8,128)(2,1)}, bf16[2048,128]{1,0:T(8,128)(2,1)S(1)}, u32[]{:S(2)}) copy-start(bf16[2048,128]{1,0:T(8,128)(2,1)S(1)} %collective-permute-done.1.rest_1_) | copy-start | bytes 1572868
  29.4 26.7 %copy-start = (bf16[2048,128]{1,0:T(8,128)(2,1)}, bf16[2048,128]{1,0:T(8,128)(2,1)S(1)}, u32[]{:S(2)}) copy-start(bf16[2048,128]{1,0:T(8,128)(2,1)S(1)} %collective-permute-done.4.rest_4_) | copy-start | bytes 1572868
  29.8 26.4 %copy-start.1 = (bf16[2048,128]{1,0:T(8,128)(2,1)}, bf16[2048,128]{1,0:T(8,128)(2,1)S(1)}, u32[]{:S(2)}) copy-start(bf16[2048,128]{1,0:T(8,128)(2,1)S(1)} %collective-permute-done.5.rest_5_) | copy-start | bytes 1572868
  31.8 15.5 %collective-permute-start.8 = (bf16[2048,128]{1,0:T(8,128)(2,1)S(1)}, bf16[2048,128]{1,0:T(8,128)(2,1)S(1)}, u32[]{:S(2)}, u32[]{:S(2)}) collective-permute-start(bf16[2048,128]{1,0:T(8,128)(2,1)S(1)} %collective-permute-done.rest_0_), channel_id=1, source_target_pairs={{0,1},{1,0},{2,3},{3,2},{4,5},{5,4},{6,7},{7,6},{8,9},{9,8},{10,11... | collective-permute-start | bytes 1572872 | tf_op jit(solution)/shard_map/ppermute | solution.py:209
  37.0 9.4 %collective-permute-start.6 = (bf16[1024,128]{1,0:T(8,128)(2,1)}, bf16[1024,128]{1,0:T(8,128)(2,1)S(1)}, u32[]{:S(2)}, u32[]{:S(2)}) collective-permute-start(bf16[1024,128]{1,0:T(8,128)(2,1)} %slice.6), channel_id=1, source_target_pairs={{0,32},{16,48},{32,64},{48,80},{64,96},{80,112},{96,0},{112,16},{1... | collective-permute-start | bytes 786440 | tf_op jit(solution)/shard_map/ppermute | solution.py:203
  37.0 10.1 %collective-permute-start.7 = (bf16[1024,128]{1,0:T(8,128)(2,1)}, bf16[1024,128]{1,0:T(8,128)(2,1)}, u32[]{:S(2)}, u32[]{:S(2)}) collective-permute-start(bf16[1024,128]{1,0:T(8,128)(2,1)} %slice.7), channel_id=1, source_target_pairs={{0,96},{16,112},{32,0},{48,16},{64,32},{80,48},{96,64},{112,80},{1... | collective-permute-start | bytes 786440 | tf_op jit(solution)/shard_map/ppermute | solution.py:203
  40.5 8.6 %collective-permute-start.9 = (bf16[2048,128]{1,0:T(8,128)(2,1)S(1)}, bf16[2048,128]{1,0:T(8,128)(2,1)S(1)}, u32[]{:S(2)}, u32[]{:S(2)}) collective-permute-start(bf16[2048,128]{1,0:T(8,128)(2,1)S(1)} %collective-permute-done.1.rest_1_), channel_id=1, source_target_pairs={{0,1},{1,0},{2,3},{3,2},{4,5},{5,4},{6,7},{7,6},{8,9},{9,8},{10,11... | collective-permute-start | bytes 1572872 | tf_op jit(solution)/shard_map/ppermute | solution.py:209
  41.1 8.1 %collective-permute-start.10 = (bf16[2048,128]{1,0:T(8,128)(2,1)S(1)}, bf16[2048,128]{1,0:T(8,128)(2,1)S(1)}, u32[]{:S(2)}, u32[]{:S(2)}) collective-permute-start(bf16[2048,128]{1,0:T(8,128)(2,1)S(1)} %collective-permute-done.2.rest_2_), channel_id=1, source_target_pairs={{0,1},{1,0},{2,3},{3,2},{4,5},{5,4},{6,7},{7,6},{8,9},{9,8},{10,11... | collective-permute-start | bytes 1572872 | tf_op jit(solution)/shard_map/ppermute | solution.py:209
  46.4 9.8 %copy-start.8 = (bf16[1024,128]{1,0:T(8,128)(2,1)}, bf16[1024,128]{1,0:T(8,128)(2,1)S(1)}, u32[]{:S(2)}) copy-start(bf16[1024,128]{1,0:T(8,128)(2,1)S(1)} %collective-permute-done.6.rest_6_) | copy-start | bytes 786436
  46.4 9.7 %collective-permute-start.12 = (bf16[2048,128]{1,0:T(8,128)(2,1)S(1)}, bf16[2048,128]{1,0:T(8,128)(2,1)}, u32[]{:S(2)}, u32[]{:S(2)}) collective-permute-start(bf16[2048,128]{1,0:T(8,128)(2,1)S(1)} %collective-permute-done.4.rest_4_), channel_id=1, source_target_pairs={{0,1},{1,0},{2,3},{3,2},{4,5},{5,4},{6,7},{7,6},{8,9},{9,8},{10,11... | collective-permute-start | bytes 1572872 | tf_op jit(solution)/shard_map/ppermute | solution.py:209
  47.2 8.9 %collective-permute-start.13 = (bf16[2048,128]{1,0:T(8,128)(2,1)S(1)}, bf16[2048,128]{1,0:T(8,128)(2,1)}, u32[]{:S(2)}, u32[]{:S(2)}) collective-permute-start(bf16[2048,128]{1,0:T(8,128)(2,1)S(1)} %collective-permute-done.5.rest_5_), channel_id=1, source_target_pairs={{0,1},{1,0},{2,3},{3,2},{4,5},{5,4},{6,7},{7,6},{8,9},{9,8},{10,11... | collective-permute-start | bytes 1572872 | tf_op jit(solution)/shard_map/ppermute | solution.py:209
  47.3 8.9 %copy-start.5 = (bf16[2048,128]{1,0:T(8,128)(2,1)}, bf16[2048,128]{1,0:T(8,128)(2,1)S(1)}, u32[]{:S(2)}) copy-start(bf16[2048,128]{1,0:T(8,128)(2,1)S(1)} %collective-permute-done.8.rest_8_) | copy-start | bytes 1572868
  47.3 8.8 %collective-permute-start.11 = (bf16[2048,128]{1,0:T(8,128)(2,1)}, bf16[2048,128]{1,0:T(8,128)(2,1)}, u32[]{:S(2)}, u32[]{:S(2)}) collective-permute-start(bf16[2048,128]{1,0:T(8,128)(2,1)} %collective-permute-done.3.rest_3_), channel_id=1, source_target_pairs={{0,1},{1,0},{2,3},{3,2},{4,5},{5,4},{6,7},{7,6},{8,9},{9,8},{10,11... | collective-permute-start | bytes 1572872 | tf_op jit(solution)/shard_map/ppermute | solution.py:209
  49.0 0.8 copy-start.6
  49.1 7.1 %collective-permute-start.14 = (bf16[1024,128]{1,0:T(8,128)(2,1)S(1)}, bf16[1024,128]{1,0:T(8,128)(2,1)}, u32[]{:S(2)}, u32[]{:S(2)}) collective-permute-start(bf16[1024,128]{1,0:T(8,128)(2,1)S(1)} %collective-permute-done.6.rest_6_), channel_id=1, source_target_pairs={{0,1},{1,0},{2,3},{3,2},{4,5},{5,4},{6,7},{7,6},{8,9},{9,8},{10,11... | collective-permute-start | bytes 786440 | tf_op jit(solution)/shard_map/ppermute | solution.py:209
  49.8 0.8 copy-start.7
  49.8 6.3 %collective-permute-start.15 = (bf16[1024,128]{1,0:T(8,128)(2,1)}, bf16[1024,128]{1,0:T(8,128)(2,1)}, u32[]{:S(2)}, u32[]{:S(2)}) collective-permute-start(bf16[1024,128]{1,0:T(8,128)(2,1)} %collective-permute-done.7.rest_7_), channel_id=1, source_target_pairs={{0,1},{1,0},{2,3},{3,2},{4,5},{5,4},{6,7},{7,6},{8,9},{9,8},{10,11... | collective-permute-start | bytes 786440 | tf_op jit(solution)/shard_map/ppermute | solution.py:209

commit v3 on v2

--- a/solution.py
+++ b/solution.py
@@ -212,14 +212,6 @@
     p1 = along_x(own, 1)
     p2 = along_x(own, -1)
     p3 = along_z(own)
-    p4 = along_x(p1, 1)
-    p5 = along_x(p3, -1)
-    p6 = along_z(p1)
-    p1, p2, p3, p4, p5, p6 = lax.optimization_barrier((p1, p2, p3, p4, p5, p6))
-    p7 = along_x(p6[:half], 1)
-    p8 = along_x(p5[half:], -1)
-    mine = (p1, p2, p3, p4, p5, p6, p7, p8)
-    other = tuple(swap(x) for x in mine)
 
     lists, counts = block_lists(verticals, slashes, place, nblk, cycle)
     owner = destination // own_rows
@@ -227,6 +219,18 @@
     first_row = jnp.min(jnp.where(member, destination[:, None], ROW_CEILING), axis=0)
     sent = jnp.sum(member.astype(jnp.int32), axis=0)
     meta = jnp.stack([core, kv_index]).astype(jnp.int32)
+    small = (meta, lists, counts, first_row, sent)
+    p1, p3, small = lax.optimization_barrier((p1, p3, small))
+
+    p4 = along_x(p1, 1)
+    p5 = along_x(p3, -1)
+    p6 = along_z(p1)
+    mine = [jnp.concatenate([p1, p2, p3], axis=0)]
+    other = [swap(mine[0])]
+    p7 = along_x(p6[:half], 1)
+    p8 = along_x(p5[half:], -1)
+    mine += [jnp.concatenate([p4, p5, p6], axis=0), p7, p8]
+    other += [swap(x) for x in mine[1:]]
 
     slots = lists.shape[1]
     outgoing = pl.pallas_call(
@@ -242,7 +246,7 @@
         ],
         compiler_params=pltpu.CompilerParams(vmem_limit_bytes=60 * 1024 * 1024),
         name="attend",
-    )(meta, lists, counts, first_row, sent, queries, destination.reshape(1, rows_here), keys, values, *mine, *other)
+    )(*small, queries, destination.reshape(1, rows_here), keys, values, *mine, *other)
 
     incoming = lax.all_to_all(
         outgoing.reshape(devices, capacity, heads * DH), ("ctx", "rows"), split_axis=0, concat_axis=0, tiled=True

time: 138 us -> 132 us (0.957)
  waiting for transfers between devices: 25.8 us -> 22.1 us
  other arithmetic: 9.29 us -> 6.59 us
  blocking collectives: 39.7 us -> 37.6 us
  starting transfers between devices: 17 us -> 19.1 us
    ppermute x2, waiting for transfers between devices: 9.32 us -> 5.41 us  [along_z(): return lax.ppermute(x, 'ctx', [(c, c ^ 1) for c in range(cycle)])]
    ppermute x8 -> x4, starting transfers between devices: 5.41 us -> 8.09 us  [swap(): return lax.ppermute(x, 'rows', [(r, r ^ 1) for r in range(groups)])]
    all_to_all x1, blocking collectives: 39.7 us -> 37.6 us  [body(): lax.all_to_all(outgoing.reshape(devices, capacity, heads * DH), ('ctx', '...]
    ppermute x2, starting transfers between devices: 3.81 us -> 1.82 us  [along_z(): return lax.ppermute(x, 'ctx', [(c, c ^ 1) for c in range(cycle)])]
    ppermute x6, starting transfers between devices: 7.73 us -> 9.21 us  [along_x(): lax.ppermute(x, 'ctx', [(c, (c + 2 * step) % cycle) for c in range(cycle)])]
    unnamed x18 -> x26, local copies, waits for them, and re-layouts: 1.27 us -> 2.69 us
  transfers between devices with their start and end apart: 16 -> 12, of which waited for: 5 -> 6; matrix products, arithmetic and copies ran while one was open for 8% -> 5% of each run, Pallas kernels for 0% -> 0%
where the time goes in v3:
time: 132 us
  Pallas kernels  41.9 us (32%)
  blocking collectives  37.6 us (28%)
  waiting for transfers between devices  22.1 us (17%)
  starting transfers between devices  19.1 us (14%)
  other arithmetic  6.59 us (5%)
  local copies, waits for them, and re-layouts  4.5 us (3%)
    pallas_call x1, Pallas kernels, body(): pl.pallas_call(functools.partial(attend_kernel, [x.shape[0] for x in mine...  38.7 us
    all_to_all x1, blocking collectives, body(): lax.all_to_all(outgoing.reshape(devices, capacity, heads * DH), ('ctx', '...  37.6 us
    ppermute x6, waiting for transfers between devices, along_x(): lax.ppermute(x, 'ctx', [(c, (c + 2 * step) % cycle) for c in range(cycle)])  15.6 us
    ppermute x6, starting transfers between devices, along_x(): lax.ppermute(x, 'ctx', [(c, (c + 2 * step) % cycle) for c in range(cycle)])  9.21 us
    ppermute x4, starting transfers between devices, swap(): return lax.ppermute(x, 'rows', [(r, r ^ 1) for r in range(groups)])  8.09 us
    ppermute x2, waiting for transfers between devices, along_z(): return lax.ppermute(x, 'ctx', [(c, c ^ 1) for c in range(cycle)])  5.41 us
    pallas_call x1, Pallas kernels, body(): pl.pallas_call(arrange_kernel, out_shape=jax.ShapeDtypeStruct((own_rows,...  3.17 us
    unnamed x26, local copies, waits for them, and re-layouts  2.69 us
  transfers between devices with their start and end apart: 12, of which 6 were waited for; matrix products, arithmetic and copies ran while one was open for 5% of the time, Pallas kernels for 0%

profile of v3, /device:TPU:1, one launch (start us, length us, event | category | flops | bytes accessed | tf_op | source)
XLA Modules:
  0.0 132.1 jit_solution(6902818691286768278)
XLA Ops:
  0.0 0.0 copy-start.9
  0.0 0.0 copy-start.10
  0.0 0.0 copy-start.8
  0.0 1.4 %dynamic-slice_select_fusion = bf16[2048,128]{1,0:T(8,128)(2,1)S(1)} fusion(bf16[2048,1024]{1,0:T(8,128)(2,1)} %values.1, s32[]{:T(128)S(6)} %select_n.137, bf16[2048,1024]{1,0:T(8,128)(2,1)} %keys.1, pred[]{:T(512)S(6)} %eq.100), kind=kLoop, calls=%fused_computation.3 | loop fusion | flops 262144 | bytes 1572869 | tf_op jit(solution)/shard_map/jit(_where)/select_n | solution.py:196
  1.4 3.4 %collective-permute-start.2 = (bf16[2048,128]{1,0:T(8,128)(2,1)S(1)}, bf16[2048,128]{1,0:T(8,128)(2,1)S(1)}, u32[]{:S(2)}, u32[]{:S(2)}) collective-permute-start(bf16[2048,128]{1,0:T(8,128)(2,1)S(1)} %dynamic-slice_select_fusion), channel_id=1, source_target_pairs={{0,96},{16,112},{32,0},{48,16},{64,32},{80,48},{96,64},{112,80},{1... | collective-permute-start | bytes 1572872 | tf_op jit(solution)/shard_map/ppermute | solution.py:203
  4.8 1.6 %collective-permute-start.1 = (bf16[2048,128]{1,0:T(8,128)(2,1)S(1)}, bf16[2048,128]{1,0:T(8,128)(2,1)}, u32[]{:S(2)}, u32[]{:S(2)}) collective-permute-start(bf16[2048,128]{1,0:T(8,128)(2,1)S(1)} %dynamic-slice_select_fusion), channel_id=1, source_target_pairs={{0,16},{16,0},{32,48},{48,32},{64,80},{80,64},{96,112},{112,96},{1... | collective-permute-start | bytes 1572872 | tf_op jit(solution)/shard_map/ppermute | solution.py:206
  6.4 0.0 collective-permute-start
  6.5 0.0 copy-done.9
  6.5 0.1 broadcast_subtract_fusion
  6.5 0.0 copy-done.10
  6.5 0.1 pad_add_fusion
  6.6 0.8 and_reduce_fusion
  7.4 0.2 convert_reduce_fusion.2
  7.6 0.0 copy-done.8
  7.7 0.6 convert_reduce_fusion.1
  8.3 0.6 pad_add_fusion.1.meta
  8.9 0.6 reshape.224.counts
  9.5 1.1 select_reduce_fusion.1
  10.5 1.8 %convert_reduce_fusion = (s32[128]{0:T(128)}, s32[128]{0:T(128)}) fusion(s32[2048]{0:T(1024)S(1)} %add_select_fusion.5, s32[2048]{0:T(1024)S(1)} %copy-done.8), kind=kLoop, calls=%fused_computation | loop fusion | flops 1310464 | bytes 17408 | tf_op jit(solution)/shard_map/reduce_sum | solution.py:220
  12.3 5.4 %collective-permute-done.1 = bf16[2048,128]{1,0:T(8,128)(2,1)} collective-permute-done((bf16[2048,128]{1,0:T(8,128)(2,1)S(1)}, bf16[2048,128]{1,0:T(8,128)(2,1)}, u32[]{:S(2)}, u32[]{:S(2)}) %collective-permute-start.1) | collective-permute-done | bytes 524320 | tf_op jit(solution)/shard_map/ppermute | solution.py:206
  17.7 2.1 %collective-permute-done = bf16[2048,128]{1,0:T(8,128)(2,1)S(1)} collective-permute-done((bf16[2048,128]{1,0:T(8,128)(2,1)S(1)}, bf16[2048,128]{1,0:T(8,128)(2,1)S(1)}, u32[]{:S(2)}, u32[]{:S(2)}) %collective-permute-start) | collective-permute-done | bytes 524320 | tf_op jit(solution)/shard_map/ppermute | solution.py:203
  19.8 0.2 collective-permute-start.5
  20.0 0.0 collective-permute-start.3
  20.0 2.7 %collective-permute-start.4 = (bf16[2048,128]{1,0:T(8,128)(2,1)}, bf16[2048,128]{1,0:T(8,128)(2,1)S(1)}, u32[]{:S(2)}, u32[]{:S(2)}) collective-permute-start(bf16[2048,128]{1,0:T(8,128)(2,1)} %collective-permute-done.1), channel_id=1, source_target_pairs={{0,96},{16,112},{32,0},{48,16},{64,32},{80,48},{96,64},{112,80},{1... | collective-permute-start | bytes 1572872 | tf_op jit(solution)/shard_map/ppermute | solution.py:203
  22.8 0.0 collective-permute-done.2
  22.8 0.1 constant_dynamic-update-slice_fusion.1
  22.8 1.1 constant_dynamic-update-slice_fusion.rest_0_
  24.0 0.0 copy-start
  24.0 2.9 %collective-permute-start.8 = (bf16[6144,128]{1,0:T(8,128)(2,1)S(1)}, bf16[6144,128]{1,0:T(8,128)(2,1)S(1)}, u32[]{:S(2)}, u32[]{:S(2)}) collective-permute-start(bf16[6144,128]{1,0:T(8,128)(2,1)S(1)} %constant_dynamic-update-slice_fusion.rest_0_), channel_id=1, source_target_pairs={{0,1},{1,0},{2,3},{3,2},{4,5},{5,4},{6,7},{7,6},{8,9},{9,8},{10,11... | collective-permute-start | bytes 4718600 | tf_op jit(solution)/shard_map/ppermute | solution.py:209
  26.9 5.5 %collective-permute-done.3 = bf16[2048,128]{1,0:T(8,128)(2,1)S(1)} collective-permute-done((bf16[2048,128]{1,0:T(8,128)(2,1)S(1)}, bf16[2048,128]{1,0:T(8,128)(2,1)S(1)}, u32[]{:S(2)}, u32[]{:S(2)}) %collective-permute-start.3) | collective-permute-done | bytes 524320 | tf_op jit(solution)/shard_map/ppermute | solution.py:203
  32.4 0.0 collective-permute-done.4
  32.4 0.1 constant_dynamic-update-slice_fusion.4
  32.5 0.0 collective-permute-done.5
  32.5 0.1 constant_dynamic-update-slice_fusion.3.rest_1_
  32.6 0.0 copy-done
  32.6 0.0 copy-start.1
  32.6 3.3 %collective-permute-start.9 = (bf16[6144,128]{1,0:T(8,128)(2,1)S(1)}, bf16[6144,128]{1,0:T(8,128)(2,1)S(1)}, u32[]{:S(2)}, u32[]{:S(2)}) collective-permute-start(bf16[6144,128]{1,0:T(8,128)(2,1)S(1)} %constant_dynamic-update-slice_fusion.3.rest_1_), channel_id=1, source_target_pairs={{0,1},{1,0},{2,3},{3,2},{4,5},{5,4},{6,7},{7,6},{8,9},{9,8},{10,11... | collective-permute-start | bytes 4718600 | tf_op jit(solution)/shard_map/ppermute | solution.py:209
  35.9 3.0 %collective-permute-start.7 = (bf16[1024,128]{1,0:T(8,128)(2,1)S(1)}, bf16[1024,128]{1,0:T(8,128)(2,1)S(1)}, u32[]{:S(2)}, u32[]{:S(2)}) collective-permute-start(bf16[1024,128]{1,0:T(8,128)(2,1)S(1)} %slice.9), channel_id=1, source_target_pairs={{0,96},{16,112},{32,0},{48,16},{64,32},{80,48},{96,64},{112,80},{1... | collective-permute-start | bytes 786440 | tf_op jit(solution)/shard_map/ppermute | solution.py:203
  38.9 0.1 collective-permute-start.6
  39.0 5.6 %collective-permute-done.7.rest_3_ = bf16[1024,128]{1,0:T(8,128)(2,1)S(1)} collective-permute-done((bf16[1024,128]{1,0:T(8,128)(2,1)S(1)}, bf16[1024,128]{1,0:T(8,128)(2,1)S(1)}, u32[]{:S(2)}, u32[]{:S(2)}) %collective-permute-start.7) | collective-permute-done | bytes 262176 | tf_op jit(solution)/shard_map/ppermute | solution.py:203
  44.6 0.0 copy-start.4
  44.6 0.8 collective-permute-start.11
  45.4 2.4 %collective-permute-done.6.rest_2_ = bf16[1024,128]{1,0:T(8,128)(2,1)S(1)} collective-permute-done((bf16[1024,128]{1,0:T(8,128)(2,1)S(1)}, bf16[1024,128]{1,0:T(8,128)(2,1)S(1)}, u32[]{:S(2)}, u32[]{:S(2)}) %collective-permute-start.6) | collective-permute-done | bytes 262176 | tf_op jit(solution)/shard_map/ppermute | solution.py:203
  47.8 0.0 copy-start.5
  47.8 1.1 collective-permute-start.10
  48.9 0.0 collective-permute-done.11.rest_7_
  48.9 0.0 copy-start.6
  48.9 1.2 collective-permute-done.10.rest_6_
  50.1 0.0 copy-start.7
  50.1 0.0 collective-permute-done.8.rest_4_
  50.1 0.0 copy-start.2
  50.1 0.0 collective-permute-done.9.rest_5_
  50.1 0.7 copy-done.7
  50.8 0.6 copy-done.2
  51.4 0.0 copy-start.3
  51.4 1.2 copy-done.3
  52.5 0.0 copy-done.1
  52.5 0.0 copy-done.4
  52.5 0.0 copy-done.5
  52.5 0.0 copy-done.6
  52.5 38.7 %attend.1 = bf16[4096,256]{1,0:T(8,128)(2,1)} custom-call(s32[2]{0:T(128)} %pad_add_fusion.1.meta, s32[32,24]{1,0:T(8,128)} %bitcast.9, s32[32]{0:T(128)} %reshape.224.counts, s32[128]{0:T(128)} %get-tuple-element.15.first_row, s32[128]{0:T(128)} %get-tuple-element.16.sent, bf16[2048,256]{1,0:T(8,128)(2,1)} %q_ref.1, s32[1,2048]{1,0:T(1,128)} %bitcast.8, ...), custom_call_target="tpu_custom_call" | custom-call | tf_op jit(solution)/shard_map/attend/pallas_call | solution.py:236
  91.3 37.6 %all_to_all.5 = bf16[128,32,256]{2,1,0:T(8,128)(2,1)} all-to-all(bf16[128,32,256]{2,1,0:T(8,128)(2,1)} %bitcast.7), channel_id=1, replica_groups=mesh['ctx'=8,'rows'=16] {'ctx','rows'}, dimensions={0} | all-to-all | bytes 4194304 | tf_op jit(solution)/shard_map/all_to_all | solution.py:251
  128.9 3.2 %arrange.1 = bf16[128,4096]{1,0:T(8,128)(2,1)} custom-call(bf16[8,16,32,256]{3,2,1,0:T(8,128)(2,1)} %bitcast.6), custom_call_target="tpu_custom_call" | custom-call | tf_op jit(solution)/shard_map/arrange/pallas_call | solution.py:255
  (8 shorter events, 0.1 us)
Async XLA Ops:
  0.0 6.5 %copy-start.9 = (s32[2,16]{1,0:T(2,128)S(1)}, s32[2,16]{1,0:T(2,128)}, u32[]{:S(2)}) copy-start(s32[2,16]{1,0:T(2,128)} %param.10) | copy-start | bytes 388
  0.0 6.5 %copy-start.10 = (s32[2,8]{1,0:T(2,128)S(1)}, s32[2,8]{1,0:T(2,128)}, u32[]{:S(2)}) copy-start(s32[2,8]{1,0:T(2,128)} %param.9) | copy-start | bytes 196
  0.0 7.6 %copy-start.8 = (s32[2048]{0:T(1024)S(1)}, s32[2048]{0:T(1024)}, u32[]{:S(2)}) copy-start(s32[2048]{0:T(1024)} %param.11) | copy-start | bytes 24580
  1.4 21.4 %collective-permute-start.2 = (bf16[2048,128]{1,0:T(8,128)(2,1)S(1)}, bf16[2048,128]{1,0:T(8,128)(2,1)S(1)}, u32[]{:S(2)}, u32[]{:S(2)}) collective-permute-start(bf16[2048,128]{1,0:T(8,128)(2,1)S(1)} %dynamic-slice_select_fusion), channel_id=1, source_target_pairs={{0,96},{16,112},{32,0},{48,16},{64,32},{80,48},{96,64},{112,80},{1... | collective-permute-start | bytes 1572872 | tf_op jit(solution)/shard_map/ppermute | solution.py:203
  4.8 12.9 %collective-permute-start.1 = (bf16[2048,128]{1,0:T(8,128)(2,1)S(1)}, bf16[2048,128]{1,0:T(8,128)(2,1)}, u32[]{:S(2)}, u32[]{:S(2)}) collective-permute-start(bf16[2048,128]{1,0:T(8,128)(2,1)S(1)} %dynamic-slice_select_fusion), channel_id=1, source_target_pairs={{0,16},{16,0},{32,48},{48,32},{64,80},{80,64},{96,112},{112,96},{1... | collective-permute-start | bytes 1572872 | tf_op jit(solution)/shard_map/ppermute | solution.py:206
  6.4 13.4 %collective-permute-start = (bf16[2048,128]{1,0:T(8,128)(2,1)S(1)}, bf16[2048,128]{1,0:T(8,128)(2,1)S(1)}, u32[]{:S(2)}, u32[]{:S(2)}) collective-permute-start(bf16[2048,128]{1,0:T(8,128)(2,1)S(1)} %dynamic-slice_select_fusion), channel_id=1, source_target_pairs={{0,32},{16,48},{32,64},{48,80},{64,96},{80,112},{96,0},{112,16},{1... | collective-permute-start | bytes 1572872 | tf_op jit(solution)/shard_map/ppermute | solution.py:203
  19.8 12.7 %collective-permute-start.5 = (bf16[2048,128]{1,0:T(8,128)(2,1)S(1)}, bf16[2048,128]{1,0:T(8,128)(2,1)S(1)}, u32[]{:S(2)}, u32[]{:S(2)}) collective-permute-start(bf16[2048,128]{1,0:T(8,128)(2,1)S(1)} %collective-permute-done), channel_id=1, source_target_pairs={{0,16},{16,0},{32,48},{48,32},{64,80},{80,64},{96,112},{112,96},{1... | collective-permute-start | bytes 1572872 | tf_op jit(solution)/shard_map/ppermute | solution.py:206
  20.0 12.4 %collective-permute-start.3 = (bf16[2048,128]{1,0:T(8,128)(2,1)S(1)}, bf16[2048,128]{1,0:T(8,128)(2,1)S(1)}, u32[]{:S(2)}, u32[]{:S(2)}) collective-permute-start(bf16[2048,128]{1,0:T(8,128)(2,1)S(1)} %collective-permute-done), channel_id=1, source_target_pairs={{0,32},{16,48},{32,64},{48,80},{64,96},{80,112},{96,0},{112,16},{1... | collective-permute-start | bytes 1572872 | tf_op jit(solution)/shard_map/ppermute | solution.py:203
  20.0 12.4 %collective-permute-start.4 = (bf16[2048,128]{1,0:T(8,128)(2,1)}, bf16[2048,128]{1,0:T(8,128)(2,1)S(1)}, u32[]{:S(2)}, u32[]{:S(2)}) collective-permute-start(bf16[2048,128]{1,0:T(8,128)(2,1)} %collective-permute-done.1), channel_id=1, source_target_pairs={{0,96},{16,112},{32,0},{48,16},{64,32},{80,48},{96,64},{112,80},{1... | collective-permute-start | bytes 1572872 | tf_op jit(solution)/shard_map/ppermute | solution.py:203
  24.0 8.6 %copy-start = (bf16[6144,128]{1,0:T(8,128)(2,1)}, bf16[6144,128]{1,0:T(8,128)(2,1)S(1)}, u32[]{:S(2)}) copy-start(bf16[6144,128]{1,0:T(8,128)(2,1)S(1)} %constant_dynamic-update-slice_fusion.rest_0_) | copy-start | bytes 4718596
  24.0 26.1 %collective-permute-start.8 = (bf16[6144,128]{1,0:T(8,128)(2,1)S(1)}, bf16[6144,128]{1,0:T(8,128)(2,1)S(1)}, u32[]{:S(2)}, u32[]{:S(2)}) collective-permute-start(bf16[6144,128]{1,0:T(8,128)(2,1)S(1)} %constant_dynamic-update-slice_fusion.rest_0_), channel_id=1, source_target_pairs={{0,1},{1,0},{2,3},{3,2},{4,5},{5,4},{6,7},{7,6},{8,9},{9,8},{10,11... | collective-permute-start | bytes 4718600 | tf_op jit(solution)/shard_map/ppermute | solution.py:209
  32.6 20.0 %copy-start.1 = (bf16[6144,128]{1,0:T(8,128)(2,1)}, bf16[6144,128]{1,0:T(8,128)(2,1)S(1)}, u32[]{:S(2)}) copy-start(bf16[6144,128]{1,0:T(8,128)(2,1)S(1)} %constant_dynamic-update-slice_fusion.3.rest_1_) | copy-start | bytes 4718596
  32.6 17.5 %collective-permute-start.9 = (bf16[6144,128]{1,0:T(8,128)(2,1)S(1)}, bf16[6144,128]{1,0:T(8,128)(2,1)S(1)}, u32[]{:S(2)}, u32[]{:S(2)}) collective-permute-start(bf16[6144,128]{1,0:T(8,128)(2,1)S(1)} %constant_dynamic-update-slice_fusion.3.rest_1_), channel_id=1, source_target_pairs={{0,1},{1,0},{2,3},{3,2},{4,5},{5,4},{6,7},{7,6},{8,9},{9,8},{10,11... | collective-permute-start | bytes 4718600 | tf_op jit(solution)/shard_map/ppermute | solution.py:209
  35.9 8.7 %collective-permute-start.7 = (bf16[1024,128]{1,0:T(8,128)(2,1)S(1)}, bf16[1024,128]{1,0:T(8,128)(2,1)S(1)}, u32[]{:S(2)}, u32[]{:S(2)}) collective-permute-start(bf16[1024,128]{1,0:T(8,128)(2,1)S(1)} %slice.9), channel_id=1, source_target_pairs={{0,96},{16,112},{32,0},{48,16},{64,32},{80,48},{96,64},{112,80},{1... | collective-permute-start | bytes 786440 | tf_op jit(solution)/shard_map/ppermute | solution.py:203
  38.9 8.9 %collective-permute-start.6 = (bf16[1024,128]{1,0:T(8,128)(2,1)S(1)}, bf16[1024,128]{1,0:T(8,128)(2,1)S(1)}, u32[]{:S(2)}, u32[]{:S(2)}) collective-permute-start(bf16[1024,128]{1,0:T(8,128)(2,1)S(1)} %slice.8), channel_id=1, source_target_pairs={{0,32},{16,48},{32,64},{48,80},{64,96},{80,112},{96,0},{112,16},{1... | collective-permute-start | bytes 786440 | tf_op jit(solution)/shard_map/ppermute | solution.py:203
  44.6 7.9 %copy-start.4 = (bf16[1024,128]{1,0:T(8,128)(2,1)}, bf16[1024,128]{1,0:T(8,128)(2,1)S(1)}, u32[]{:S(2)}) copy-start(bf16[1024,128]{1,0:T(8,128)(2,1)S(1)} %collective-permute-done.7.rest_3_) | copy-start | bytes 786436
  44.6 4.3 %collective-permute-start.11 = (bf16[1024,128]{1,0:T(8,128)(2,1)S(1)}, bf16[1024,128]{1,0:T(8,128)(2,1)S(1)}, u32[]{:S(2)}, u32[]{:S(2)}) collective-permute-start(bf16[1024,128]{1,0:T(8,128)(2,1)S(1)} %collective-permute-done.7.rest_3_), channel_id=1, source_target_pairs={{0,1},{1,0},{2,3},{3,2},{4,5},{5,4},{6,7},{7,6},{8,9},{9,8},{10,11... | collective-permute-start | bytes 786440 | tf_op jit(solution)/shard_map/ppermute | solution.py:209
  47.8 4.8 %copy-start.5 = (bf16[1024,128]{1,0:T(8,128)(2,1)}, bf16[1024,128]{1,0:T(8,128)(2,1)S(1)}, u32[]{:S(2)}) copy-start(bf16[1024,128]{1,0:T(8,128)(2,1)S(1)} %collective-permute-done.6.rest_2_) | copy-start | bytes 786436
  47.8 2.3 %collective-permute-start.10 = (bf16[1024,128]{1,0:T(8,128)(2,1)S(1)}, bf16[1024,128]{1,0:T(8,128)(2,1)S(1)}, u32[]{:S(2)}, u32[]{:S(2)}) collective-permute-start(bf16[1024,128]{1,0:T(8,128)(2,1)S(1)} %collective-permute-done.6.rest_2_), channel_id=1, source_target_pairs={{0,1},{1,0},{2,3},{3,2},{4,5},{5,4},{6,7},{7,6},{8,9},{9,8},{10,11... | collective-permute-start | bytes 786440 | tf_op jit(solution)/shard_map/ppermute | solution.py:209
  48.9 3.6 %copy-start.6 = (bf16[1024,128]{1,0:T(8,128)(2,1)}, bf16[1024,128]{1,0:T(8,128)(2,1)S(1)}, u32[]{:S(2)}) copy-start(bf16[1024,128]{1,0:T(8,128)(2,1)S(1)} %collective-permute-done.11.rest_7_) | copy-start | bytes 786436
  50.1 0.7 copy-start.7
  50.1 1.3 copy-start.2
  51.4 1.2 copy-start.3

commit v4 on v3

v4 whole, which is shorter than its diff:
```python
import functools

import jax
import jax.numpy as jnp
from jax import lax
from jax.experimental import pallas as pl
from jax.experimental.pallas import tpu as pltpu
from jax.sharding import PartitionSpec as P

HEADS = 32
KV_HEADS = 8
DH = 128
BLOCK = 128
NEG = -1e30
ROW_CEILING = 1 << 30
EMPTY = 1048576.0
SCALE2 = DH**-0.5 * 1.4426950408889634
GROUP = 4
SLOT = 32
PIECE = {(0, 0): 0, (3, 0): 1, (1, 0): 2, (0, 1): 3, (2, 0): 4, (1, 1): 5, (3, 1): 6, (2, 1): 7}
ANY = pl.BlockSpec(memory_space=pl.ANY)
SMEM = pl.BlockSpec(memory_space=pltpu.SMEM)
VMEM = pl.BlockSpec(memory_space=pltpu.VMEM)


def dot_t(a, b):
    return lax.dot_general(a, b, (((1,), (1,)), ((), ())), preferred_element_type=jnp.float32)


def own_kernel(meta, keys, values, own_ref, keys_ref, values_ref, value_s, sem):
    column = pl.ds(pl.multiple_of(meta[1] * DH, DH), DH)
    value_copy = pltpu.make_async_copy(values.at[:, column], value_s, sem.at[0])
    key_copy = pltpu.make_async_copy(keys.at[:, column], keys_ref, sem.at[1])
    value_copy.start()
    key_copy.start()
    value_copy.wait()
    for start in range(0, value_s.shape[0], BLOCK):
        rows = slice(start, start + BLOCK)
        values_ref[rows, :] = value_s[rows, :].T
    key_copy.wait()

    @pl.when(meta[0] == 0)
    def _():
        own_ref[...] = keys_ref[...]

    @pl.when(meta[0] != 0)
    def _():
        own_ref[...] = values_ref[...]


def attend_kernel(sizes, slots, heads, meta, lists, counts, sent, start, q_ref, rank_ref, *rest):
    rest = list(rest)
    take = lambda n: [rest.pop(0) for _ in range(n)]
    pieces = len(sizes)
    own, mine, other = take(2), take(pieces), take(pieces)
    out_ref, k_s, v_s = take(3)
    score_s = [take(heads), take(heads)]
    peak_s = [take(heads), take(heads)]
    att, sorted_s, sem = take(3)
    shard = q_ref.shape[0]
    nblk = shard // BLOCK
    core = meta[0]
    key_copies, value_copies = [], []
    for number, (ref, to, held) in enumerate(zip(own, (k_s, v_s), (key_copies, value_copies))):
        copy = pltpu.make_async_copy(ref, to.at[pl.ds(0, shard)], sem.at[number])
        copy.start()
        held.append(copy)
    begin = shard
    for p in range(pieces):
        spot = pl.ds(begin, sizes[p])
        begin += sizes[p]
        number = 2 + 2 * p

        @pl.when(core == 0)
        def _():
            pltpu.make_async_copy(mine[p], k_s.at[spot], sem.at[number]).start()
            pltpu.make_async_copy(other[p], v_s.at[spot], sem.at[number + 1]).start()

        @pl.when(core != 0)
        def _():
            pltpu.make_async_copy(other[p], k_s.at[spot], sem.at[number]).start()
            pltpu.make_async_copy(mine[p], v_s.at[spot], sem.at[number + 1]).start()

        key_copies.append(pltpu.make_async_copy(mine[p], k_s.at[spot], sem.at[number]))
        value_copies.append(pltpu.make_async_copy(mine[p], v_s.at[spot], sem.at[number + 1]))

    def block_of(ref, index):
        return ref[pl.ds(pl.multiple_of(index * BLOCK, BLOCK), BLOCK), :]

    def lane_of(h):
        return slice(h * DH, (h + 1) * DH)

    chunks = [[-1]] + [list(range(c, min(c + GROUP, slots))) for c in range(0, slots, GROUP)]

    def place(slot):
        return slice((slot + 1) * BLOCK, (slot + 2) * BLOCK)

    def fold(op, reduced, parts):
        return functools.reduce(op, [reduced(p.reshape(-1, 8, BLOCK), axis=0) for p in parts])

    def score(qb, h, turn, group, peaks):
        row = h * nblk + qb
        query = block_of(q_ref, qb)[:, lane_of(h)]
        if group == [-1]:
            tri = lax.broadcasted_iota(jnp.int32, (BLOCK, BLOCK), 0) <= lax.broadcasted_iota(
                jnp.int32, (BLOCK, BLOCK), 1
            )
            parts = [jnp.where(tri, dot_t(block_of(k_s, qb), query), NEG)]
        else:
            keys_block = jnp.concatenate([block_of(k_s, lists[row, u]) for u in group], axis=0)
            scores = dot_t(keys_block, query)
            parts = [
                jnp.where(u < counts[row], scores[i * BLOCK : (i + 1) * BLOCK], NEG) for i, u in enumerate(group)
            ]
        for u, one in zip(group, parts):
            score_s[turn][h][place(u), :] = one
        peaks[h] = fold(jnp.maximum, jnp.max, parts + ([peaks[h]] if h in peaks else []))
        if group == chunks[-1]:
            peak_s[turn][h][...] = peaks[h]

    def mix(qb, h, turn, group, state):
        high, total, mixed = state
        row = h * nblk + qb
        weights = [jnp.exp2((score_s[turn][h][place(u), :] - high) * SCALE2) for u in group]
        low = jnp.concatenate([w.astype(jnp.bfloat16) for w in weights], axis=0)
        values_block = jnp.concatenate([block_of(v_s, qb if u < 0 else lists[row, u]) for u in group], axis=1)
        fresh = jnp.dot(values_block, low, preferred_element_type=jnp.float32)
        total = fold(jnp.add, jnp.sum, weights + ([] if total is None else [total]))
        return high, total, fresh if mixed is None else mixed + fresh

    def phase(qb, turn, ahead):
        if qb is not None:
            states = [(jnp.max(peak_s[turn][h][...], axis=0, keepdims=True), None, None) for h in range(heads)]
        peaks = {}
        for group in chunks:
            for h in range(heads):
                score(ahead, h, 1 - turn, group, peaks)
            if qb is not None:
                for h in range(heads):
                    states[h] = mix(qb, h, turn, group, states[h])
        if qb is not None:
            for h in range(heads):
                _, total, mixed = states[h]
                attended = mixed / jnp.sum(total, axis=0, keepdims=True)
                rows = pl.ds(pl.multiple_of((qb * heads + h) * DH, DH), DH)
                att[rows, :] = attended.astype(jnp.bfloat16)

    for copy in key_copies:
        copy.wait()

    def lead(qb, _):
        phase(None, 1, qb)
        return 0

    lax.fori_loop(0, jnp.minimum(counts[0], 0) + 1, lead, 0)
    for copy in value_copies:
        copy.wait()

    def two_blocks(pair, _):
        qb = 2 * pair
        phase(qb, 0, qb + 1)
        phase(qb + 1, 1, jnp.minimum(qb + 2, nblk - 1))
        return 0

    lax.fori_loop(0, nblk // 2, two_blocks, 0)
    scatter_rows(sent, start, rank_ref, att, sorted_s, out_ref)


def scatter_rows(sent, start, rank_ref, att, sorted_s, out_ref):
    shard = rank_ref.shape[1]
    nblk = shard // BLOCK
    width = att.shape[0] // nblk
    owners = sent.shape[0]
    batch = 512

    def per_batch(step, _):
        place = lax.broadcasted_iota(jnp.int32, (batch, shard), 0)
        hot = jnp.where(rank_ref[...] - step * batch == place, 1.0, 0.0).astype(jnp.bfloat16)
        rows = pl.ds(pl.multiple_of(step * batch, batch), batch)
        sorted_s[rows, :] = dot_t(hot, jnp.concatenate([att[i * width : (i + 1) * width, :] for i in range(nblk)], axis=1))
        return 0

    lax.fori_loop(0, shard // batch, per_batch, 0)
    sorted_s[shard:, :] = jnp.zeros((SLOT + 8, width), jnp.float32)

    def per_owners(step, _):
        line = lax.broadcasted_iota(jnp.int32, (SLOT, width), 0)
        for u in range(8):
            owner = step * 8 + u
            shift = lax.rem(start[owner], 8)
            rows = sorted_s[pl.ds(pl.multiple_of(start[owner] - shift, 8), SLOT + 8), :]
            rows = pltpu.roll(rows, SLOT + 8 - shift, 0)[:SLOT]
            kept = jnp.where(line < sent[owner], rows, EMPTY).astype(jnp.bfloat16)
            out_ref[pl.ds(pl.multiple_of(owner * SLOT, SLOT), SLOT), :] = kept
        return 0

    lax.fori_loop(0, owners // 8, per_owners, 0)


def arrange_kernel(in_ref, out_ref):
    shards, groups, capacity, width = in_ref.shape
    slots = shards * capacity
    rows = out_ref.shape[0]
    block = in_ref[:, 0].reshape(slots, width)
    used = jnp.where(block[:, :rows].astype(jnp.float32) < EMPTY / 2, 1.0, 0.0).astype(jnp.bfloat16)
    one = lax.broadcasted_iota(jnp.int32, (slots, slots), 0)
    two = lax.broadcasted_iota(jnp.int32, (slots, slots), 1)
    contract = (((0,), (0,)), ((), ()))
    before = lax.dot_general(
        used, jnp.where(one < two, 1.0, 0.0).astype(jnp.bfloat16), contract, preferred_element_type=jnp.float32
    )
    here = lax.dot_general(
        used, jnp.where(one == two, 1.0, 0.0).astype(jnp.bfloat16), contract, preferred_element_type=jnp.float32
    )
    line = lax.broadcasted_iota(jnp.int32, (rows, slots), 0).astype(jnp.float32)
    pick = jnp.where((before == line) & (here > 0.5), 1.0, 0.0).astype(jnp.bfloat16)
    for g in range(groups):
        block = in_ref[:, g].reshape(slots, width)
        out_ref[:, g * width : (g + 1) * width] = jnp.dot(pick, block, preferred_element_type=jnp.float32).astype(
            jnp.bfloat16
        )


def block_lists(verticals, slashes, place, nblk, nshards):
    heads = verticals.shape[0]
    query_blocks = place * nblk + jnp.arange(nblk, dtype=jnp.int32)
    vertical = jnp.broadcast_to(verticals[:, None, :], (heads, nblk, verticals.shape[1]))
    slash = query_blocks[None, :, None] - slashes[:, None, :]
    cand = jnp.concatenate([vertical, slash], axis=2)
    slots = cand.shape[2]
    order = jnp.arange(slots, dtype=jnp.int32)
    earlier = order[None, :] < order[:, None]
    repeated = jnp.any((cand[:, :, :, None] == cand[:, :, None, :]) & earlier[None, None], axis=3)
    valid = (cand >= 0) & (cand < query_blocks[None, :, None]) & jnp.logical_not(repeated)
    source = cand // nblk
    dx = (source // 2 - place // 2) % (nshards // 2)
    dz = (source - place) % 2
    piece = jnp.zeros_like(cand)
    for (ox, oz), number in PIECE.items():
        piece = jnp.where((dx == ox) & (dz == oz), number, piece)
    local = jnp.clip(piece * nblk + cand % nblk, 0, nshards * nblk - 1)
    rank = jnp.sum((valid[:, :, None, :] & earlier[None, None]).astype(jnp.int32), axis=3)
    chosen = valid[:, :, :, None] & (rank[:, :, :, None] == order)
    lists = jnp.sum(jnp.where(chosen, local[:, :, :, None], 0), axis=2)
    return lists.reshape(heads * nblk, slots), jnp.sum(valid.astype(jnp.int32), axis=2).reshape(heads * nblk)


def body(queries, keys, values, verticals, slashes, destination):
    cycle = lax.axis_size("ctx")
    groups = lax.axis_size("rows")
    place = lax.axis_index("ctx")
    group = lax.axis_index("rows")
    rows_here = queries.shape[0]
    heads = verticals.shape[0]
    nblk = rows_here // BLOCK
    devices = cycle * groups
    own_rows = rows_here // groups
    kv_index = group * heads // (HEADS // KV_HEADS)
    core = group % 2

    meta = jnp.stack([core, kv_index]).astype(jnp.int32)
    own, *here = pl.pallas_call(
        own_kernel,
        out_shape=[jax.ShapeDtypeStruct((rows_here, DH), jnp.bfloat16)] * 3,
        in_specs=[SMEM, ANY, ANY],
        out_specs=[VMEM] * 3,
        scratch_shapes=[pltpu.VMEM((rows_here, DH), jnp.bfloat16), pltpu.SemaphoreType.DMA((2,))],
        compiler_params=pltpu.CompilerParams(vmem_limit_bytes=24 * 1024 * 1024),
        name="own",
    )(meta, keys, values)

    def along_x(x, step):
        return lax.ppermute(x, "ctx", [(c, (c + 2 * step) % cycle) for c in range(cycle)])

    def along_z(x):
        return lax.ppermute(x, "ctx", [(c, c ^ 1) for c in range(cycle)])

    def swap(x):
        return lax.ppermute(x, "rows", [(r, r ^ 1) for r in range(groups)])

    half = rows_here // 2
    p1 = along_x(own, 1)
    p2 = along_x(own, -1)
    p3 = along_z(own)

    lists, counts = block_lists(verticals, slashes, place, nblk, cycle)
    owner = destination // own_rows
    member = owner[:, None] == jnp.arange(devices, dtype=jnp.int32)[None, :]
    first_row = jnp.min(jnp.where(member, destination[:, None], ROW_CEILING), axis=0)
    sent = jnp.sum(member.astype(jnp.int32), axis=0)
    numbers = jnp.arange(devices, dtype=jnp.int32)
    start = jnp.sum(jnp.where(numbers[:, None] < numbers[None, :], sent[:, None], 0), axis=0)
    rank = destination + jnp.sum(jnp.where(member, (start - first_row)[None, :], 0), axis=1)
    small = (lists, counts, sent, start, rank.reshape(1, rows_here))
    p1, p3, small = lax.optimization_barrier((p1, p3, small))

    p4 = along_x(p1, 1)
    p5 = along_x(p3, -1)
    p6 = along_z(p1)
    mine = [jnp.concatenate([p1, p2, p3], axis=0)]
    other = [swap(mine[0])]
    p7 = along_x(p6[:half], 1)
    p8 = along_x(p5[half:], -1)
    mine += [jnp.concatenate([p4, p5, p6], axis=0), p7, p8]
    other += [swap(x) for x in mine[1:]]

    lists, counts, sent, start, rank = small
    slots = lists.shape[1]
    outgoing = pl.pallas_call(
        functools.partial(attend_kernel, [x.shape[0] for x in mine], slots, heads),
        out_shape=jax.ShapeDtypeStruct((devices * SLOT, heads * DH), jnp.bfloat16),
        in_specs=[SMEM] * 5 + [VMEM] * 2 + [ANY] * (2 + 2 * len(mine)),
        out_specs=VMEM,
        scratch_shapes=[pltpu.VMEM((cycle * rows_here, DH), jnp.bfloat16)] * 2
        + [pltpu.VMEM(((slots + 1) * BLOCK, BLOCK), jnp.float32)] * (2 * heads)
        + [pltpu.VMEM((8, BLOCK), jnp.float32)] * (2 * heads)
        + [
            pltpu.VMEM((nblk * heads * DH, BLOCK), jnp.bfloat16),
            pltpu.VMEM((rows_here + SLOT + 8, heads * DH), jnp.float32),
            pltpu.SemaphoreType.DMA((2 + 2 * len(mine),)),
        ],
        compiler_params=pltpu.CompilerParams(vmem_limit_bytes=28 * 1024 * 1024),
        name="attend",
    )(meta, lists, counts, sent, start, queries, rank, *here, *mine, *other)

    incoming = lax.all_to_all(
        outgoing.reshape(devices, SLOT, heads * DH), ("ctx", "rows"), split_axis=0, concat_axis=0, tiled=True
    )
    incoming = incoming.reshape(cycle, groups, SLOT, heads * DH)
    return pl.pallas_call(
        arrange_kernel,
        out_shape=jax.ShapeDtypeStruct((own_rows, groups * heads * DH), jnp.bfloat16),
        in_specs=[VMEM],
        out_specs=VMEM,
        compiler_params=pltpu.CompilerParams(vmem_limit_bytes=28 * 1024 * 1024),
        name="arrange",
    )(incoming)


def solution(mesh):
    placed = (
        P("ctx", "rows"),
        P("ctx", None),
        P("ctx", None),
        P("rows", None),
        P("rows", None),
        P("ctx"),
    )
    return jax.shard_map(
        body, mesh=mesh, in_specs=placed, out_specs=P(("ctx", "rows"), None), check_vma=False
    )
```

time: 132 us -> 119 us (0.902)
  Pallas kernels: 41.9 us -> 28.5 us
  waiting for transfers between devices: 22.1 us -> 24.7 us
  other arithmetic: 6.59 us -> 4.3 us
    pallas_call x1, Pallas kernels: 38.7 us -> 25.8 us  [body(): pl.pallas_call(functools.partial(attend_kernel, [x.shape[0] for x in mine...]
    unnamed x26 -> x16, local copies, waits for them, and re-layouts: 2.69 us -> 4.6 us
    pallas_call x1, Pallas kernels: 3.17 us -> 1.58 us  [body(): pl.pallas_call(arrange_kernel, out_shape=jax.ShapeDtypeStruct((own_rows,...]
    ppermute x2, waiting for transfers between devices: 5.41 us -> 6.8 us  [along_z(): return lax.ppermute(x, 'ctx', [(c, c ^ 1) for c in range(cycle)])]
    select_n x1 -> x0, other arithmetic: 1.36 us -> none  [body(): jnp.where(core == 0, lax.dynamic_slice_in_dim(keys, kv_index * DH, DH, 1)...]
  transfers between devices with their start and end apart: 12 -> 12, of which waited for: 6 -> 6; matrix products, arithmetic and copies ran while one was open for 5% -> 4% of each run, Pallas kernels for 0% -> 0%
where the time goes in v4:
time: 119 us
  blocking collectives  37.3 us (31%)
  Pallas kernels  28.5 us (24%)
  waiting for transfers between devices  24.7 us (21%)
  starting transfers between devices  18.9 us (16%)
  local copies, waits for them, and re-layouts  4.86 us (4%)
  other arithmetic  4.3 us (4%)
    all_to_all x1, blocking collectives, body(): lax.all_to_all(outgoing.reshape(devices, SLOT, heads * DH), ('ctx', 'rows...  37.3 us
    pallas_call x1, Pallas kernels, body(): pl.pallas_call(functools.partial(attend_kernel, [x.shape[0] for x in mine...  25.8 us
    ppermute x6, waiting for transfers between devices, along_x(): lax.ppermute(x, 'ctx', [(c, (c + 2 * step) % cycle) for c in range(cycle)])  16.7 us
    ppermute x6, starting transfers between devices, along_x(): lax.ppermute(x, 'ctx', [(c, (c + 2 * step) % cycle) for c in range(cycle)])  8.99 us
    ppermute x4, starting transfers between devices, swap(): return lax.ppermute(x, 'rows', [(r, r ^ 1) for r in range(groups)])  8.09 us
    ppermute x2, waiting for transfers between devices, along_z(): return lax.ppermute(x, 'ctx', [(c, c ^ 1) for c in range(cycle)])  6.8 us
    unnamed x16, local copies, waits for them, and re-layouts  4.6 us
  transfers between devices with their start and end apart: 12, of which 6 were waited for; matrix products, arithmetic and copies ran while one was open for 4% of the time, Pallas kernels for 0%

profile of v4, /device:TPU:1, one launch (start us, length us, event | category | flops | bytes accessed | tf_op | source)
XLA Modules:
  0.0 118.7 jit_solution(12557732405597803110)
XLA Ops:
  0.0 0.1 pad_add_fusion.1.meta
  0.1 0.0 copy-start
  0.1 2.2 %copy-done = bf16[2048,1024]{1,0:T(8,128)(2,1)S(1)} copy-done((bf16[2048,1024]{1,0:T(8,128)(2,1)S(1)}, bf16[2048,1024]{1,0:T(8,128)(2,1)}, u32[]{:S(2)}) %copy-start) | copy-done | bytes 4194328
  2.3 0.0 copy-start.1
  2.3 2.2 %copy-done.1 = bf16[2048,1024]{1,0:T(8,128)(2,1)S(1)} copy-done((bf16[2048,1024]{1,0:T(8,128)(2,1)S(1)}, bf16[2048,1024]{1,0:T(8,128)(2,1)}, u32[]{:S(2)}) %copy-start.1) | copy-done | bytes 4194328
  4.5 0.0 copy-start.3
  4.5 0.0 copy-start.4
  4.5 0.0 copy-start.5
  4.5 1.1 own.1
  5.5 3.4 %collective-permute-start.2 = (bf16[2048,128]{1,0:T(8,128)(2,1)S(1)}, bf16[2048,128]{1,0:T(8,128)(2,1)S(1)}, u32[]{:S(2)}, u32[]{:S(2)}) collective-permute-start(bf16[2048,128]{1,0:T(8,128)(2,1)S(1)} %get-tuple-element.15), channel_id=1, source_target_pairs={{0,96},{16,112},{32,0},{48,16},{64,32},{80,48},{96,64},{112,80},{1... | collective-permute-start | bytes 1572872 | tf_op jit(solution)/shard_map/ppermute | solution.py:273
  8.9 1.6 %collective-permute-start.1 = (bf16[2048,128]{1,0:T(8,128)(2,1)S(1)}, bf16[2048,128]{1,0:T(8,128)(2,1)S(1)}, u32[]{:S(2)}, u32[]{:S(2)}) collective-permute-start(bf16[2048,128]{1,0:T(8,128)(2,1)S(1)} %get-tuple-element.15), channel_id=1, source_target_pairs={{0,16},{16,0},{32,48},{48,32},{64,80},{80,64},{96,112},{112,96},{1... | collective-permute-start | bytes 1572872 | tf_op jit(solution)/shard_map/ppermute | solution.py:276
  10.5 0.0 collective-permute-start
  10.6 0.0 copy-done.3
  10.6 1.2 %select_reduce_fusion.1 = (s32[128]{0:T(128)S(1)}, s32[128]{0:T(128)S(1)}) fusion(s32[2048]{0:T(1024)S(1)} %copy-done.3, s32[2048]{0:T(1024)S(1)} %add_select_fusion.5), kind=kLoop, calls=%fused_computation.1 | loop fusion | flops 1310464 | bytes 17408 | tf_op jit(solution)/shard_map/reduce_min | solution.py:289
  11.8 0.1 select_reduce_fusion.3.start
  11.9 0.0 copy-done.4
  11.9 0.1 broadcast_subtract_fusion
  12.0 0.0 copy-done.5
  12.0 0.1 pad_add_fusion
  12.1 0.8 and_reduce_fusion
  12.9 0.2 convert_reduce_fusion.2
  13.1 0.6 select_reduce_fusion
  13.8 0.1 reshape.230.counts
  13.8 0.6 convert_reduce_fusion.1
  14.5 0.5 select_reduce_fusion.2
  15.0 6.8 %collective-permute-done.1 = bf16[2048,128]{1,0:T(8,128)(2,1)S(1)} collective-permute-done((bf16[2048,128]{1,0:T(8,128)(2,1)S(1)}, bf16[2048,128]{1,0:T(8,128)(2,1)S(1)}, u32[]{:S(2)}, u32[]{:S(2)}) %collective-permute-start.1) | collective-permute-done | bytes 524320 | tf_op jit(solution)/shard_map/ppermute | solution.py:276
  21.8 2.2 %collective-permute-done = bf16[2048,128]{1,0:T(8,128)(2,1)S(1)} collective-permute-done((bf16[2048,128]{1,0:T(8,128)(2,1)S(1)}, bf16[2048,128]{1,0:T(8,128)(2,1)S(1)}, u32[]{:S(2)}, u32[]{:S(2)}) %collective-permute-start) | collective-permute-done | bytes 524320 | tf_op jit(solution)/shard_map/ppermute | solution.py:273
  23.9 0.2 collective-permute-start.5
  24.1 0.0 collective-permute-start.3
  24.2 2.7 %collective-permute-start.4 = (bf16[2048,128]{1,0:T(8,128)(2,1)S(1)}, bf16[2048,128]{1,0:T(8,128)(2,1)S(1)}, u32[]{:S(2)}, u32[]{:S(2)}) collective-permute-start(bf16[2048,128]{1,0:T(8,128)(2,1)S(1)} %collective-permute-done.1), channel_id=1, source_target_pairs={{0,96},{16,112},{32,0},{48,16},{64,32},{80,48},{96,64},{112,80},{1... | collective-permute-start | bytes 1572872 | tf_op jit(solution)/shard_map/ppermute | solution.py:273
  26.9 0.0 collective-permute-done.2
  26.9 0.1 constant_dynamic-update-slice_fusion.1
  27.0 0.1 constant_dynamic-update-slice_fusion.rest_2_
  27.1 2.9 %collective-permute-start.8 = (bf16[6144,128]{1,0:T(8,128)(2,1)S(1)}, bf16[6144,128]{1,0:T(8,128)(2,1)S(1)}, u32[]{:S(2)}, u32[]{:S(2)}) collective-permute-start(bf16[6144,128]{1,0:T(8,128)(2,1)S(1)} %constant_dynamic-update-slice_fusion.rest_2_), channel_id=1, source_target_pairs={{0,1},{1,0},{2,3},{3,2},{4,5},{5,4},{6,7},{7,6},{8,9},{9,8},{10,11... | collective-permute-start | bytes 4718600 | tf_op jit(solution)/shard_map/ppermute | solution.py:279
  30.0 6.5 %collective-permute-done.3 = bf16[2048,128]{1,0:T(8,128)(2,1)S(1)} collective-permute-done((bf16[2048,128]{1,0:T(8,128)(2,1)S(1)}, bf16[2048,128]{1,0:T(8,128)(2,1)S(1)}, u32[]{:S(2)}, u32[]{:S(2)}) %collective-permute-start.3) | collective-permute-done | bytes 524320 | tf_op jit(solution)/shard_map/ppermute | solution.py:273
  36.5 0.0 copy-start.2
  36.5 0.0 collective-permute-done.4
  36.5 0.1 constant_dynamic-update-slice_fusion.4
  36.6 0.0 collective-permute-done.5
  36.6 0.1 constant_dynamic-update-slice_fusion.3.rest_3_
  36.7 3.3 %collective-permute-start.9 = (bf16[6144,128]{1,0:T(8,128)(2,1)S(1)}, bf16[6144,128]{1,0:T(8,128)(2,1)S(1)}, u32[]{:S(2)}, u32[]{:S(2)}) collective-permute-start(bf16[6144,128]{1,0:T(8,128)(2,1)S(1)} %constant_dynamic-update-slice_fusion.3.rest_3_), channel_id=1, source_target_pairs={{0,1},{1,0},{2,3},{3,2},{4,5},{5,4},{6,7},{7,6},{8,9},{9,8},{10,11... | collective-permute-start | bytes 4718600 | tf_op jit(solution)/shard_map/ppermute | solution.py:279
  40.0 2.8 %collective-permute-start.7 = (bf16[1024,128]{1,0:T(8,128)(2,1)S(1)}, bf16[1024,128]{1,0:T(8,128)(2,1)S(1)}, u32[]{:S(2)}, u32[]{:S(2)}) collective-permute-start(bf16[1024,128]{1,0:T(8,128)(2,1)S(1)} %slice.9), channel_id=1, source_target_pairs={{0,96},{16,112},{32,0},{48,16},{64,32},{80,48},{96,64},{112,80},{1... | collective-permute-start | bytes 786440 | tf_op jit(solution)/shard_map/ppermute | solution.py:273
  42.8 0.1 collective-permute-start.6
  42.9 5.6 %collective-permute-done.7.rest_5_ = bf16[1024,128]{1,0:T(8,128)(2,1)S(1)} collective-permute-done((bf16[1024,128]{1,0:T(8,128)(2,1)S(1)}, bf16[1024,128]{1,0:T(8,128)(2,1)S(1)}, u32[]{:S(2)}, u32[]{:S(2)}) %collective-permute-start.7) | collective-permute-done | bytes 262176 | tf_op jit(solution)/shard_map/ppermute | solution.py:273
  48.5 0.8 collective-permute-start.11
  49.3 2.4 %collective-permute-done.6.rest_4_ = bf16[1024,128]{1,0:T(8,128)(2,1)S(1)} collective-permute-done((bf16[1024,128]{1,0:T(8,128)(2,1)S(1)}, bf16[1024,128]{1,0:T(8,128)(2,1)S(1)}, u32[]{:S(2)}, u32[]{:S(2)}) %collective-permute-start.6) | collective-permute-done | bytes 262176 | tf_op jit(solution)/shard_map/ppermute | solution.py:273
  51.7 1.1 collective-permute-start.10
  52.8 0.0 collective-permute-done.11.rest_9_
  52.8 1.2 collective-permute-done.10.rest_8_
  54.0 0.0 collective-permute-done.8.rest_6_
  54.0 0.0 collective-permute-done.9.rest_7_
  54.0 0.0 copy-done.2
  54.0 25.8 %attend.1 = bf16[4096,256]{1,0:T(8,128)(2,1)S(1)} custom-call(s32[2]{0:T(128)S(1)} %pad_add_fusion.1.meta, s32[32,24]{1,0:T(8,128)S(1)} %bitcast.8, s32[32]{0:T(128)S(1)} %reshape.230.counts, s32[128]{0:T(128)S(1)} %get-tuple-element.18.sent, s32[128]{0:T(128)S(1)} %select_reduce_fusion.3.start, bf16[2048,256]{1,0:T(8,128)(2,1)S(1)} %copy-done.2, ...), custom_call_target="tpu_custom_call" | custom-call | tf_op jit(solution)/shard_map/attend/pallas_call | solution.py:309
  79.8 37.3 %all_to_all.5 = bf16[128,32,256]{2,1,0:T(8,128)(2,1)S(1)} all-to-all(bf16[128,32,256]{2,1,0:T(8,128)(2,1)S(1)} %bitcast.7), channel_id=1, replica_groups=mesh['ctx'=8,'rows'=16] {'ctx','rows'}, dimensions={0} | all-to-all | bytes 4194304 | tf_op jit(solution)/shard_map/all_to_all | solution.py:326
  117.1 1.6 %arrange.1 = bf16[128,4096]{1,0:T(8,128)(2,1)} custom-call(bf16[8,16,32,256]{3,2,1,0:T(8,128)(2,1)S(1)} %bitcast.6), custom_call_target="tpu_custom_call" | custom-call | tf_op jit(solution)/shard_map/arrange/pallas_call | solution.py:330
  (10 shorter events, 0.1 us)
Async XLA Ops:
  0.1 2.2 %copy-start = (bf16[2048,1024]{1,0:T(8,128)(2,1)S(1)}, bf16[2048,1024]{1,0:T(8,128)(2,1)}, u32[]{:S(2)}) copy-start(bf16[2048,1024]{1,0:T(8,128)(2,1)} %keys.1) | copy-start | bytes 12582916
  2.3 2.2 %copy-start.1 = (bf16[2048,1024]{1,0:T(8,128)(2,1)S(1)}, bf16[2048,1024]{1,0:T(8,128)(2,1)}, u32[]{:S(2)}) copy-start(bf16[2048,1024]{1,0:T(8,128)(2,1)} %values.1) | copy-start | bytes 12582916
  4.5 6.1 %copy-start.3 = (s32[2048]{0:T(1024)S(1)}, s32[2048]{0:T(1024)}, u32[]{:S(2)}) copy-start(s32[2048]{0:T(1024)} %param.11) | copy-start | bytes 24580
  4.5 7.5 %copy-start.4 = (s32[2,16]{1,0:T(2,128)S(1)}, s32[2,16]{1,0:T(2,128)}, u32[]{:S(2)}) copy-start(s32[2,16]{1,0:T(2,128)} %param.10) | copy-start | bytes 388
  4.5 7.6 %copy-start.5 = (s32[2,8]{1,0:T(2,128)S(1)}, s32[2,8]{1,0:T(2,128)}, u32[]{:S(2)}) copy-start(s32[2,8]{1,0:T(2,128)} %param.9) | copy-start | bytes 196
  5.5 21.4 %collective-permute-start.2 = (bf16[2048,128]{1,0:T(8,128)(2,1)S(1)}, bf16[2048,128]{1,0:T(8,128)(2,1)S(1)}, u32[]{:S(2)}, u32[]{:S(2)}) collective-permute-start(bf16[2048,128]{1,0:T(8,128)(2,1)S(1)} %get-tuple-element.15), channel_id=1, source_target_pairs={{0,96},{16,112},{32,0},{48,16},{64,32},{80,48},{96,64},{112,80},{1... | collective-permute-start | bytes 1572872 | tf_op jit(solution)/shard_map/ppermute | solution.py:273
  8.9 12.8 %collective-permute-start.1 = (bf16[2048,128]{1,0:T(8,128)(2,1)S(1)}, bf16[2048,128]{1,0:T(8,128)(2,1)S(1)}, u32[]{:S(2)}, u32[]{:S(2)}) collective-permute-start(bf16[2048,128]{1,0:T(8,128)(2,1)S(1)} %get-tuple-element.15), channel_id=1, source_target_pairs={{0,16},{16,0},{32,48},{48,32},{64,80},{80,64},{96,112},{112,96},{1... | collective-permute-start | bytes 1572872 | tf_op jit(solution)/shard_map/ppermute | solution.py:276
  10.5 13.4 %collective-permute-start = (bf16[2048,128]{1,0:T(8,128)(2,1)S(1)}, bf16[2048,128]{1,0:T(8,128)(2,1)S(1)}, u32[]{:S(2)}, u32[]{:S(2)}) collective-permute-start(bf16[2048,128]{1,0:T(8,128)(2,1)S(1)} %get-tuple-element.15), channel_id=1, source_target_pairs={{0,32},{16,48},{32,64},{48,80},{64,96},{80,112},{96,0},{112,16},{1... | collective-permute-start | bytes 1572872 | tf_op jit(solution)/shard_map/ppermute | solution.py:273
  23.9 12.7 %collective-permute-start.5 = (bf16[2048,128]{1,0:T(8,128)(2,1)S(1)}, bf16[2048,128]{1,0:T(8,128)(2,1)S(1)}, u32[]{:S(2)}, u32[]{:S(2)}) collective-permute-start(bf16[2048,128]{1,0:T(8,128)(2,1)S(1)} %collective-permute-done), channel_id=1, source_target_pairs={{0,16},{16,0},{32,48},{48,32},{64,80},{80,64},{96,112},{112,96},{1... | collective-permute-start | bytes 1572872 | tf_op jit(solution)/shard_map/ppermute | solution.py:276
  24.1 12.4 %collective-permute-start.3 = (bf16[2048,128]{1,0:T(8,128)(2,1)S(1)}, bf16[2048,128]{1,0:T(8,128)(2,1)S(1)}, u32[]{:S(2)}, u32[]{:S(2)}) collective-permute-start(bf16[2048,128]{1,0:T(8,128)(2,1)S(1)} %collective-permute-done), channel_id=1, source_target_pairs={{0,32},{16,48},{32,64},{48,80},{64,96},{80,112},{96,0},{112,16},{1... | collective-permute-start | bytes 1572872 | tf_op jit(solution)/shard_map/ppermute | solution.py:273
  24.2 12.4 %collective-permute-start.4 = (bf16[2048,128]{1,0:T(8,128)(2,1)S(1)}, bf16[2048,128]{1,0:T(8,128)(2,1)S(1)}, u32[]{:S(2)}, u32[]{:S(2)}) collective-permute-start(bf16[2048,128]{1,0:T(8,128)(2,1)S(1)} %collective-permute-done.1), channel_id=1, source_target_pairs={{0,96},{16,112},{32,0},{48,16},{64,32},{80,48},{96,64},{112,80},{1... | collective-permute-start | bytes 1572872 | tf_op jit(solution)/shard_map/ppermute | solution.py:273
  27.1 26.9 %collective-permute-start.8 = (bf16[6144,128]{1,0:T(8,128)(2,1)S(1)}, bf16[6144,128]{1,0:T(8,128)(2,1)S(1)}, u32[]{:S(2)}, u32[]{:S(2)}) collective-permute-start(bf16[6144,128]{1,0:T(8,128)(2,1)S(1)} %constant_dynamic-update-slice_fusion.rest_2_), channel_id=1, source_target_pairs={{0,1},{1,0},{2,3},{3,2},{4,5},{5,4},{6,7},{7,6},{8,9},{9,8},{10,11... | collective-permute-start | bytes 4718600 | tf_op jit(solution)/shard_map/ppermute | solution.py:279
  36.5 17.5 %copy-start.2 = (bf16[2048,256]{1,0:T(8,128)(2,1)S(1)}, bf16[2048,256]{1,0:T(8,128)(2,1)}, u32[]{:S(2)}) copy-start(bf16[2048,256]{1,0:T(8,128)(2,1)} %q_ref.1) | copy-start | bytes 3145732
  36.7 17.3 %collective-permute-start.9 = (bf16[6144,128]{1,0:T(8,128)(2,1)S(1)}, bf16[6144,128]{1,0:T(8,128)(2,1)S(1)}, u32[]{:S(2)}, u32[]{:S(2)}) collective-permute-start(bf16[6144,128]{1,0:T(8,128)(2,1)S(1)} %constant_dynamic-update-slice_fusion.3.rest_3_), channel_id=1, source_target_pairs={{0,1},{1,0},{2,3},{3,2},{4,5},{5,4},{6,7},{7,6},{8,9},{9,8},{10,11... | collective-permute-start | bytes 4718600 | tf_op jit(solution)/shard_map/ppermute | solution.py:279
  40.0 8.5 %collective-permute-start.7 = (bf16[1024,128]{1,0:T(8,128)(2,1)S(1)}, bf16[1024,128]{1,0:T(8,128)(2,1)S(1)}, u32[]{:S(2)}, u32[]{:S(2)}) collective-permute-start(bf16[1024,128]{1,0:T(8,128)(2,1)S(1)} %slice.9), channel_id=1, source_target_pairs={{0,96},{16,112},{32,0},{48,16},{64,32},{80,48},{96,64},{112,80},{1... | collective-permute-start | bytes 786440 | tf_op jit(solution)/shard_map/ppermute | solution.py:273
  42.8 8.9 %collective-permute-start.6 = (bf16[1024,128]{1,0:T(8,128)(2,1)S(1)}, bf16[1024,128]{1,0:T(8,128)(2,1)S(1)}, u32[]{:S(2)}, u32[]{:S(2)}) collective-permute-start(bf16[1024,128]{1,0:T(8,128)(2,1)S(1)} %slice.8), channel_id=1, source_target_pairs={{0,32},{16,48},{32,64},{48,80},{64,96},{80,112},{96,0},{112,16},{1... | collective-permute-start | bytes 786440 | tf_op jit(solution)/shard_map/ppermute | solution.py:273
  48.5 4.3 %collective-permute-start.11 = (bf16[1024,128]{1,0:T(8,128)(2,1)S(1)}, bf16[1024,128]{1,0:T(8,128)(2,1)S(1)}, u32[]{:S(2)}, u32[]{:S(2)}) collective-permute-start(bf16[1024,128]{1,0:T(8,128)(2,1)S(1)} %collective-permute-done.7.rest_5_), channel_id=1, source_target_pairs={{0,1},{1,0},{2,3},{3,2},{4,5},{5,4},{6,7},{7,6},{8,9},{9,8},{10,11... | collective-permute-start | bytes 786440 | tf_op jit(solution)/shard_map/ppermute | solution.py:279
  51.7 2.3 %collective-permute-start.10 = (bf16[1024,128]{1,0:T(8,128)(2,1)S(1)}, bf16[1024,128]{1,0:T(8,128)(2,1)S(1)}, u32[]{:S(2)}, u32[]{:S(2)}) collective-permute-start(bf16[1024,128]{1,0:T(8,128)(2,1)S(1)} %collective-permute-done.6.rest_4_), channel_id=1, source_target_pairs={{0,1},{1,0},{2,3},{3,2},{4,5},{5,4},{6,7},{7,6},{8,9},{9,8},{10,11... | collective-permute-start | bytes 786440 | tf_op jit(solution)/shard_map/ppermute | solution.py:279

commit v5 on v4

--- a/solution.py
+++ b/solution.py
@@ -19,6 +19,7 @@
 SLOT = 32
 PIECE = {(0, 0): 0, (3, 0): 1, (1, 0): 2, (0, 1): 3, (2, 0): 4, (1, 1): 5, (3, 1): 6, (2, 1): 7}
 ANY = pl.BlockSpec(memory_space=pl.ANY)
+HBM = pl.BlockSpec(memory_space=pltpu.HBM)
 SMEM = pl.BlockSpec(memory_space=pltpu.SMEM)
 VMEM = pl.BlockSpec(memory_space=pltpu.VMEM)
 
@@ -95,8 +96,8 @@
     def place(slot):
         return slice((slot + 1) * BLOCK, (slot + 2) * BLOCK)
 
-    def fold(op, reduced, parts):
-        return functools.reduce(op, [reduced(p.reshape(-1, 8, BLOCK), axis=0) for p in parts])
+    def fold(reduced, block):
+        return reduced(block.reshape(-1, 8, BLOCK), axis=0)
 
     def score(qb, h, turn, group, peaks):
         row = h * nblk + qb
@@ -109,23 +110,24 @@
         else:
             keys_block = jnp.concatenate([block_of(k_s, lists[row, u]) for u in group], axis=0)
             scores = dot_t(keys_block, query)
-            parts = [
-                jnp.where(u < counts[row], scores[i * BLOCK : (i + 1) * BLOCK], NEG) for i, u in enumerate(group)
-            ]
+            parts = [scores[i * BLOCK : (i + 1) * BLOCK] for i in range(len(group))]
         for u, one in zip(group, parts):
             score_s[turn][h][place(u), :] = one
-        peaks[h] = fold(jnp.maximum, jnp.max, parts + ([peaks[h]] if h in peaks else []))
+            peak = jnp.where(u < counts[row], fold(jnp.max, one), NEG)
+            peaks[h] = jnp.maximum(peaks[h], peak) if h in peaks else peak
         if group == chunks[-1]:
             peak_s[turn][h][...] = peaks[h]
 
     def mix(qb, h, turn, group, state):
         high, total, mixed = state
         row = h * nblk + qb
-        weights = [jnp.exp2((score_s[turn][h][place(u), :] - high) * SCALE2) for u in group]
+        tops = [jnp.where(u < counts[row], high, -NEG) for u in group]
+        weights = [jnp.exp2((score_s[turn][h][place(u), :] - top) * SCALE2) for u, top in zip(group, tops)]
         low = jnp.concatenate([w.astype(jnp.bfloat16) for w in weights], axis=0)
         values_block = jnp.concatenate([block_of(v_s, qb if u < 0 else lists[row, u]) for u in group], axis=1)
         fresh = jnp.dot(values_block, low, preferred_element_type=jnp.float32)
-        total = fold(jnp.add, jnp.sum, weights + ([] if total is None else [total]))
+        for w in weights:
+            total = fold(jnp.sum, w) if total is None else total + fold(jnp.sum, w)
         return high, total, fresh if mixed is None else mixed + fresh
 
     def phase(qb, turn, ahead):
@@ -262,7 +264,7 @@
     own, *here = pl.pallas_call(
         own_kernel,
         out_shape=[jax.ShapeDtypeStruct((rows_here, DH), jnp.bfloat16)] * 3,
-        in_specs=[SMEM, ANY, ANY],
+        in_specs=[SMEM, HBM, HBM],
         out_specs=[VMEM] * 3,
         scratch_shapes=[pltpu.VMEM((rows_here, DH), jnp.bfloat16), pltpu.SemaphoreType.DMA((2,))],
         compiler_params=pltpu.CompilerParams(vmem_limit_bytes=24 * 1024 * 1024),
@@ -280,8 +282,8 @@
 
     half = rows_here // 2
     p1 = along_x(own, 1)
+    p3 = along_z(own)
     p2 = along_x(own, -1)
-    p3 = along_z(own)
 
     lists, counts = block_lists(verticals, slashes, place, nblk, cycle)
     owner = destination // own_rows
@@ -294,14 +296,14 @@
     small = (lists, counts, sent, start, rank.reshape(1, rows_here))
     p1, p3, small = lax.optimization_barrier((p1, p3, small))
 
+    p6a, p5b = along_z(p1[:half]), along_x(p3[half:], -1)
     p4 = along_x(p1, 1)
-    p5 = along_x(p3, -1)
-    p6 = along_z(p1)
+    p6b, p5a = along_z(p1[half:]), along_x(p3[:half], -1)
     mine = [jnp.concatenate([p1, p2, p3], axis=0)]
     other = [swap(mine[0])]
-    p7 = along_x(p6[:half], 1)
-    p8 = along_x(p5[half:], -1)
-    mine += [jnp.concatenate([p4, p5, p6], axis=0), p7, p8]
+    p7 = along_x(p6a, 1)
+    p8 = along_x(p5b, -1)
+    mine += [jnp.concatenate([p4, p5a, p5b, p6a, p6b], axis=0), p7, p8]
     other += [swap(x) for x in mine[1:]]
 
     lists, counts, sent, start, rank = small

time: 119 us -> 117 us (0.983)
  Pallas kernels: 28.5 us -> 26.5 us
  starting transfers between devices: 18.9 us -> 17.6 us
    pallas_call x1, Pallas kernels: 25.8 us -> 23.9 us  [body(): pl.pallas_call(functools.partial(attend_kernel, [x.shape[0] for x in mine...]
    ppermute x4, starting transfers between devices: 8.09 us -> 6.74 us  [swap(): return lax.ppermute(x, 'rows', [(r, r ^ 1) for r in range(groups)])]
    ppermute x2 -> x3, starting transfers between devices: 1.82 us -> 3.1 us  [along_z(): return lax.ppermute(x, 'ctx', [(c, c ^ 1) for c in range(cycle)])]
    ppermute x6 -> x7, starting transfers between devices: 8.99 us -> 7.74 us  [along_x(): lax.ppermute(x, 'ctx', [(c, (c + 2 * step) % cycle) for c in range(cycle)])]
    ppermute x6 -> x7, waiting for transfers between devices: 16.7 us -> 17.8 us  [along_x(): lax.ppermute(x, 'ctx', [(c, (c + 2 * step) % cycle) for c in range(cycle)])]
    unnamed x16 -> x18, local copies, waits for them, and re-layouts: 4.6 us -> 4.64 us
    ppermute x2 -> x3, waiting for transfers between devices: 6.8 us -> 6.8 us  [along_z(): return lax.ppermute(x, 'ctx', [(c, c ^ 1) for c in range(cycle)])]
  transfers between devices with their start and end apart: 12 -> 14, of which waited for: 6 -> 6; matrix products, arithmetic and copies ran while one was open for 4% -> 4% of each run, Pallas kernels for 0% -> 0%
where the time goes in v5:
time: 117 us
  blocking collectives  37.6 us (32%)
  Pallas kernels  26.5 us (23%)
  waiting for transfers between devices  25.7 us (22%)
  starting transfers between devices  17.6 us (15%)
  local copies, waits for them, and re-layouts  4.9 us (4%)
  other arithmetic  4.3 us (4%)
    all_to_all x1, blocking collectives, body(): lax.all_to_all(outgoing.reshape(devices, SLOT, heads * DH), ('ctx', 'rows...  37.6 us
    pallas_call x1, Pallas kernels, body(): pl.pallas_call(functools.partial(attend_kernel, [x.shape[0] for x in mine...  23.9 us
    ppermute x7, waiting for transfers between devices, along_x(): lax.ppermute(x, 'ctx', [(c, (c + 2 * step) % cycle) for c in range(cycle)])  17.8 us
    ppermute x7, starting transfers between devices, along_x(): lax.ppermute(x, 'ctx', [(c, (c + 2 * step) % cycle) for c in range(cycle)])  7.74 us
    ppermute x3, waiting for transfers between devices, along_z(): return lax.ppermute(x, 'ctx', [(c, c ^ 1) for c in range(cycle)])  6.8 us
    ppermute x4, starting transfers between devices, swap(): return lax.ppermute(x, 'rows', [(r, r ^ 1) for r in range(groups)])  6.74 us
    unnamed x18, local copies, waits for them, and re-layouts  4.64 us
    ppermute x3, starting transfers between devices, along_z(): return lax.ppermute(x, 'ctx', [(c, c ^ 1) for c in range(cycle)])  3.1 us
  transfers between devices with their start and end apart: 14, of which 6 were waited for; matrix products, arithmetic and copies ran while one was open for 4% of the time, Pallas kernels for 0%

profile of v5, /device:TPU:1, one launch (start us, length us, event | category | flops | bytes accessed | tf_op | source)
XLA Modules:
  0.0 116.9 jit_solution(12235104979012562577)
XLA Ops:
  0.0 0.1 pad_add_fusion.1.meta
  0.1 0.0 copy-start
  0.1 2.2 %copy-done = bf16[2048,1024]{1,0:T(8,128)(2,1)S(1)} copy-done((bf16[2048,1024]{1,0:T(8,128)(2,1)S(1)}, bf16[2048,1024]{1,0:T(8,128)(2,1)}, u32[]{:S(2)}) %copy-start) | copy-done | bytes 4194328
  2.3 0.0 copy-start.1
  2.3 2.2 %copy-done.1 = bf16[2048,1024]{1,0:T(8,128)(2,1)S(1)} copy-done((bf16[2048,1024]{1,0:T(8,128)(2,1)S(1)}, bf16[2048,1024]{1,0:T(8,128)(2,1)}, u32[]{:S(2)}) %copy-start.1) | copy-done | bytes 4194328
  4.5 0.0 copy-start.3
  4.5 0.0 copy-start.4
  4.5 0.0 copy-start.5
  4.5 1.1 own.1
  5.5 3.4 %collective-permute-start.2 = (bf16[2048,128]{1,0:T(8,128)(2,1)S(1)}, bf16[2048,128]{1,0:T(8,128)(2,1)S(1)}, u32[]{:S(2)}, u32[]{:S(2)}) collective-permute-start(bf16[2048,128]{1,0:T(8,128)(2,1)S(1)} %get-tuple-element.15), channel_id=1, source_target_pairs={{0,96},{16,112},{32,0},{48,16},{64,32},{80,48},{96,64},{112,80},{1... | collective-permute-start | bytes 1572872 | tf_op jit(solution)/shard_map/ppermute | solution.py:275
  8.9 1.6 %collective-permute-start.1 = (bf16[2048,128]{1,0:T(8,128)(2,1)S(1)}, bf16[2048,128]{1,0:T(8,128)(2,1)S(1)}, u32[]{:S(2)}, u32[]{:S(2)}) collective-permute-start(bf16[2048,128]{1,0:T(8,128)(2,1)S(1)} %get-tuple-element.15), channel_id=1, source_target_pairs={{0,16},{16,0},{32,48},{48,32},{64,80},{80,64},{96,112},{112,96},{1... | collective-permute-start | bytes 1572872 | tf_op jit(solution)/shard_map/ppermute | solution.py:278
  10.5 0.0 collective-permute-start
  10.6 0.0 copy-done.3
  10.6 1.2 %select_reduce_fusion.1 = (s32[128]{0:T(128)S(1)}, s32[128]{0:T(128)S(1)}) fusion(s32[2048]{0:T(1024)S(1)} %copy-done.3, s32[2048]{0:T(1024)S(1)} %add_select_fusion.5), kind=kLoop, calls=%fused_computation.1 | loop fusion | flops 1310464 | bytes 17408 | tf_op jit(solution)/shard_map/reduce_min | solution.py:291
  11.8 0.1 select_reduce_fusion.3.start
  11.9 0.6 select_reduce_fusion
  12.6 0.0 copy-done.4
  12.6 0.1 broadcast_subtract_fusion
  12.6 0.0 copy-done.5
  12.6 0.1 pad_add_fusion
  12.7 0.8 and_reduce_fusion
  13.5 0.2 convert_reduce_fusion.2
  13.8 0.1 reshape.230.counts
  13.8 0.6 convert_reduce_fusion.1
  14.5 0.5 select_reduce_fusion.2
  15.0 6.8 %collective-permute-done.1 = bf16[2048,128]{1,0:T(8,128)(2,1)S(1)} collective-permute-done((bf16[2048,128]{1,0:T(8,128)(2,1)S(1)}, bf16[2048,128]{1,0:T(8,128)(2,1)S(1)}, u32[]{:S(2)}, u32[]{:S(2)}) %collective-permute-start.1) | collective-permute-done | bytes 524320 | tf_op jit(solution)/shard_map/ppermute | solution.py:278
  21.8 2.2 %collective-permute-done = bf16[2048,128]{1,0:T(8,128)(2,1)S(1)} collective-permute-done((bf16[2048,128]{1,0:T(8,128)(2,1)S(1)}, bf16[2048,128]{1,0:T(8,128)(2,1)S(1)}, u32[]{:S(2)}, u32[]{:S(2)}) %collective-permute-start) | collective-permute-done | bytes 524320 | tf_op jit(solution)/shard_map/ppermute | solution.py:275
  24.0 0.1 collective-permute-start.3
  24.1 2.7 %collective-permute-start.5 = (bf16[1024,128]{1,0:T(8,128)(2,1)S(1)}, bf16[1024,128]{1,0:T(8,128)(2,1)S(1)}, u32[]{:S(2)}, u32[]{:S(2)}) collective-permute-start(bf16[1024,128]{1,0:T(8,128)(2,1)S(1)} %get-tuple-element.31), channel_id=1, source_target_pairs={{0,96},{16,112},{32,0},{48,16},{64,32},{80,48},{96,64},{112,80},{1... | collective-permute-start | bytes 786440 | tf_op jit(solution)/shard_map/ppermute | solution.py:275
  26.9 0.1 collective-permute-start.4
  27.0 0.2 collective-permute-start.7
  27.1 0.0 collective-permute-done.2
  27.1 1.3 %collective-permute-start.6 = (bf16[1024,128]{1,0:T(8,128)(2,1)S(1)}, bf16[1024,128]{1,0:T(8,128)(2,1)S(1)}, u32[]{:S(2)}, u32[]{:S(2)}) collective-permute-start(bf16[1024,128]{1,0:T(8,128)(2,1)S(1)} %get-tuple-element.30), channel_id=1, source_target_pairs={{0,16},{16,0},{32,48},{48,32},{64,80},{80,64},{96,112},{112,96},{1... | collective-permute-start | bytes 786440 | tf_op jit(solution)/shard_map/ppermute | solution.py:278
  28.4 0.1 constant_dynamic-update-slice_fusion.1
  28.5 0.1 constant_dynamic-update-slice_fusion.rest_2_
  28.6 0.0 copy-start.2
  28.6 7.9 %collective-permute-done.3 = bf16[2048,128]{1,0:T(8,128)(2,1)S(1)} collective-permute-done((bf16[2048,128]{1,0:T(8,128)(2,1)S(1)}, bf16[2048,128]{1,0:T(8,128)(2,1)S(1)}, u32[]{:S(2)}, u32[]{:S(2)}) %collective-permute-start.3) | collective-permute-done | bytes 524320 | tf_op jit(solution)/shard_map/ppermute | solution.py:275
  36.5 3.1 %collective-permute-start.10 = (bf16[6144,128]{1,0:T(8,128)(2,1)S(1)}, bf16[6144,128]{1,0:T(8,128)(2,1)S(1)}, u32[]{:S(2)}, u32[]{:S(2)}) collective-permute-start(bf16[6144,128]{1,0:T(8,128)(2,1)S(1)} %constant_dynamic-update-slice_fusion.rest_2_), channel_id=1, source_target_pairs={{0,1},{1,0},{2,3},{3,2},{4,5},{5,4},{6,7},{7,6},{8,9},{9,8},{10,11... | collective-permute-start | bytes 4718600 | tf_op jit(solution)/shard_map/ppermute | solution.py:281
  39.6 0.0 collective-permute-done.4
  39.7 0.0 collective-permute-done.5
  39.7 0.0 collective-permute-done.6
  39.8 0.0 collective-permute-done.7
  39.9 1.6 %collective-permute-start.11 = (bf16[6144,128]{1,0:T(8,128)(2,1)S(1)}, bf16[6144,128]{1,0:T(8,128)(2,1)S(1)}, u32[]{:S(2)}, u32[]{:S(2)}) collective-permute-start(bf16[6144,128]{1,0:T(8,128)(2,1)S(1)} %constant_dynamic-update-slice_fusion.3.rest_3_), channel_id=1, source_target_pairs={{0,1},{1,0},{2,3},{3,2},{4,5},{5,4},{6,7},{7,6},{8,9},{9,8},{10,11... | collective-permute-start | bytes 4718600 | tf_op jit(solution)/shard_map/ppermute | solution.py:281
  41.5 1.3 %collective-permute-start.9 = (bf16[1024,128]{1,0:T(8,128)(2,1)S(1)}, bf16[1024,128]{1,0:T(8,128)(2,1)S(1)}, u32[]{:S(2)}, u32[]{:S(2)}) collective-permute-start(bf16[1024,128]{1,0:T(8,128)(2,1)S(1)} %collective-permute-done.5), channel_id=1, source_target_pairs={{0,96},{16,112},{32,0},{48,16},{64,32},{80,48},{96,64},{112,80},{1... | collective-permute-start | bytes 786440 | tf_op jit(solution)/shard_map/ppermute | solution.py:275
  42.7 0.2 collective-permute-start.8
  42.9 6.4 %collective-permute-done.9.rest_5_ = bf16[1024,128]{1,0:T(8,128)(2,1)S(1)} collective-permute-done((bf16[1024,128]{1,0:T(8,128)(2,1)S(1)}, bf16[1024,128]{1,0:T(8,128)(2,1)S(1)}, u32[]{:S(2)}, u32[]{:S(2)}) %collective-permute-start.9) | collective-permute-done | bytes 262176 | tf_op jit(solution)/shard_map/ppermute | solution.py:275
  49.3 0.9 collective-permute-start.13
  50.2 1.3 %collective-permute-done.8.rest_4_ = bf16[1024,128]{1,0:T(8,128)(2,1)S(1)} collective-permute-done((bf16[1024,128]{1,0:T(8,128)(2,1)S(1)}, bf16[1024,128]{1,0:T(8,128)(2,1)S(1)}, u32[]{:S(2)}, u32[]{:S(2)}) %collective-permute-start.8) | collective-permute-done | bytes 262176 | tf_op jit(solution)/shard_map/ppermute | solution.py:275
  51.5 1.2 %collective-permute-start.12 = (bf16[1024,128]{1,0:T(8,128)(2,1)S(1)}, bf16[1024,128]{1,0:T(8,128)(2,1)S(1)}, u32[]{:S(2)}, u32[]{:S(2)}) collective-permute-start(bf16[1024,128]{1,0:T(8,128)(2,1)S(1)} %collective-permute-done.8.rest_4_), channel_id=1, source_target_pairs={{0,1},{1,0},{2,3},{3,2},{4,5},{5,4},{6,7},{7,6},{8,9},{9,8},{10,11... | collective-permute-start | bytes 786440 | tf_op jit(solution)/shard_map/ppermute | solution.py:281
  52.7 0.0 collective-permute-done.13.rest_9_
  52.7 1.2 collective-permute-done.12.rest_8_
  53.8 0.0 collective-permute-done.10.rest_6_
  53.8 0.0 collective-permute-done.11.rest_7_
  53.8 0.0 copy-done.2
  53.8 23.9 %attend.1 = bf16[4096,256]{1,0:T(8,128)(2,1)S(1)} custom-call(s32[2]{0:T(128)S(1)} %pad_add_fusion.1.meta, s32[32,24]{1,0:T(8,128)S(1)} %bitcast.8, s32[32]{0:T(128)S(1)} %reshape.230.counts, s32[128]{0:T(128)S(1)} %get-tuple-element.18.sent, s32[128]{0:T(128)S(1)} %select_reduce_fusion.3.start, bf16[2048,256]{1,0:T(8,128)(2,1)S(1)} %copy-done.2, ...), custom_call_target="tpu_custom_call" | custom-call | tf_op jit(solution)/shard_map/attend/pallas_call | solution.py:311
  77.7 37.6 %all_to_all.5 = bf16[128,32,256]{2,1,0:T(8,128)(2,1)S(1)} all-to-all(bf16[128,32,256]{2,1,0:T(8,128)(2,1)S(1)} %bitcast.7), channel_id=1, replica_groups=mesh['ctx'=8,'rows'=16] {'ctx','rows'}, dimensions={0} | all-to-all | bytes 4194304 | tf_op jit(solution)/shard_map/all_to_all | solution.py:328
  115.3 1.6 %arrange.1 = bf16[128,4096]{1,0:T(8,128)(2,1)} custom-call(bf16[8,16,32,256]{3,2,1,0:T(8,128)(2,1)S(1)} %bitcast.6), custom_call_target="tpu_custom_call" | custom-call | tf_op jit(solution)/shard_map/arrange/pallas_call | solution.py:332
  (14 shorter events, 0.3 us)
Async XLA Ops:
  0.1 2.2 %copy-start = (bf16[2048,1024]{1,0:T(8,128)(2,1)S(1)}, bf16[2048,1024]{1,0:T(8,128)(2,1)}, u32[]{:S(2)}) copy-start(bf16[2048,1024]{1,0:T(8,128)(2,1)} %keys.1) | copy-start | bytes 12582916
  2.3 2.2 %copy-start.1 = (bf16[2048,1024]{1,0:T(8,128)(2,1)S(1)}, bf16[2048,1024]{1,0:T(8,128)(2,1)}, u32[]{:S(2)}) copy-start(bf16[2048,1024]{1,0:T(8,128)(2,1)} %values.1) | copy-start | bytes 12582916
  4.5 6.1 %copy-start.3 = (s32[2048]{0:T(1024)S(1)}, s32[2048]{0:T(1024)}, u32[]{:S(2)}) copy-start(s32[2048]{0:T(1024)} %param.11) | copy-start | bytes 24580
  4.5 8.1 %copy-start.4 = (s32[2,16]{1,0:T(2,128)S(1)}, s32[2,16]{1,0:T(2,128)}, u32[]{:S(2)}) copy-start(s32[2,16]{1,0:T(2,128)} %param.10) | copy-start | bytes 388
  4.5 8.2 %copy-start.5 = (s32[2,8]{1,0:T(2,128)S(1)}, s32[2,8]{1,0:T(2,128)}, u32[]{:S(2)}) copy-start(s32[2,8]{1,0:T(2,128)} %param.9) | copy-start | bytes 196
  5.5 21.6 %collective-permute-start.2 = (bf16[2048,128]{1,0:T(8,128)(2,1)S(1)}, bf16[2048,128]{1,0:T(8,128)(2,1)S(1)}, u32[]{:S(2)}, u32[]{:S(2)}) collective-permute-start(bf16[2048,128]{1,0:T(8,128)(2,1)S(1)} %get-tuple-element.15), channel_id=1, source_target_pairs={{0,96},{16,112},{32,0},{48,16},{64,32},{80,48},{96,64},{112,80},{1... | collective-permute-start | bytes 1572872 | tf_op jit(solution)/shard_map/ppermute | solution.py:275
  8.9 12.8 %collective-permute-start.1 = (bf16[2048,128]{1,0:T(8,128)(2,1)S(1)}, bf16[2048,128]{1,0:T(8,128)(2,1)S(1)}, u32[]{:S(2)}, u32[]{:S(2)}) collective-permute-start(bf16[2048,128]{1,0:T(8,128)(2,1)S(1)} %get-tuple-element.15), channel_id=1, source_target_pairs={{0,16},{16,0},{32,48},{48,32},{64,80},{80,64},{96,112},{112,96},{1... | collective-permute-start | bytes 1572872 | tf_op jit(solution)/shard_map/ppermute | solution.py:278
  10.5 13.4 %collective-permute-start = (bf16[2048,128]{1,0:T(8,128)(2,1)S(1)}, bf16[2048,128]{1,0:T(8,128)(2,1)S(1)}, u32[]{:S(2)}, u32[]{:S(2)}) collective-permute-start(bf16[2048,128]{1,0:T(8,128)(2,1)S(1)} %get-tuple-element.15), channel_id=1, source_target_pairs={{0,32},{16,48},{32,64},{48,80},{64,96},{80,112},{96,0},{112,16},{1... | collective-permute-start | bytes 1572872 | tf_op jit(solution)/shard_map/ppermute | solution.py:275
  24.0 12.5 %collective-permute-start.3 = (bf16[2048,128]{1,0:T(8,128)(2,1)S(1)}, bf16[2048,128]{1,0:T(8,128)(2,1)S(1)}, u32[]{:S(2)}, u32[]{:S(2)}) collective-permute-start(bf16[2048,128]{1,0:T(8,128)(2,1)S(1)} %collective-permute-done), channel_id=1, source_target_pairs={{0,32},{16,48},{32,64},{48,80},{64,96},{80,112},{96,0},{112,16},{1... | collective-permute-start | bytes 1572872 | tf_op jit(solution)/shard_map/ppermute | solution.py:275
  24.1 15.5 %collective-permute-start.5 = (bf16[1024,128]{1,0:T(8,128)(2,1)S(1)}, bf16[1024,128]{1,0:T(8,128)(2,1)S(1)}, u32[]{:S(2)}, u32[]{:S(2)}) collective-permute-start(bf16[1024,128]{1,0:T(8,128)(2,1)S(1)} %get-tuple-element.31), channel_id=1, source_target_pairs={{0,96},{16,112},{32,0},{48,16},{64,32},{80,48},{96,64},{112,80},{1... | collective-permute-start | bytes 786440 | tf_op jit(solution)/shard_map/ppermute | solution.py:275
  26.9 12.8 %collective-permute-start.4 = (bf16[1024,128]{1,0:T(8,128)(2,1)S(1)}, bf16[1024,128]{1,0:T(8,128)(2,1)S(1)}, u32[]{:S(2)}, u32[]{:S(2)}) collective-permute-start(bf16[1024,128]{1,0:T(8,128)(2,1)S(1)} %get-tuple-element.32), channel_id=1, source_target_pairs={{0,96},{16,112},{32,0},{48,16},{64,32},{80,48},{96,64},{112,80},{1... | collective-permute-start | bytes 786440 | tf_op jit(solution)/shard_map/ppermute | solution.py:275
  27.0 12.8 %collective-permute-start.7 = (bf16[1024,128]{1,0:T(8,128)(2,1)S(1)}, bf16[1024,128]{1,0:T(8,128)(2,1)S(1)}, u32[]{:S(2)}, u32[]{:S(2)}) collective-permute-start(bf16[1024,128]{1,0:T(8,128)(2,1)S(1)} %get-tuple-element.29), channel_id=1, source_target_pairs={{0,16},{16,0},{32,48},{48,32},{64,80},{80,64},{96,112},{112,96},{1... | collective-permute-start | bytes 786440 | tf_op jit(solution)/shard_map/ppermute | solution.py:278
  27.1 12.6 %collective-permute-start.6 = (bf16[1024,128]{1,0:T(8,128)(2,1)S(1)}, bf16[1024,128]{1,0:T(8,128)(2,1)S(1)}, u32[]{:S(2)}, u32[]{:S(2)}) collective-permute-start(bf16[1024,128]{1,0:T(8,128)(2,1)S(1)} %get-tuple-element.30), channel_id=1, source_target_pairs={{0,16},{16,0},{32,48},{48,32},{64,80},{80,64},{96,112},{112,96},{1... | collective-permute-start | bytes 786440 | tf_op jit(solution)/shard_map/ppermute | solution.py:278
  28.6 25.2 %copy-start.2 = (bf16[2048,256]{1,0:T(8,128)(2,1)S(1)}, bf16[2048,256]{1,0:T(8,128)(2,1)}, u32[]{:S(2)}) copy-start(bf16[2048,256]{1,0:T(8,128)(2,1)} %q_ref.1) | copy-start | bytes 3145732
  36.5 17.3 %collective-permute-start.10 = (bf16[6144,128]{1,0:T(8,128)(2,1)S(1)}, bf16[6144,128]{1,0:T(8,128)(2,1)S(1)}, u32[]{:S(2)}, u32[]{:S(2)}) collective-permute-start(bf16[6144,128]{1,0:T(8,128)(2,1)S(1)} %constant_dynamic-update-slice_fusion.rest_2_), channel_id=1, source_target_pairs={{0,1},{1,0},{2,3},{3,2},{4,5},{5,4},{6,7},{7,6},{8,9},{9,8},{10,11... | collective-permute-start | bytes 4718600 | tf_op jit(solution)/shard_map/ppermute | solution.py:281
  39.9 14.0 %collective-permute-start.11 = (bf16[6144,128]{1,0:T(8,128)(2,1)S(1)}, bf16[6144,128]{1,0:T(8,128)(2,1)S(1)}, u32[]{:S(2)}, u32[]{:S(2)}) collective-permute-start(bf16[6144,128]{1,0:T(8,128)(2,1)S(1)} %constant_dynamic-update-slice_fusion.3.rest_3_), channel_id=1, source_target_pairs={{0,1},{1,0},{2,3},{3,2},{4,5},{5,4},{6,7},{7,6},{8,9},{9,8},{10,11... | collective-permute-start | bytes 4718600 | tf_op jit(solution)/shard_map/ppermute | solution.py:281
  41.5 7.9 %collective-permute-start.9 = (bf16[1024,128]{1,0:T(8,128)(2,1)S(1)}, bf16[1024,128]{1,0:T(8,128)(2,1)S(1)}, u32[]{:S(2)}, u32[]{:S(2)}) collective-permute-start(bf16[1024,128]{1,0:T(8,128)(2,1)S(1)} %collective-permute-done.5), channel_id=1, source_target_pairs={{0,96},{16,112},{32,0},{48,16},{64,32},{80,48},{96,64},{112,80},{1... | collective-permute-start | bytes 786440 | tf_op jit(solution)/shard_map/ppermute | solution.py:275
  42.7 8.8 %collective-permute-start.8 = (bf16[1024,128]{1,0:T(8,128)(2,1)S(1)}, bf16[1024,128]{1,0:T(8,128)(2,1)S(1)}, u32[]{:S(2)}, u32[]{:S(2)}) collective-permute-start(bf16[1024,128]{1,0:T(8,128)(2,1)S(1)} %collective-permute-done.6), channel_id=1, source_target_pairs={{0,32},{16,48},{32,64},{48,80},{64,96},{80,112},{96,0},{112,16},{1... | collective-permute-start | bytes 786440 | tf_op jit(solution)/shard_map/ppermute | solution.py:275
  49.3 3.3 %collective-permute-start.13 = (bf16[1024,128]{1,0:T(8,128)(2,1)S(1)}, bf16[1024,128]{1,0:T(8,128)(2,1)S(1)}, u32[]{:S(2)}, u32[]{:S(2)}) collective-permute-start(bf16[1024,128]{1,0:T(8,128)(2,1)S(1)} %collective-permute-done.9.rest_5_), channel_id=1, source_target_pairs={{0,1},{1,0},{2,3},{3,2},{4,5},{5,4},{6,7},{7,6},{8,9},{9,8},{10,11... | collective-permute-start | bytes 786440 | tf_op jit(solution)/shard_map/ppermute | solution.py:281
  51.5 2.3 %collective-permute-start.12 = (bf16[1024,128]{1,0:T(8,128)(2,1)S(1)}, bf16[1024,128]{1,0:T(8,128)(2,1)S(1)}, u32[]{:S(2)}, u32[]{:S(2)}) collective-permute-start(bf16[1024,128]{1,0:T(8,128)(2,1)S(1)} %collective-permute-done.8.rest_4_), channel_id=1, source_target_pairs={{0,1},{1,0},{2,3},{3,2},{4,5},{5,4},{6,7},{7,6},{8,9},{9,8},{10,11... | collective-permute-start | bytes 786440 | tf_op jit(solution)/shard_map/ppermute | solution.py:281

commit v6 on v5

--- a/solution.py
+++ b/solution.py
@@ -19,7 +19,6 @@
 SLOT = 32
 PIECE = {(0, 0): 0, (3, 0): 1, (1, 0): 2, (0, 1): 3, (2, 0): 4, (1, 1): 5, (3, 1): 6, (2, 1): 7}
 ANY = pl.BlockSpec(memory_space=pl.ANY)
-HBM = pl.BlockSpec(memory_space=pltpu.HBM)
 SMEM = pl.BlockSpec(memory_space=pltpu.SMEM)
 VMEM = pl.BlockSpec(memory_space=pltpu.VMEM)
 
@@ -264,10 +263,10 @@
     own, *here = pl.pallas_call(
         own_kernel,
         out_shape=[jax.ShapeDtypeStruct((rows_here, DH), jnp.bfloat16)] * 3,
-        in_specs=[SMEM, HBM, HBM],
+        in_specs=[SMEM, ANY, ANY],
         out_specs=[VMEM] * 3,
         scratch_shapes=[pltpu.VMEM((rows_here, DH), jnp.bfloat16), pltpu.SemaphoreType.DMA((2,))],
-        compiler_params=pltpu.CompilerParams(vmem_limit_bytes=24 * 1024 * 1024),
+        compiler_params=pltpu.CompilerParams(vmem_limit_bytes=60 * 1024 * 1024),
         name="own",
     )(meta, keys, values)
 
@@ -281,11 +280,6 @@
         return lax.ppermute(x, "rows", [(r, r ^ 1) for r in range(groups)])
 
     half = rows_here // 2
-    p1 = along_x(own, 1)
-    p3 = along_z(own)
-    p2 = along_x(own, -1)
-
-    lists, counts = block_lists(verticals, slashes, place, nblk, cycle)
     owner = destination // own_rows
     member = owner[:, None] == jnp.arange(devices, dtype=jnp.int32)[None, :]
     first_row = jnp.min(jnp.where(member, destination[:, None], ROW_CEILING), axis=0)
@@ -293,17 +287,22 @@
     numbers = jnp.arange(devices, dtype=jnp.int32)
     start = jnp.sum(jnp.where(numbers[:, None] < numbers[None, :], sent[:, None], 0), axis=0)
     rank = destination + jnp.sum(jnp.where(member, (start - first_row)[None, :], 0), axis=1)
+    p1 = along_x(own, 1)
+    p3 = along_z(own)
+    own, sent = lax.optimization_barrier((own, sent))
+    p2 = along_x(own, -1)
+    lists, counts = block_lists(verticals, slashes, place, nblk, cycle)
     small = (lists, counts, sent, start, rank.reshape(1, rows_here))
     p1, p3, small = lax.optimization_barrier((p1, p3, small))
 
-    p6a, p5b = along_z(p1[:half]), along_x(p3[half:], -1)
     p4 = along_x(p1, 1)
-    p6b, p5a = along_z(p1[half:]), along_x(p3[:half], -1)
+    p5 = along_x(p3, -1)
+    p6 = along_z(p1)
     mine = [jnp.concatenate([p1, p2, p3], axis=0)]
     other = [swap(mine[0])]
-    p7 = along_x(p6a, 1)
-    p8 = along_x(p5b, -1)
-    mine += [jnp.concatenate([p4, p5a, p5b, p6a, p6b], axis=0), p7, p8]
+    p7 = along_x(p6[:half], 1)
+    p8 = along_x(p5[half:], -1)
+    mine += [jnp.concatenate([p4, p5, p6], axis=0), p7, p8]
     other += [swap(x) for x in mine[1:]]
 
     lists, counts, sent, start, rank = small

time: 117 us -> 113 us (0.966)
  local copies, waits for them, and re-layouts: 4.9 us -> 0.5 us
  waiting for transfers between devices: 25.7 us -> 23.3 us
  Pallas kernels: 26.5 us -> 28.7 us
    unnamed x18, local copies, waits for them, and re-layouts: 4.64 us -> 0.24 us
    pallas_call x1, Pallas kernels: 1.07 us -> 3.24 us  [body(): pl.pallas_call(own_kernel, out_shape=[jax.ShapeDtypeStruct((rows_here, DH...]
    ppermute x3 -> x2, waiting for transfers between devices: 6.8 us -> 4.71 us  [along_z(): return lax.ppermute(x, 'ctx', [(c, c ^ 1) for c in range(cycle)])]
    ppermute x7 -> x6, starting transfers between devices: 7.74 us -> 8.32 us  [along_x(): lax.ppermute(x, 'ctx', [(c, (c + 2 * step) % cycle) for c in range(cycle)])]
    ppermute x7 -> x6, waiting for transfers between devices: 17.8 us -> 17.5 us  [along_x(): lax.ppermute(x, 'ctx', [(c, (c + 2 * step) % cycle) for c in range(cycle)])]
    ppermute x3 -> x2, starting transfers between devices: 3.1 us -> 2.95 us  [along_z(): return lax.ppermute(x, 'ctx', [(c, c ^ 1) for c in range(cycle)])]
  transfers between devices with their start and end apart: 14 -> 12, of which waited for: 6 -> 6; matrix products, arithmetic and copies ran while one was open for 4% -> 4% of each run, Pallas kernels for 0% -> 0%
where the time goes in v6:
time: 113 us
  blocking collectives  37.1 us (33%)
  Pallas kernels  28.7 us (25%)
  waiting for transfers between devices  23.3 us (21%)
  starting transfers between devices  18.5 us (16%)
  other arithmetic  4.88 us (4%)
    all_to_all x1, blocking collectives, body(): lax.all_to_all(outgoing.reshape(devices, SLOT, heads * DH), ('ctx', 'rows...  37.1 us
    pallas_call x1, Pallas kernels, body(): pl.pallas_call(functools.partial(attend_kernel, [x.shape[0] for x in mine...  23.9 us
    ppermute x6, waiting for transfers between devices, along_x(): lax.ppermute(x, 'ctx', [(c, (c + 2 * step) % cycle) for c in range(cycle)])  17.5 us
    ppermute x6, starting transfers between devices, along_x(): lax.ppermute(x, 'ctx', [(c, (c + 2 * step) % cycle) for c in range(cycle)])  8.32 us
    ppermute x4, starting transfers between devices, swap(): return lax.ppermute(x, 'rows', [(r, r ^ 1) for r in range(groups)])  7.21 us
    ppermute x2, waiting for transfers between devices, along_z(): return lax.ppermute(x, 'ctx', [(c, c ^ 1) for c in range(cycle)])  4.71 us
    pallas_call x1, Pallas kernels, body(): pl.pallas_call(own_kernel, out_shape=[jax.ShapeDtypeStruct((rows_here, DH...  3.24 us
    ppermute x2, starting transfers between devices, along_z(): return lax.ppermute(x, 'ctx', [(c, c ^ 1) for c in range(cycle)])  2.95 us
  transfers between devices with their start and end apart: 12, of which 6 were waited for; matrix products, arithmetic and copies ran while one was open for 4% of the time, Pallas kernels for 0%

profile of v6, /device:TPU:1, one launch (start us, length us, event | category | flops | bytes accessed | tf_op | source)
XLA Modules:
  0.0 113.2 jit_solution(5667905193675695844)
XLA Ops:
  0.0 0.7 pad_add_fusion.1.meta
  0.7 0.0 copy-start.4
  0.7 0.0 copy-start.5
  0.7 0.0 copy-start.6
  0.7 3.2 %own.1 = (bf16[2048,128]{1,0:T(8,128)(2,1)}, bf16[2048,128]{1,0:T(8,128)(2,1)}, bf16[2048,128]{1,0:T(8,128)(2,1)}) custom-call(s32[2]{0:T(128)} %pad_add_fusion.1.meta, bf16[2048,1024]{1,0:T(8,128)(2,1)} %keys.1, bf16[2048,1024]{1,0:T(8,128)(2,1)} %values.1), custom_call_target="tpu_custom_call" | custom-call | tf_op jit(solution)/shard_map/own/pallas_call | solution.py:263
  3.9 2.5 %collective-permute-start.1 = (bf16[2048,128]{1,0:T(8,128)(2,1)}, bf16[2048,128]{1,0:T(8,128)(2,1)S(1)}, u32[]{:S(2)}, u32[]{:S(2)}) collective-permute-start(bf16[2048,128]{1,0:T(8,128)(2,1)} %get-tuple-element.27), channel_id=1, source_target_pairs={{0,16},{16,0},{32,48},{48,32},{64,80},{80,64},{96,112},{112,96},{1... | collective-permute-start | bytes 1572872 | tf_op jit(solution)/shard_map/ppermute | solution.py:277
  6.5 1.2 %collective-permute-start = (bf16[2048,128]{1,0:T(8,128)(2,1)}, bf16[2048,128]{1,0:T(8,128)(2,1)S(1)}, u32[]{:S(2)}, u32[]{:S(2)}) collective-permute-start(bf16[2048,128]{1,0:T(8,128)(2,1)} %get-tuple-element.27), channel_id=1, source_target_pairs={{0,32},{16,48},{32,64},{48,80},{64,96},{80,112},{96,0},{112,16},{1... | collective-permute-start | bytes 1572872 | tf_op jit(solution)/shard_map/ppermute | solution.py:274
  7.7 0.0 copy-done.4
  7.7 1.2 %select_reduce_fusion.1 = (s32[128]{0:T(128)S(1)}, s32[128]{0:T(128)S(1)}) fusion(s32[2048]{0:T(1024)S(1)} %copy-done.4, s32[2048]{0:T(1024)S(1)} %add_select_fusion.5), kind=kLoop, calls=%fused_computation.1 | loop fusion | flops 1310464 | bytes 17408 | tf_op jit(solution)/shard_map/reduce_min | solution.py:285
  8.9 1.5 %collective-permute-start.2 = (bf16[2048,128]{1,0:T(8,128)(2,1)}, bf16[2048,128]{1,0:T(8,128)(2,1)S(1)}, u32[]{:S(2)}, u32[]{:S(2)}) collective-permute-start(bf16[2048,128]{1,0:T(8,128)(2,1)} %get-tuple-element.27), channel_id=1, source_target_pairs={{0,96},{16,112},{32,0},{48,16},{64,32},{80,48},{96,64},{112,80},{1... | collective-permute-start | bytes 1572872 | tf_op jit(solution)/shard_map/ppermute | solution.py:274
  10.4 0.1 select_reduce_fusion.3.start
  10.6 0.0 copy-done.5
  10.6 0.1 broadcast_subtract_fusion
  10.7 0.0 copy-done.6
  10.7 0.1 pad_add_fusion
  10.7 0.8 and_reduce_fusion
  11.5 0.2 convert_reduce_fusion.2
  11.8 0.6 select_reduce_fusion
  12.4 0.1 reshape.230.counts
  12.5 0.6 convert_reduce_fusion.1
  13.1 0.5 select_reduce_fusion.2
  13.6 4.7 %collective-permute-done.1 = bf16[2048,128]{1,0:T(8,128)(2,1)S(1)} collective-permute-done((bf16[2048,128]{1,0:T(8,128)(2,1)}, bf16[2048,128]{1,0:T(8,128)(2,1)S(1)}, u32[]{:S(2)}, u32[]{:S(2)}) %collective-permute-start.1) | collective-permute-done | bytes 524320 | tf_op jit(solution)/shard_map/ppermute | solution.py:277
  18.3 2.1 %collective-permute-done = bf16[2048,128]{1,0:T(8,128)(2,1)S(1)} collective-permute-done((bf16[2048,128]{1,0:T(8,128)(2,1)}, bf16[2048,128]{1,0:T(8,128)(2,1)S(1)}, u32[]{:S(2)}, u32[]{:S(2)}) %collective-permute-start) | collective-permute-done | bytes 524320 | tf_op jit(solution)/shard_map/ppermute | solution.py:274
  20.4 0.4 collective-permute-start.5
  20.8 0.0 collective-permute-start.3
  20.8 2.7 %collective-permute-start.4 = (bf16[2048,128]{1,0:T(8,128)(2,1)S(1)}, bf16[2048,128]{1,0:T(8,128)(2,1)S(1)}, u32[]{:S(2)}, u32[]{:S(2)}) collective-permute-start(bf16[2048,128]{1,0:T(8,128)(2,1)S(1)} %collective-permute-done.1), channel_id=1, source_target_pairs={{0,96},{16,112},{32,0},{48,16},{64,32},{80,48},{96,64},{112,80},{1... | collective-permute-start | bytes 1572872 | tf_op jit(solution)/shard_map/ppermute | solution.py:274
  23.5 0.0 collective-permute-done.2
  23.5 0.1 constant_dynamic-update-slice_fusion.1
  23.6 0.1 constant_dynamic-update-slice_fusion.rest_2_
  23.7 2.5 %collective-permute-start.8 = (bf16[6144,128]{1,0:T(8,128)(2,1)S(1)}, bf16[6144,128]{1,0:T(8,128)(2,1)S(1)}, u32[]{:S(2)}, u32[]{:S(2)}) collective-permute-start(bf16[6144,128]{1,0:T(8,128)(2,1)S(1)} %constant_dynamic-update-slice_fusion.rest_2_), channel_id=1, source_target_pairs={{0,1},{1,0},{2,3},{3,2},{4,5},{5,4},{6,7},{7,6},{8,9},{9,8},{10,11... | collective-permute-start | bytes 4718600 | tf_op jit(solution)/shard_map/ppermute | solution.py:280
  26.2 7.4 %collective-permute-done.3 = bf16[2048,128]{1,0:T(8,128)(2,1)S(1)} collective-permute-done((bf16[2048,128]{1,0:T(8,128)(2,1)S(1)}, bf16[2048,128]{1,0:T(8,128)(2,1)S(1)}, u32[]{:S(2)}, u32[]{:S(2)}) %collective-permute-start.3) | collective-permute-done | bytes 524320 | tf_op jit(solution)/shard_map/ppermute | solution.py:274
  33.6 0.0 copy-start
  33.6 0.0 copy-start.1
  33.6 0.0 copy-start.2
  33.6 0.0 copy-start.3
  33.6 0.0 collective-permute-done.4
  33.7 0.1 constant_dynamic-update-slice_fusion.4
  33.7 0.0 collective-permute-done.5
  33.7 0.1 constant_dynamic-update-slice_fusion.3.rest_3_
  33.8 2.8 %collective-permute-start.9 = (bf16[6144,128]{1,0:T(8,128)(2,1)S(1)}, bf16[6144,128]{1,0:T(8,128)(2,1)S(1)}, u32[]{:S(2)}, u32[]{:S(2)}) collective-permute-start(bf16[6144,128]{1,0:T(8,128)(2,1)S(1)} %constant_dynamic-update-slice_fusion.3.rest_3_), channel_id=1, source_target_pairs={{0,1},{1,0},{2,3},{3,2},{4,5},{5,4},{6,7},{7,6},{8,9},{9,8},{10,11... | collective-permute-start | bytes 4718600 | tf_op jit(solution)/shard_map/ppermute | solution.py:280
  36.7 2.8 %collective-permute-start.7 = (bf16[1024,128]{1,0:T(8,128)(2,1)S(1)}, bf16[1024,128]{1,0:T(8,128)(2,1)S(1)}, u32[]{:S(2)}, u32[]{:S(2)}) collective-permute-start(bf16[1024,128]{1,0:T(8,128)(2,1)S(1)} %slice.9), channel_id=1, source_target_pairs={{0,96},{16,112},{32,0},{48,16},{64,32},{80,48},{96,64},{112,80},{1... | collective-permute-start | bytes 786440 | tf_op jit(solution)/shard_map/ppermute | solution.py:274
  39.4 0.1 collective-permute-start.6
  39.5 5.6 %collective-permute-done.7.rest_5_ = bf16[1024,128]{1,0:T(8,128)(2,1)S(1)} collective-permute-done((bf16[1024,128]{1,0:T(8,128)(2,1)S(1)}, bf16[1024,128]{1,0:T(8,128)(2,1)S(1)}, u32[]{:S(2)}, u32[]{:S(2)}) %collective-permute-start.7) | collective-permute-done | bytes 262176 | tf_op jit(solution)/shard_map/ppermute | solution.py:274
  45.1 0.8 collective-permute-start.11
  45.9 2.4 %collective-permute-done.6.rest_4_ = bf16[1024,128]{1,0:T(8,128)(2,1)S(1)} collective-permute-done((bf16[1024,128]{1,0:T(8,128)(2,1)S(1)}, bf16[1024,128]{1,0:T(8,128)(2,1)S(1)}, u32[]{:S(2)}, u32[]{:S(2)}) %collective-permute-start.6) | collective-permute-done | bytes 262176 | tf_op jit(solution)/shard_map/ppermute | solution.py:274
  48.3 1.1 collective-permute-start.10
  49.4 0.0 collective-permute-done.11.rest_9_
  49.5 1.2 %collective-permute-done.10.rest_8_ = bf16[1024,128]{1,0:T(8,128)(2,1)S(1)} collective-permute-done((bf16[1024,128]{1,0:T(8,128)(2,1)S(1)}, bf16[1024,128]{1,0:T(8,128)(2,1)S(1)}, u32[]{:S(2)}, u32[]{:S(2)}) %collective-permute-start.10) | collective-permute-done | bytes 262176 | tf_op jit(solution)/shard_map/ppermute | solution.py:280
  50.6 0.0 collective-permute-done.8.rest_6_
  50.6 0.0 collective-permute-done.9.rest_7_
  50.6 0.0 copy-done
  50.6 0.0 copy-done.1
  50.6 0.0 copy-done.2
  50.6 0.0 copy-done.3
  50.7 23.9 %attend.1 = bf16[4096,256]{1,0:T(8,128)(2,1)S(1)} custom-call(s32[2]{0:T(128)S(1)} %copy-done.3, s32[32,24]{1,0:T(8,128)S(1)} %bitcast.8, s32[32]{0:T(128)S(1)} %reshape.230.counts, s32[128]{0:T(128)S(1)} %get-tuple-element.21.sent, s32[128]{0:T(128)S(1)} %select_reduce_fusion.3.start, bf16[2048,256]{1,0:T(8,128)(2,1)S(1)} %copy-done, ...), custom_call_target="tpu_custom_call" | custom-call | tf_op jit(solution)/shard_map/attend/pallas_call | solution.py:310
  74.5 37.1 %all_to_all.5 = bf16[128,32,256]{2,1,0:T(8,128)(2,1)S(1)} all-to-all(bf16[128,32,256]{2,1,0:T(8,128)(2,1)S(1)} %bitcast.7), channel_id=1, replica_groups=mesh['ctx'=8,'rows'=16] {'ctx','rows'}, dimensions={0} | all-to-all | bytes 4194304 | tf_op jit(solution)/shard_map/all_to_all | solution.py:327
  111.6 1.6 %arrange.1 = bf16[128,4096]{1,0:T(8,128)(2,1)} custom-call(bf16[8,16,32,256]{3,2,1,0:T(8,128)(2,1)S(1)} %bitcast.6), custom_call_target="tpu_custom_call" | custom-call | tf_op jit(solution)/shard_map/arrange/pallas_call | solution.py:331
  (10 shorter events, 0.1 us)
Async XLA Ops:
  0.7 7.0 %copy-start.4 = (s32[2048]{0:T(1024)S(1)}, s32[2048]{0:T(1024)}, u32[]{:S(2)}) copy-start(s32[2048]{0:T(1024)} %param.11) | copy-start | bytes 24580
  0.7 9.9 %copy-start.5 = (s32[2,16]{1,0:T(2,128)S(1)}, s32[2,16]{1,0:T(2,128)}, u32[]{:S(2)}) copy-start(s32[2,16]{1,0:T(2,128)} %param.10) | copy-start | bytes 388
  0.7 10.0 %copy-start.6 = (s32[2,8]{1,0:T(2,128)S(1)}, s32[2,8]{1,0:T(2,128)}, u32[]{:S(2)}) copy-start(s32[2,8]{1,0:T(2,128)} %param.9) | copy-start | bytes 196
  3.9 14.4 %collective-permute-start.1 = (bf16[2048,128]{1,0:T(8,128)(2,1)}, bf16[2048,128]{1,0:T(8,128)(2,1)S(1)}, u32[]{:S(2)}, u32[]{:S(2)}) collective-permute-start(bf16[2048,128]{1,0:T(8,128)(2,1)} %get-tuple-element.27), channel_id=1, source_target_pairs={{0,16},{16,0},{32,48},{48,32},{64,80},{80,64},{96,112},{112,96},{1... | collective-permute-start | bytes 1572872 | tf_op jit(solution)/shard_map/ppermute | solution.py:277
  6.5 13.9 %collective-permute-start = (bf16[2048,128]{1,0:T(8,128)(2,1)}, bf16[2048,128]{1,0:T(8,128)(2,1)S(1)}, u32[]{:S(2)}, u32[]{:S(2)}) collective-permute-start(bf16[2048,128]{1,0:T(8,128)(2,1)} %get-tuple-element.27), channel_id=1, source_target_pairs={{0,32},{16,48},{32,64},{48,80},{64,96},{80,112},{96,0},{112,16},{1... | collective-permute-start | bytes 1572872 | tf_op jit(solution)/shard_map/ppermute | solution.py:274
  8.9 14.6 %collective-permute-start.2 = (bf16[2048,128]{1,0:T(8,128)(2,1)}, bf16[2048,128]{1,0:T(8,128)(2,1)S(1)}, u32[]{:S(2)}, u32[]{:S(2)}) collective-permute-start(bf16[2048,128]{1,0:T(8,128)(2,1)} %get-tuple-element.27), channel_id=1, source_target_pairs={{0,96},{16,112},{32,0},{48,16},{64,32},{80,48},{96,64},{112,80},{1... | collective-permute-start | bytes 1572872 | tf_op jit(solution)/shard_map/ppermute | solution.py:274
  20.4 13.4 %collective-permute-start.5 = (bf16[2048,128]{1,0:T(8,128)(2,1)S(1)}, bf16[2048,128]{1,0:T(8,128)(2,1)S(1)}, u32[]{:S(2)}, u32[]{:S(2)}) collective-permute-start(bf16[2048,128]{1,0:T(8,128)(2,1)S(1)} %collective-permute-done), channel_id=1, source_target_pairs={{0,16},{16,0},{32,48},{48,32},{64,80},{80,64},{96,112},{112,96},{1... | collective-permute-start | bytes 1572872 | tf_op jit(solution)/shard_map/ppermute | solution.py:277
  20.8 12.8 %collective-permute-start.3 = (bf16[2048,128]{1,0:T(8,128)(2,1)S(1)}, bf16[2048,128]{1,0:T(8,128)(2,1)S(1)}, u32[]{:S(2)}, u32[]{:S(2)}) collective-permute-start(bf16[2048,128]{1,0:T(8,128)(2,1)S(1)} %collective-permute-done), channel_id=1, source_target_pairs={{0,32},{16,48},{32,64},{48,80},{64,96},{80,112},{96,0},{112,16},{1... | collective-permute-start | bytes 1572872 | tf_op jit(solution)/shard_map/ppermute | solution.py:274
  20.8 12.8 %collective-permute-start.4 = (bf16[2048,128]{1,0:T(8,128)(2,1)S(1)}, bf16[2048,128]{1,0:T(8,128)(2,1)S(1)}, u32[]{:S(2)}, u32[]{:S(2)}) collective-permute-start(bf16[2048,128]{1,0:T(8,128)(2,1)S(1)} %collective-permute-done.1), channel_id=1, source_target_pairs={{0,96},{16,112},{32,0},{48,16},{64,32},{80,48},{96,64},{112,80},{1... | collective-permute-start | bytes 1572872 | tf_op jit(solution)/shard_map/ppermute | solution.py:274
  23.7 26.9 %collective-permute-start.8 = (bf16[6144,128]{1,0:T(8,128)(2,1)S(1)}, bf16[6144,128]{1,0:T(8,128)(2,1)S(1)}, u32[]{:S(2)}, u32[]{:S(2)}) collective-permute-start(bf16[6144,128]{1,0:T(8,128)(2,1)S(1)} %constant_dynamic-update-slice_fusion.rest_2_), channel_id=1, source_target_pairs={{0,1},{1,0},{2,3},{3,2},{4,5},{5,4},{6,7},{7,6},{8,9},{9,8},{10,11... | collective-permute-start | bytes 4718600 | tf_op jit(solution)/shard_map/ppermute | solution.py:280
  33.6 17.0 %copy-start = (bf16[2048,256]{1,0:T(8,128)(2,1)S(1)}, bf16[2048,256]{1,0:T(8,128)(2,1)}, u32[]{:S(2)}) copy-start(bf16[2048,256]{1,0:T(8,128)(2,1)} %q_ref.1) | copy-start | bytes 3145732
  33.6 17.0 %copy-start.1 = (bf16[2048,128]{1,0:T(8,128)(2,1)S(1)}, bf16[2048,128]{1,0:T(8,128)(2,1)}, u32[]{:S(2)}) copy-start(bf16[2048,128]{1,0:T(8,128)(2,1)} %get-tuple-element.24.rest_0_) | copy-start | bytes 1572868
  33.6 17.0 %copy-start.2 = (bf16[2048,128]{1,0:T(8,128)(2,1)S(1)}, bf16[2048,128]{1,0:T(8,128)(2,1)}, u32[]{:S(2)}) copy-start(bf16[2048,128]{1,0:T(8,128)(2,1)} %get-tuple-element.25.rest_1_) | copy-start | bytes 1572868
  33.6 17.0 %copy-start.3 = (s32[2]{0:T(128)S(1)}, s32[2]{0:T(128)}, u32[]{:S(2)}) copy-start(s32[2]{0:T(128)} %pad_add_fusion.1.meta) | copy-start | bytes 28
  33.8 16.8 %collective-permute-start.9 = (bf16[6144,128]{1,0:T(8,128)(2,1)S(1)}, bf16[6144,128]{1,0:T(8,128)(2,1)S(1)}, u32[]{:S(2)}, u32[]{:S(2)}) collective-permute-start(bf16[6144,128]{1,0:T(8,128)(2,1)S(1)} %constant_dynamic-update-slice_fusion.3.rest_3_), channel_id=1, source_target_pairs={{0,1},{1,0},{2,3},{3,2},{4,5},{5,4},{6,7},{7,6},{8,9},{9,8},{10,11... | collective-permute-start | bytes 4718600 | tf_op jit(solution)/shard_map/ppermute | solution.py:280
  36.7 8.5 %collective-permute-start.7 = (bf16[1024,128]{1,0:T(8,128)(2,1)S(1)}, bf16[1024,128]{1,0:T(8,128)(2,1)S(1)}, u32[]{:S(2)}, u32[]{:S(2)}) collective-permute-start(bf16[1024,128]{1,0:T(8,128)(2,1)S(1)} %slice.9), channel_id=1, source_target_pairs={{0,96},{16,112},{32,0},{48,16},{64,32},{80,48},{96,64},{112,80},{1... | collective-permute-start | bytes 786440 | tf_op jit(solution)/shard_map/ppermute | solution.py:274
  39.4 8.9 %collective-permute-start.6 = (bf16[1024,128]{1,0:T(8,128)(2,1)S(1)}, bf16[1024,128]{1,0:T(8,128)(2,1)S(1)}, u32[]{:S(2)}, u32[]{:S(2)}) collective-permute-start(bf16[1024,128]{1,0:T(8,128)(2,1)S(1)} %slice.8), channel_id=1, source_target_pairs={{0,32},{16,48},{32,64},{48,80},{64,96},{80,112},{96,0},{112,16},{1... | collective-permute-start | bytes 786440 | tf_op jit(solution)/shard_map/ppermute | solution.py:274
  45.1 4.3 %collective-permute-start.11 = (bf16[1024,128]{1,0:T(8,128)(2,1)S(1)}, bf16[1024,128]{1,0:T(8,128)(2,1)S(1)}, u32[]{:S(2)}, u32[]{:S(2)}) collective-permute-start(bf16[1024,128]{1,0:T(8,128)(2,1)S(1)} %collective-permute-done.7.rest_5_), channel_id=1, source_target_pairs={{0,1},{1,0},{2,3},{3,2},{4,5},{5,4},{6,7},{7,6},{8,9},{9,8},{10,11... | collective-permute-start | bytes 786440 | tf_op jit(solution)/shard_map/ppermute | solution.py:280
  48.3 2.3 %collective-permute-start.10 = (bf16[1024,128]{1,0:T(8,128)(2,1)S(1)}, bf16[1024,128]{1,0:T(8,128)(2,1)S(1)}, u32[]{:S(2)}, u32[]{:S(2)}) collective-permute-start(bf16[1024,128]{1,0:T(8,128)(2,1)S(1)} %collective-permute-done.6.rest_4_), channel_id=1, source_target_pairs={{0,1},{1,0},{2,3},{3,2},{4,5},{5,4},{6,7},{7,6},{8,9},{9,8},{10,11... | collective-permute-start | bytes 786440 | tf_op jit(solution)/shard_map/ppermute | solution.py:280

commit v7 on v6

--- a/solution.py
+++ b/solution.py
@@ -27,25 +27,37 @@
     return lax.dot_general(a, b, (((1,), (1,)), ((), ())), preferred_element_type=jnp.float32)
 
 
-def own_kernel(meta, keys, values, own_ref, keys_ref, values_ref, value_s, sem):
+def sent_kernel(meta, keys, values, sent_ref, value_s, sem):
     column = pl.ds(pl.multiple_of(meta[1] * DH, DH), DH)
-    value_copy = pltpu.make_async_copy(values.at[:, column], value_s, sem.at[0])
-    key_copy = pltpu.make_async_copy(keys.at[:, column], keys_ref, sem.at[1])
-    value_copy.start()
-    key_copy.start()
-    value_copy.wait()
+
+    @pl.when(meta[0] == 0)
+    def _():
+        pltpu.make_async_copy(keys.at[:, column], value_s, sem.at[0]).start()
+
+    @pl.when(meta[0] != 0)
+    def _():
+        pltpu.make_async_copy(values.at[:, column], value_s, sem.at[0]).start()
+
+    pltpu.make_async_copy(keys.at[:, column], value_s, sem.at[0]).wait()
+    for start in range(0, value_s.shape[0], BLOCK):
+        rows = slice(start, start + BLOCK)
+        block = value_s[rows, :]
+        sent_ref[rows, :] = jnp.where(meta[0] == 0, block, block.T)
+
+
+def own_kernel(meta, keys, values, keys_ref, values_ref, value_s, sem):
+    column = pl.ds(pl.multiple_of(meta[1] * DH, DH), DH)
+    copies = [
+        pltpu.make_async_copy(values.at[:, column], value_s, sem.at[0]),
+        pltpu.make_async_copy(keys.at[:, column], keys_ref, sem.at[1]),
+    ]
+    for copy in copies:
+        copy.start()
+    for copy in copies:
+        copy.wait()
     for start in range(0, value_s.shape[0], BLOCK):
         rows = slice(start, start + BLOCK)
         values_ref[rows, :] = value_s[rows, :].T
-    key_copy.wait()
-
-    @pl.when(meta[0] == 0)
-    def _():
-        own_ref[...] = keys_ref[...]
-
-    @pl.when(meta[0] != 0)
-    def _():
-        own_ref[...] = values_ref[...]
 
 
 def attend_kernel(sizes, slots, heads, meta, lists, counts, sent, start, q_ref, rank_ref, *rest):
@@ -250,25 +262,27 @@
     cycle = lax.axis_size("ctx")
     groups = lax.axis_size("rows")
     place = lax.axis_index("ctx")
-    group = lax.axis_index("rows")
     rows_here = queries.shape[0]
     heads = verticals.shape[0]
     nblk = rows_here // BLOCK
     devices = cycle * groups
     own_rows = rows_here // groups
-    kv_index = group * heads // (HEADS // KV_HEADS)
-    core = group % 2
-
-    meta = jnp.stack([core, kv_index]).astype(jnp.int32)
-    own, *here = pl.pallas_call(
-        own_kernel,
-        out_shape=[jax.ShapeDtypeStruct((rows_here, DH), jnp.bfloat16)] * 3,
-        in_specs=[SMEM, ANY, ANY],
-        out_specs=[VMEM] * 3,
-        scratch_shapes=[pltpu.VMEM((rows_here, DH), jnp.bfloat16), pltpu.SemaphoreType.DMA((2,))],
-        compiler_params=pltpu.CompilerParams(vmem_limit_bytes=60 * 1024 * 1024),
-        name="own",
-    )(meta, keys, values)
+    group = lax.axis_index("rows")
+    meta = jnp.stack([group % 2, group * heads // (HEADS // KV_HEADS)]).astype(jnp.int32)
+    piece = jax.ShapeDtypeStruct((rows_here, DH), jnp.bfloat16)
+
+    def slices(kernel, outs, keys, values):
+        return pl.pallas_call(
+            kernel,
+            out_shape=[piece] * outs,
+            in_specs=[SMEM, ANY, ANY],
+            out_specs=[VMEM] * outs,
+            scratch_shapes=[pltpu.VMEM((rows_here, DH), jnp.bfloat16), pltpu.SemaphoreType.DMA((outs,))],
+            compiler_params=pltpu.CompilerParams(vmem_limit_bytes=60 * 1024 * 1024),
+            name="own",
+        )(meta, keys, values)
+
+    (own,) = slices(sent_kernel, 1, keys, values)
 
     def along_x(x, step):
         return lax.ppermute(x, "ctx", [(c, (c + 2 * step) % cycle) for c in range(cycle)])
@@ -289,11 +303,12 @@
     rank = destination + jnp.sum(jnp.where(member, (start - first_row)[None, :], 0), axis=1)
     p1 = along_x(own, 1)
     p3 = along_z(own)
-    own, sent = lax.optimization_barrier((own, sent))
+    own, sent, keys, values = lax.optimization_barrier((own, sent, keys, values))
     p2 = along_x(own, -1)
+    here = slices(own_kernel, 2, keys, values)
     lists, counts = block_lists(verticals, slashes, place, nblk, cycle)
     small = (lists, counts, sent, start, rank.reshape(1, rows_here))
-    p1, p3, small = lax.optimization_barrier((p1, p3, small))
+    p1, p3, small, here = lax.optimization_barrier((p1, p3, small, here))
 
     p4 = along_x(p1, 1)
     p5 = along_x(p3, -1)

time: 113 us -> 114 us (level)
  Pallas kernels: 28.7 us -> 32.4 us
  waiting for transfers between devices: 23.3 us -> 20.4 us
    ppermute x2, waiting for transfers between devices: 4.71 us -> 1.82 us  [along_z(): return lax.ppermute(x, 'ctx', [(c, c ^ 1) for c in range(cycle)])]
    pallas_call x1 -> x2, Pallas kernels: 3.24 us -> 5.73 us  [slices(): pl.pallas_call(kernel, out_shape=[piece] * outs, in_specs=[SMEM, ANY, ANY...]
    pallas_call x1, Pallas kernels: 23.9 us -> 25.1 us  [body(): pl.pallas_call(functools.partial(attend_kernel, [x.shape[0] for x in mine...]
  transfers between devices with their start and end apart: 12 -> 12, of which waited for: 6 -> 6; matrix products, arithmetic and copies ran while one was open for 4% -> 4% of each run, Pallas kernels for 0% -> 3%
where the time goes in v7:
time: 114 us
  blocking collectives  37.1 us (33%)
  Pallas kernels  32.4 us (28%)
  waiting for transfers between devices  20.4 us (18%)
  starting transfers between devices  18.5 us (16%)
  other arithmetic  4.88 us (4%)
    all_to_all x1, blocking collectives, body(): lax.all_to_all(outgoing.reshape(devices, SLOT, heads * DH), ('ctx', 'rows...  37.1 us
    pallas_call x1, Pallas kernels, body(): pl.pallas_call(functools.partial(attend_kernel, [x.shape[0] for x in mine...  25.1 us
    ppermute x6, waiting for transfers between devices, along_x(): lax.ppermute(x, 'ctx', [(c, (c + 2 * step) % cycle) for c in range(cycle)])  17.5 us
    ppermute x6, starting transfers between devices, along_x(): lax.ppermute(x, 'ctx', [(c, (c + 2 * step) % cycle) for c in range(cycle)])  8.32 us
    ppermute x4, starting transfers between devices, swap(): return lax.ppermute(x, 'rows', [(r, r ^ 1) for r in range(groups)])  7.21 us
    pallas_call x2, Pallas kernels, slices(): pl.pallas_call(kernel, out_shape=[piece] * outs, in_specs=[SMEM, ANY, ANY...  5.73 us
    ppermute x2, starting transfers between devices, along_z(): return lax.ppermute(x, 'ctx', [(c, c ^ 1) for c in range(cycle)])  2.95 us
  transfers between devices with their start and end apart: 12, of which 6 were waited for; matrix products, arithmetic and copies ran while one was open for 4% of the time, Pallas kernels for 3%

profile of v7, /device:TPU:1, one launch (start us, length us, event | category | flops | bytes accessed | tf_op | source)
XLA Modules:
  0.0 114.0 jit_solution(7005380802634893284)
XLA Ops:
  0.0 0.7 pad_add_fusion.1.meta
  0.7 0.0 copy-start.4
  0.7 0.0 copy-start.5
  0.7 0.0 copy-start.6
  0.7 2.8 %own.2 = bf16[2048,128]{1,0:T(8,128)(2,1)} custom-call(s32[2]{0:T(128)} %pad_add_fusion.1.meta, bf16[2048,1024]{1,0:T(8,128)(2,1)} %keys.2, bf16[2048,1024]{1,0:T(8,128)(2,1)} %values.2), custom_call_target="tpu_custom_call" | custom-call | tf_op jit(solution)/shard_map/own/pallas_call | solution.py:275
  3.5 2.5 %collective-permute-start.1 = (bf16[2048,128]{1,0:T(8,128)(2,1)}, bf16[2048,128]{1,0:T(8,128)(2,1)S(1)}, u32[]{:S(2)}, u32[]{:S(2)}) collective-permute-start(bf16[2048,128]{1,0:T(8,128)(2,1)} %own.2), channel_id=1, source_target_pairs={{0,16},{16,0},{32,48},{48,32},{64,80},{80,64},{96,112},{112,96},{1... | collective-permute-start | bytes 1572872 | tf_op jit(solution)/shard_map/ppermute | solution.py:291
  6.1 1.2 %collective-permute-start = (bf16[2048,128]{1,0:T(8,128)(2,1)}, bf16[2048,128]{1,0:T(8,128)(2,1)S(1)}, u32[]{:S(2)}, u32[]{:S(2)}) collective-permute-start(bf16[2048,128]{1,0:T(8,128)(2,1)} %own.2), channel_id=1, source_target_pairs={{0,32},{16,48},{32,64},{48,80},{64,96},{80,112},{96,0},{112,16},{1... | collective-permute-start | bytes 1572872 | tf_op jit(solution)/shard_map/ppermute | solution.py:288
  7.3 0.0 copy-done.4
  7.3 1.2 %select_reduce_fusion.1 = (s32[128]{0:T(128)S(1)}, s32[128]{0:T(128)S(1)}) fusion(s32[2048]{0:T(1024)S(1)} %copy-done.4, s32[2048]{0:T(1024)S(1)} %add_select_fusion.5), kind=kLoop, calls=%fused_computation.1 | loop fusion | flops 1310464 | bytes 17408 | tf_op jit(solution)/shard_map/reduce_min | solution.py:299
  8.5 1.5 %collective-permute-start.2 = (bf16[2048,128]{1,0:T(8,128)(2,1)}, bf16[2048,128]{1,0:T(8,128)(2,1)S(1)}, u32[]{:S(2)}, u32[]{:S(2)}) collective-permute-start(bf16[2048,128]{1,0:T(8,128)(2,1)} %own.2), channel_id=1, source_target_pairs={{0,96},{16,112},{32,0},{48,16},{64,32},{80,48},{96,64},{112,80},{1... | collective-permute-start | bytes 1572872 | tf_op jit(solution)/shard_map/ppermute | solution.py:288
  10.1 0.1 select_reduce_fusion.3.start
  10.2 0.0 copy-done.5
  10.2 0.1 broadcast_subtract_fusion
  10.3 0.0 copy-done.6
  10.3 0.1 pad_add_fusion
  10.4 0.8 and_reduce_fusion
  11.1 0.2 convert_reduce_fusion.2
  11.4 0.6 select_reduce_fusion
  12.0 0.1 reshape.230.counts
  12.1 2.9 %own.3 = (bf16[2048,128]{1,0:T(8,128)(2,1)}, bf16[2048,128]{1,0:T(8,128)(2,1)}) custom-call(s32[2]{0:T(128)} %pad_add_fusion.1.meta, bf16[2048,1024]{1,0:T(8,128)(2,1)} %keys.2, bf16[2048,1024]{1,0:T(8,128)(2,1)} %values.2), custom_call_target="tpu_custom_call" | custom-call | tf_op jit(solution)/shard_map/own/pallas_call | solution.py:275
  15.0 0.6 convert_reduce_fusion.1
  15.6 0.5 select_reduce_fusion.2
  16.1 1.8 %collective-permute-done.1 = bf16[2048,128]{1,0:T(8,128)(2,1)S(1)} collective-permute-done((bf16[2048,128]{1,0:T(8,128)(2,1)}, bf16[2048,128]{1,0:T(8,128)(2,1)S(1)}, u32[]{:S(2)}, u32[]{:S(2)}) %collective-permute-start.1) | collective-permute-done | bytes 524320 | tf_op jit(solution)/shard_map/ppermute | solution.py:291
  17.9 2.1 %collective-permute-done = bf16[2048,128]{1,0:T(8,128)(2,1)S(1)} collective-permute-done((bf16[2048,128]{1,0:T(8,128)(2,1)}, bf16[2048,128]{1,0:T(8,128)(2,1)S(1)}, u32[]{:S(2)}, u32[]{:S(2)}) %collective-permute-start) | collective-permute-done | bytes 524320 | tf_op jit(solution)/shard_map/ppermute | solution.py:288
  20.0 0.4 collective-permute-start.5
  20.4 0.0 collective-permute-start.3
  20.4 2.7 %collective-permute-start.4 = (bf16[2048,128]{1,0:T(8,128)(2,1)S(1)}, bf16[2048,128]{1,0:T(8,128)(2,1)S(1)}, u32[]{:S(2)}, u32[]{:S(2)}) collective-permute-start(bf16[2048,128]{1,0:T(8,128)(2,1)S(1)} %collective-permute-done.1), channel_id=1, source_target_pairs={{0,96},{16,112},{32,0},{48,16},{64,32},{80,48},{96,64},{112,80},{1... | collective-permute-start | bytes 1572872 | tf_op jit(solution)/shard_map/ppermute | solution.py:288
  23.2 0.0 collective-permute-done.2
  23.2 0.1 constant_dynamic-update-slice_fusion.1
  23.2 0.1 constant_dynamic-update-slice_fusion.rest_2_
  23.3 2.5 %collective-permute-start.8 = (bf16[6144,128]{1,0:T(8,128)(2,1)S(1)}, bf16[6144,128]{1,0:T(8,128)(2,1)S(1)}, u32[]{:S(2)}, u32[]{:S(2)}) collective-permute-start(bf16[6144,128]{1,0:T(8,128)(2,1)S(1)} %constant_dynamic-update-slice_fusion.rest_2_), channel_id=1, source_target_pairs={{0,1},{1,0},{2,3},{3,2},{4,5},{5,4},{6,7},{7,6},{8,9},{9,8},{10,11... | collective-permute-start | bytes 4718600 | tf_op jit(solution)/shard_map/ppermute | solution.py:294
  25.8 7.4 %collective-permute-done.3 = bf16[2048,128]{1,0:T(8,128)(2,1)S(1)} collective-permute-done((bf16[2048,128]{1,0:T(8,128)(2,1)S(1)}, bf16[2048,128]{1,0:T(8,128)(2,1)S(1)}, u32[]{:S(2)}, u32[]{:S(2)}) %collective-permute-start.3) | collective-permute-done | bytes 524320 | tf_op jit(solution)/shard_map/ppermute | solution.py:288
  33.2 0.0 copy-start
  33.2 0.0 copy-start.1
  33.2 0.0 copy-start.2
  33.2 0.0 copy-start.3
  33.3 0.0 collective-permute-done.4
  33.3 0.1 constant_dynamic-update-slice_fusion.4
  33.3 0.0 collective-permute-done.5
  33.4 0.1 constant_dynamic-update-slice_fusion.3.rest_3_
  33.4 2.8 %collective-permute-start.9 = (bf16[6144,128]{1,0:T(8,128)(2,1)S(1)}, bf16[6144,128]{1,0:T(8,128)(2,1)S(1)}, u32[]{:S(2)}, u32[]{:S(2)}) collective-permute-start(bf16[6144,128]{1,0:T(8,128)(2,1)S(1)} %constant_dynamic-update-slice_fusion.3.rest_3_), channel_id=1, source_target_pairs={{0,1},{1,0},{2,3},{3,2},{4,5},{5,4},{6,7},{7,6},{8,9},{9,8},{10,11... | collective-permute-start | bytes 4718600 | tf_op jit(solution)/shard_map/ppermute | solution.py:294
  36.3 2.8 %collective-permute-start.7 = (bf16[1024,128]{1,0:T(8,128)(2,1)S(1)}, bf16[1024,128]{1,0:T(8,128)(2,1)S(1)}, u32[]{:S(2)}, u32[]{:S(2)}) collective-permute-start(bf16[1024,128]{1,0:T(8,128)(2,1)S(1)} %slice.9), channel_id=1, source_target_pairs={{0,96},{16,112},{32,0},{48,16},{64,32},{80,48},{96,64},{112,80},{1... | collective-permute-start | bytes 786440 | tf_op jit(solution)/shard_map/ppermute | solution.py:288
  39.1 0.1 collective-permute-start.6
  39.1 5.6 %collective-permute-done.7.rest_5_ = bf16[1024,128]{1,0:T(8,128)(2,1)S(1)} collective-permute-done((bf16[1024,128]{1,0:T(8,128)(2,1)S(1)}, bf16[1024,128]{1,0:T(8,128)(2,1)S(1)}, u32[]{:S(2)}, u32[]{:S(2)}) %collective-permute-start.7) | collective-permute-done | bytes 262176 | tf_op jit(solution)/shard_map/ppermute | solution.py:288
  44.8 0.8 collective-permute-start.11
  45.6 2.4 %collective-permute-done.6.rest_4_ = bf16[1024,128]{1,0:T(8,128)(2,1)S(1)} collective-permute-done((bf16[1024,128]{1,0:T(8,128)(2,1)S(1)}, bf16[1024,128]{1,0:T(8,128)(2,1)S(1)}, u32[]{:S(2)}, u32[]{:S(2)}) %collective-permute-start.6) | collective-permute-done | bytes 262176 | tf_op jit(solution)/shard_map/ppermute | solution.py:288
  47.9 1.1 collective-permute-start.10
  49.1 0.0 collective-permute-done.11.rest_9_
  49.1 1.2 %collective-permute-done.10.rest_8_ = bf16[1024,128]{1,0:T(8,128)(2,1)S(1)} collective-permute-done((bf16[1024,128]{1,0:T(8,128)(2,1)S(1)}, bf16[1024,128]{1,0:T(8,128)(2,1)S(1)}, u32[]{:S(2)}, u32[]{:S(2)}) %collective-permute-start.10) | collective-permute-done | bytes 262176 | tf_op jit(solution)/shard_map/ppermute | solution.py:294
  50.2 0.0 collective-permute-done.8.rest_6_
  50.2 0.0 collective-permute-done.9.rest_7_
  50.2 0.0 copy-done
  50.2 0.0 copy-done.1
  50.2 0.0 copy-done.2
  50.2 0.0 copy-done.3
  50.3 25.1 %attend.1 = bf16[4096,256]{1,0:T(8,128)(2,1)S(1)} custom-call(s32[2]{0:T(128)S(1)} %copy-done.3, s32[32,24]{1,0:T(8,128)S(1)} %bitcast.8, s32[32]{0:T(128)S(1)} %reshape.230.counts, s32[128]{0:T(128)S(1)} %get-tuple-element.27.sent, s32[128]{0:T(128)S(1)} %select_reduce_fusion.3.start, bf16[2048,256]{1,0:T(8,128)(2,1)S(1)} %copy-done, ...), custom_call_target="tpu_custom_call" | custom-call | tf_op jit(solution)/shard_map/attend/pallas_call | solution.py:325
  75.3 37.1 %all_to_all.5 = bf16[128,32,256]{2,1,0:T(8,128)(2,1)S(1)} all-to-all(bf16[128,32,256]{2,1,0:T(8,128)(2,1)S(1)} %bitcast.7), channel_id=1, replica_groups=mesh['ctx'=8,'rows'=16] {'ctx','rows'}, dimensions={0} | all-to-all | bytes 4194304 | tf_op jit(solution)/shard_map/all_to_all | solution.py:342
  112.4 1.6 %arrange.1 = bf16[128,4096]{1,0:T(8,128)(2,1)} custom-call(bf16[8,16,32,256]{3,2,1,0:T(8,128)(2,1)S(1)} %bitcast.6), custom_call_target="tpu_custom_call" | custom-call | tf_op jit(solution)/shard_map/arrange/pallas_call | solution.py:346
  (10 shorter events, 0.1 us)
Async XLA Ops:
  0.7 6.6 %copy-start.4 = (s32[2048]{0:T(1024)S(1)}, s32[2048]{0:T(1024)}, u32[]{:S(2)}) copy-start(s32[2048]{0:T(1024)} %param.11) | copy-start | bytes 24580
  0.7 9.5 %copy-start.5 = (s32[2,16]{1,0:T(2,128)S(1)}, s32[2,16]{1,0:T(2,128)}, u32[]{:S(2)}) copy-start(s32[2,16]{1,0:T(2,128)} %param.10) | copy-start | bytes 388
  0.7 9.6 %copy-start.6 = (s32[2,8]{1,0:T(2,128)S(1)}, s32[2,8]{1,0:T(2,128)}, u32[]{:S(2)}) copy-start(s32[2,8]{1,0:T(2,128)} %param.9) | copy-start | bytes 196
  3.5 14.4 %collective-permute-start.1 = (bf16[2048,128]{1,0:T(8,128)(2,1)}, bf16[2048,128]{1,0:T(8,128)(2,1)S(1)}, u32[]{:S(2)}, u32[]{:S(2)}) collective-permute-start(bf16[2048,128]{1,0:T(8,128)(2,1)} %own.2), channel_id=1, source_target_pairs={{0,16},{16,0},{32,48},{48,32},{64,80},{80,64},{96,112},{112,96},{1... | collective-permute-start | bytes 1572872 | tf_op jit(solution)/shard_map/ppermute | solution.py:291
  6.1 13.9 %collective-permute-start = (bf16[2048,128]{1,0:T(8,128)(2,1)}, bf16[2048,128]{1,0:T(8,128)(2,1)S(1)}, u32[]{:S(2)}, u32[]{:S(2)}) collective-permute-start(bf16[2048,128]{1,0:T(8,128)(2,1)} %own.2), channel_id=1, source_target_pairs={{0,32},{16,48},{32,64},{48,80},{64,96},{80,112},{96,0},{112,16},{1... | collective-permute-start | bytes 1572872 | tf_op jit(solution)/shard_map/ppermute | solution.py:288
  8.5 14.6 %collective-permute-start.2 = (bf16[2048,128]{1,0:T(8,128)(2,1)}, bf16[2048,128]{1,0:T(8,128)(2,1)S(1)}, u32[]{:S(2)}, u32[]{:S(2)}) collective-permute-start(bf16[2048,128]{1,0:T(8,128)(2,1)} %own.2), channel_id=1, source_target_pairs={{0,96},{16,112},{32,0},{48,16},{64,32},{80,48},{96,64},{112,80},{1... | collective-permute-start | bytes 1572872 | tf_op jit(solution)/shard_map/ppermute | solution.py:288
  20.0 13.4 %collective-permute-start.5 = (bf16[2048,128]{1,0:T(8,128)(2,1)S(1)}, bf16[2048,128]{1,0:T(8,128)(2,1)S(1)}, u32[]{:S(2)}, u32[]{:S(2)}) collective-permute-start(bf16[2048,128]{1,0:T(8,128)(2,1)S(1)} %collective-permute-done), channel_id=1, source_target_pairs={{0,16},{16,0},{32,48},{48,32},{64,80},{80,64},{96,112},{112,96},{1... | collective-permute-start | bytes 1572872 | tf_op jit(solution)/shard_map/ppermute | solution.py:291
  20.4 12.8 %collective-permute-start.3 = (bf16[2048,128]{1,0:T(8,128)(2,1)S(1)}, bf16[2048,128]{1,0:T(8,128)(2,1)S(1)}, u32[]{:S(2)}, u32[]{:S(2)}) collective-permute-start(bf16[2048,128]{1,0:T(8,128)(2,1)S(1)} %collective-permute-done), channel_id=1, source_target_pairs={{0,32},{16,48},{32,64},{48,80},{64,96},{80,112},{96,0},{112,16},{1... | collective-permute-start | bytes 1572872 | tf_op jit(solution)/shard_map/ppermute | solution.py:288
  20.4 12.8 %collective-permute-start.4 = (bf16[2048,128]{1,0:T(8,128)(2,1)S(1)}, bf16[2048,128]{1,0:T(8,128)(2,1)S(1)}, u32[]{:S(2)}, u32[]{:S(2)}) collective-permute-start(bf16[2048,128]{1,0:T(8,128)(2,1)S(1)} %collective-permute-done.1), channel_id=1, source_target_pairs={{0,96},{16,112},{32,0},{48,16},{64,32},{80,48},{96,64},{112,80},{1... | collective-permute-start | bytes 1572872 | tf_op jit(solution)/shard_map/ppermute | solution.py:288
  23.3 26.9 %collective-permute-start.8 = (bf16[6144,128]{1,0:T(8,128)(2,1)S(1)}, bf16[6144,128]{1,0:T(8,128)(2,1)S(1)}, u32[]{:S(2)}, u32[]{:S(2)}) collective-permute-start(bf16[6144,128]{1,0:T(8,128)(2,1)S(1)} %constant_dynamic-update-slice_fusion.rest_2_), channel_id=1, source_target_pairs={{0,1},{1,0},{2,3},{3,2},{4,5},{5,4},{6,7},{7,6},{8,9},{9,8},{10,11... | collective-permute-start | bytes 4718600 | tf_op jit(solution)/shard_map/ppermute | solution.py:294
  33.2 17.0 %copy-start = (bf16[2048,256]{1,0:T(8,128)(2,1)S(1)}, bf16[2048,256]{1,0:T(8,128)(2,1)}, u32[]{:S(2)}) copy-start(bf16[2048,256]{1,0:T(8,128)(2,1)} %q_ref.1) | copy-start | bytes 3145732
  33.2 17.0 %copy-start.1 = (bf16[2048,128]{1,0:T(8,128)(2,1)S(1)}, bf16[2048,128]{1,0:T(8,128)(2,1)}, u32[]{:S(2)}) copy-start(bf16[2048,128]{1,0:T(8,128)(2,1)} %get-tuple-element.30.rest_0_) | copy-start | bytes 1572868
  33.2 17.0 %copy-start.2 = (bf16[2048,128]{1,0:T(8,128)(2,1)S(1)}, bf16[2048,128]{1,0:T(8,128)(2,1)}, u32[]{:S(2)}) copy-start(bf16[2048,128]{1,0:T(8,128)(2,1)} %get-tuple-element.31.rest_1_) | copy-start | bytes 1572868
  33.2 17.0 %copy-start.3 = (s32[2]{0:T(128)S(1)}, s32[2]{0:T(128)}, u32[]{:S(2)}) copy-start(s32[2]{0:T(128)} %pad_add_fusion.1.meta) | copy-start | bytes 28
  33.4 16.8 %collective-permute-start.9 = (bf16[6144,128]{1,0:T(8,128)(2,1)S(1)}, bf16[6144,128]{1,0:T(8,128)(2,1)S(1)}, u32[]{:S(2)}, u32[]{:S(2)}) collective-permute-start(bf16[6144,128]{1,0:T(8,128)(2,1)S(1)} %constant_dynamic-update-slice_fusion.3.rest_3_), channel_id=1, source_target_pairs={{0,1},{1,0},{2,3},{3,2},{4,5},{5,4},{6,7},{7,6},{8,9},{9,8},{10,11... | collective-permute-start | bytes 4718600 | tf_op jit(solution)/shard_map/ppermute | solution.py:294
  36.3 8.5 %collective-permute-start.7 = (bf16[1024,128]{1,0:T(8,128)(2,1)S(1)}, bf16[1024,128]{1,0:T(8,128)(2,1)S(1)}, u32[]{:S(2)}, u32[]{:S(2)}) collective-permute-start(bf16[1024,128]{1,0:T(8,128)(2,1)S(1)} %slice.9), channel_id=1, source_target_pairs={{0,96},{16,112},{32,0},{48,16},{64,32},{80,48},{96,64},{112,80},{1... | collective-permute-start | bytes 786440 | tf_op jit(solution)/shard_map/ppermute | solution.py:288
  39.1 8.9 %collective-permute-start.6 = (bf16[1024,128]{1,0:T(8,128)(2,1)S(1)}, bf16[1024,128]{1,0:T(8,128)(2,1)S(1)}, u32[]{:S(2)}, u32[]{:S(2)}) collective-permute-start(bf16[1024,128]{1,0:T(8,128)(2,1)S(1)} %slice.8), channel_id=1, source_target_pairs={{0,32},{16,48},{32,64},{48,80},{64,96},{80,112},{96,0},{112,16},{1... | collective-permute-start | bytes 786440 | tf_op jit(solution)/shard_map/ppermute | solution.py:288
  44.8 4.3 %collective-permute-start.11 = (bf16[1024,128]{1,0:T(8,128)(2,1)S(1)}, bf16[1024,128]{1,0:T(8,128)(2,1)S(1)}, u32[]{:S(2)}, u32[]{:S(2)}) collective-permute-start(bf16[1024,128]{1,0:T(8,128)(2,1)S(1)} %collective-permute-done.7.rest_5_), channel_id=1, source_target_pairs={{0,1},{1,0},{2,3},{3,2},{4,5},{5,4},{6,7},{7,6},{8,9},{9,8},{10,11... | collective-permute-start | bytes 786440 | tf_op jit(solution)/shard_map/ppermute | solution.py:294
  47.9 2.3 %collective-permute-start.10 = (bf16[1024,128]{1,0:T(8,128)(2,1)S(1)}, bf16[1024,128]{1,0:T(8,128)(2,1)S(1)}, u32[]{:S(2)}, u32[]{:S(2)}) collective-permute-start(bf16[1024,128]{1,0:T(8,128)(2,1)S(1)} %collective-permute-done.6.rest_4_), channel_id=1, source_target_pairs={{0,1},{1,0},{2,3},{3,2},{4,5},{5,4},{6,7},{7,6},{8,9},{9,8},{10,11... | collective-permute-start | bytes 786440 | tf_op jit(solution)/shard_map/ppermute | solution.py:294

commit v8 on v6

--- a/solution.py
+++ b/solution.py
@@ -27,28 +27,31 @@
     return lax.dot_general(a, b, (((1,), (1,)), ((), ())), preferred_element_type=jnp.float32)
 
 
-def own_kernel(meta, keys, values, own_ref, keys_ref, values_ref, value_s, sem):
-    column = pl.ds(pl.multiple_of(meta[1] * DH, DH), DH)
-    value_copy = pltpu.make_async_copy(values.at[:, column], value_s, sem.at[0])
-    key_copy = pltpu.make_async_copy(keys.at[:, column], keys_ref, sem.at[1])
-    value_copy.start()
-    key_copy.start()
-    value_copy.wait()
-    for start in range(0, value_s.shape[0], BLOCK):
-        rows = slice(start, start + BLOCK)
-        values_ref[rows, :] = value_s[rows, :].T
-    key_copy.wait()
-
-    @pl.when(meta[0] == 0)
-    def _():
-        own_ref[...] = keys_ref[...]
-
-    @pl.when(meta[0] != 0)
-    def _():
-        own_ref[...] = values_ref[...]
-
-
-def attend_kernel(sizes, slots, heads, meta, lists, counts, sent, start, q_ref, rank_ref, *rest):
+def own_kernel(keys, values, own_ref, keys_ref, values_ref, value_s, sem):
+    core = lax.rem(lax.axis_index("rows"), 2)
+    head = lax.axis_index("rows") * (HEADS // lax.axis_size("rows")) // (HEADS // KV_HEADS)
+    column = pl.ds(pl.multiple_of(head * DH, DH), DH)
+    parts = [slice(start, start + BLOCK) for start in range(0, value_s.shape[0], BLOCK)]
+    copies = []
+    for i, rows in enumerate(parts):
+        copies.append(
+            (
+                pltpu.make_async_copy(values.at[rows, column], value_s.at[rows], sem.at[2 * i]),
+                pltpu.make_async_copy(keys.at[rows, column], keys_ref.at[rows], sem.at[2 * i + 1]),
+            )
+        )
+    for value_copy, key_copy in copies:
+        value_copy.start()
+        key_copy.start()
+    for rows, (value_copy, key_copy) in zip(parts, copies):
+        value_copy.wait()
+        turned = value_s[rows, :].T
+        values_ref[rows, :] = turned
+        key_copy.wait()
+        own_ref[rows, :] = jnp.where(core == 0, keys_ref[rows, :], turned)
+
+
+def attend_kernel(sizes, slots, heads, lists, counts, sent, start, q_ref, rank_ref, *rest):
     rest = list(rest)
     take = lambda n: [rest.pop(0) for _ in range(n)]
     pieces = len(sizes)
@@ -59,7 +62,7 @@
     att, sorted_s, sem = take(3)
     shard = q_ref.shape[0]
     nblk = shard // BLOCK
-    core = meta[0]
+    core = lax.rem(lax.axis_index("rows"), 2)
     key_copies, value_copies = [], []
     for number, (ref, to, held) in enumerate(zip(own, (k_s, v_s), (key_copies, value_copies))):
         copy = pltpu.make_async_copy(ref, to.at[pl.ds(0, shard)], sem.at[number])
@@ -250,25 +253,20 @@
     cycle = lax.axis_size("ctx")
     groups = lax.axis_size("rows")
     place = lax.axis_index("ctx")
-    group = lax.axis_index("rows")
     rows_here = queries.shape[0]
     heads = verticals.shape[0]
     nblk = rows_here // BLOCK
     devices = cycle * groups
     own_rows = rows_here // groups
-    kv_index = group * heads // (HEADS // KV_HEADS)
-    core = group % 2
-
-    meta = jnp.stack([core, kv_index]).astype(jnp.int32)
     own, *here = pl.pallas_call(
         own_kernel,
         out_shape=[jax.ShapeDtypeStruct((rows_here, DH), jnp.bfloat16)] * 3,
-        in_specs=[SMEM, ANY, ANY],
+        in_specs=[ANY, ANY],
         out_specs=[VMEM] * 3,
-        scratch_shapes=[pltpu.VMEM((rows_here, DH), jnp.bfloat16), pltpu.SemaphoreType.DMA((2,))],
+        scratch_shapes=[pltpu.VMEM((rows_here, DH), jnp.bfloat16), pltpu.SemaphoreType.DMA((2 * nblk,))],
         compiler_params=pltpu.CompilerParams(vmem_limit_bytes=60 * 1024 * 1024),
         name="own",
-    )(meta, keys, values)
+    )(keys, values)
 
     def along_x(x, step):
         return lax.ppermute(x, "ctx", [(c, (c + 2 * step) % cycle) for c in range(cycle)])
@@ -293,7 +291,7 @@
     p2 = along_x(own, -1)
     lists, counts = block_lists(verticals, slashes, place, nblk, cycle)
     small = (lists, counts, sent, start, rank.reshape(1, rows_here))
-    p1, p3, small = lax.optimization_barrier((p1, p3, small))
+    p1, small = lax.optimization_barrier((p1, small))
 
     p4 = along_x(p1, 1)
     p5 = along_x(p3, -1)
@@ -310,7 +308,7 @@
     outgoing = pl.pallas_call(
         functools.partial(attend_kernel, [x.shape[0] for x in mine], slots, heads),
         out_shape=jax.ShapeDtypeStruct((devices * SLOT, heads * DH), jnp.bfloat16),
-        in_specs=[SMEM] * 5 + [VMEM] * 2 + [ANY] * (2 + 2 * len(mine)),
+        in_specs=[SMEM] * 4 + [VMEM] * 2 + [ANY] * (2 + 2 * len(mine)),
         out_specs=VMEM,
         scratch_shapes=[pltpu.VMEM((cycle * rows_here, DH), jnp.bfloat16)] * 2
         + [pltpu.VMEM(((slots + 1) * BLOCK, BLOCK), jnp.float32)] * (2 * heads)
@@ -322,7 +320,7 @@
         ],
         compiler_params=pltpu.CompilerParams(vmem_limit_bytes=28 * 1024 * 1024),
         name="attend",
-    )(meta, lists, counts, sent, start, queries, rank, *here, *mine, *other)
+    )(lists, counts, sent, start, queries, rank, *here, *mine, *other)
 
     incoming = lax.all_to_all(
         outgoing.reshape(devices, SLOT, heads * DH), ("ctx", "rows"), split_axis=0, concat_axis=0, tiled=True

time: 113 us -> 113 us (level)
    ppermute x2, waiting for transfers between devices: 4.71 us -> 0.01 us  [along_z(): return lax.ppermute(x, 'ctx', [(c, c ^ 1) for c in range(cycle)])]
    ppermute x6, waiting for transfers between devices: 17.5 us -> 22.1 us  [along_x(): lax.ppermute(x, 'ctx', [(c, (c + 2 * step) % cycle) for c in range(cycle)])]
  transfers between devices with their start and end apart: 12 -> 12, of which waited for: 6 -> 5; matrix products, arithmetic and copies ran while one was open for 4% -> 4% of each run, Pallas kernels for 0% -> 0%
where the time goes in v8:
time: 113 us
  blocking collectives  37.1 us (33%)
  Pallas kernels  29.1 us (26%)
  waiting for transfers between devices  23.3 us (21%)
  starting transfers between devices  18.5 us (16%)
  other arithmetic  4.22 us (4%)
    all_to_all x1, blocking collectives, body(): lax.all_to_all(outgoing.reshape(devices, SLOT, heads * DH), ('ctx', 'rows...  37.1 us
    pallas_call x1, Pallas kernels, body(): pl.pallas_call(functools.partial(attend_kernel, [x.shape[0] for x in mine...  24 us
    ppermute x6, waiting for transfers between devices, along_x(): lax.ppermute(x, 'ctx', [(c, (c + 2 * step) % cycle) for c in range(cycle)])  22.1 us
    ppermute x6, starting transfers between devices, along_x(): lax.ppermute(x, 'ctx', [(c, (c + 2 * step) % cycle) for c in range(cycle)])  8.34 us
    ppermute x4, starting transfers between devices, swap(): return lax.ppermute(x, 'rows', [(r, r ^ 1) for r in range(groups)])  7.21 us
    pallas_call x1, Pallas kernels, body(): pl.pallas_call(own_kernel, out_shape=[jax.ShapeDtypeStruct((rows_here, DH...  3.48 us
    ppermute x2, starting transfers between devices, along_z(): return lax.ppermute(x, 'ctx', [(c, c ^ 1) for c in range(cycle)])  2.95 us
  transfers between devices with their start and end apart: 12, of which 5 were waited for; matrix products, arithmetic and copies ran while one was open for 4% of the time, Pallas kernels for 0%

profile of v8, /device:TPU:1, one launch (start us, length us, event | category | flops | bytes accessed | tf_op | source)
XLA Modules:
  0.0 112.9 jit_solution(3923061290596540502)
XLA Ops:
  0.0 0.0 copy-start.3
  0.0 0.0 copy-start.4
  0.0 0.0 copy-start.5
  0.0 3.5 %own.1 = (bf16[2048,128]{1,0:T(8,128)(2,1)}, bf16[2048,128]{1,0:T(8,128)(2,1)}, bf16[2048,128]{1,0:T(8,128)(2,1)}) custom-call(bf16[2048,1024]{1,0:T(8,128)(2,1)} %keys.1, bf16[2048,1024]{1,0:T(8,128)(2,1)} %values.1), custom_call_target="tpu_custom_call" | custom-call | tf_op jit(solution)/shard_map/own/pallas_call | solution.py:261
  3.5 2.5 %collective-permute-start.2 = (bf16[2048,128]{1,0:T(8,128)(2,1)}, bf16[2048,128]{1,0:T(8,128)(2,1)S(1)}, u32[]{:S(2)}, u32[]{:S(2)}) collective-permute-start(bf16[2048,128]{1,0:T(8,128)(2,1)} %get-tuple-element.26), channel_id=1, source_target_pairs={{0,16},{16,0},{32,48},{48,32},{64,80},{80,64},{96,112},{112,96},{1... | collective-permute-start | bytes 1572872 | tf_op jit(solution)/shard_map/ppermute | solution.py:275
  6.0 1.2 %collective-permute-start = (bf16[2048,128]{1,0:T(8,128)(2,1)}, bf16[2048,128]{1,0:T(8,128)(2,1)S(1)}, u32[]{:S(2)}, u32[]{:S(2)}) collective-permute-start(bf16[2048,128]{1,0:T(8,128)(2,1)} %get-tuple-element.26), channel_id=1, source_target_pairs={{0,32},{16,48},{32,64},{48,80},{64,96},{80,112},{96,0},{112,16},{1... | collective-permute-start | bytes 1572872 | tf_op jit(solution)/shard_map/ppermute | solution.py:272
  7.3 0.0 copy-done.3
  7.3 1.2 %select_reduce_fusion.1 = (s32[128]{0:T(128)S(1)}, s32[128]{0:T(128)S(1)}) fusion(s32[2048]{0:T(1024)S(1)} %copy-done.3, s32[2048]{0:T(1024)S(1)} %add_select_fusion.5), kind=kLoop, calls=%fused_computation.1 | loop fusion | flops 1310464 | bytes 17408 | tf_op jit(solution)/shard_map/reduce_min | solution.py:283
  8.5 1.5 %collective-permute-start.1 = (bf16[2048,128]{1,0:T(8,128)(2,1)}, bf16[2048,128]{1,0:T(8,128)(2,1)S(1)}, u32[]{:S(2)}, u32[]{:S(2)}) collective-permute-start(bf16[2048,128]{1,0:T(8,128)(2,1)} %get-tuple-element.26), channel_id=1, source_target_pairs={{0,96},{16,112},{32,0},{48,16},{64,32},{80,48},{96,64},{112,80},{1... | collective-permute-start | bytes 1572872 | tf_op jit(solution)/shard_map/ppermute | solution.py:272
  10.0 0.1 select_reduce_fusion.3.start
  10.2 0.0 copy-done.4
  10.2 0.1 broadcast_subtract_fusion
  10.2 0.0 copy-done.5
  10.2 0.1 pad_add_fusion
  10.3 0.8 and_reduce_fusion
  11.1 0.2 convert_reduce_fusion.2
  11.3 0.6 select_reduce_fusion
  12.0 0.1 reshape.230.counts
  12.1 0.6 convert_reduce_fusion.1
  12.7 0.5 select_reduce_fusion.2
  13.2 6.8 %collective-permute-done = bf16[2048,128]{1,0:T(8,128)(2,1)S(1)} collective-permute-done((bf16[2048,128]{1,0:T(8,128)(2,1)}, bf16[2048,128]{1,0:T(8,128)(2,1)S(1)}, u32[]{:S(2)}, u32[]{:S(2)}) %collective-permute-start) | collective-permute-done | bytes 524320 | tf_op jit(solution)/shard_map/ppermute | solution.py:272
  19.9 0.4 collective-permute-start.5
  20.3 0.0 collective-permute-start.3
  20.4 0.0 collective-permute-done.2
  20.4 2.7 %collective-permute-start.4 = (bf16[2048,128]{1,0:T(8,128)(2,1)S(1)}, bf16[2048,128]{1,0:T(8,128)(2,1)S(1)}, u32[]{:S(2)}, u32[]{:S(2)}) collective-permute-start(bf16[2048,128]{1,0:T(8,128)(2,1)S(1)} %collective-permute-done.2), channel_id=1, source_target_pairs={{0,96},{16,112},{32,0},{48,16},{64,32},{80,48},{96,64},{112,80},{1... | collective-permute-start | bytes 1572872 | tf_op jit(solution)/shard_map/ppermute | solution.py:272
  23.1 0.0 collective-permute-done.1
  23.1 0.1 constant_dynamic-update-slice_fusion.1
  23.2 0.1 constant_dynamic-update-slice_fusion.rest_2_
  23.3 2.5 %collective-permute-start.8 = (bf16[6144,128]{1,0:T(8,128)(2,1)S(1)}, bf16[6144,128]{1,0:T(8,128)(2,1)S(1)}, u32[]{:S(2)}, u32[]{:S(2)}) collective-permute-start(bf16[6144,128]{1,0:T(8,128)(2,1)S(1)} %constant_dynamic-update-slice_fusion.rest_2_), channel_id=1, source_target_pairs={{0,1},{1,0},{2,3},{3,2},{4,5},{5,4},{6,7},{7,6},{8,9},{9,8},{10,11... | collective-permute-start | bytes 4718600 | tf_op jit(solution)/shard_map/ppermute | solution.py:278
  25.8 7.4 %collective-permute-done.3 = bf16[2048,128]{1,0:T(8,128)(2,1)S(1)} collective-permute-done((bf16[2048,128]{1,0:T(8,128)(2,1)S(1)}, bf16[2048,128]{1,0:T(8,128)(2,1)S(1)}, u32[]{:S(2)}, u32[]{:S(2)}) %collective-permute-start.3) | collective-permute-done | bytes 524320 | tf_op jit(solution)/shard_map/ppermute | solution.py:272
  33.2 0.0 copy-start
  33.2 0.0 copy-start.1
  33.2 0.0 copy-start.2
  33.2 0.0 collective-permute-done.4
  33.2 0.1 constant_dynamic-update-slice_fusion.4
  33.3 0.0 collective-permute-done.5
  33.3 0.1 constant_dynamic-update-slice_fusion.3.rest_3_
  33.4 2.8 %collective-permute-start.9 = (bf16[6144,128]{1,0:T(8,128)(2,1)S(1)}, bf16[6144,128]{1,0:T(8,128)(2,1)S(1)}, u32[]{:S(2)}, u32[]{:S(2)}) collective-permute-start(bf16[6144,128]{1,0:T(8,128)(2,1)S(1)} %constant_dynamic-update-slice_fusion.3.rest_3_), channel_id=1, source_target_pairs={{0,1},{1,0},{2,3},{3,2},{4,5},{5,4},{6,7},{7,6},{8,9},{9,8},{10,11... | collective-permute-start | bytes 4718600 | tf_op jit(solution)/shard_map/ppermute | solution.py:278
  36.2 2.8 %collective-permute-start.7 = (bf16[1024,128]{1,0:T(8,128)(2,1)S(1)}, bf16[1024,128]{1,0:T(8,128)(2,1)S(1)}, u32[]{:S(2)}, u32[]{:S(2)}) collective-permute-start(bf16[1024,128]{1,0:T(8,128)(2,1)S(1)} %slice.9), channel_id=1, source_target_pairs={{0,96},{16,112},{32,0},{48,16},{64,32},{80,48},{96,64},{112,80},{1... | collective-permute-start | bytes 786440 | tf_op jit(solution)/shard_map/ppermute | solution.py:272
  39.0 0.1 collective-permute-start.6
  39.1 5.6 %collective-permute-done.7.rest_5_ = bf16[1024,128]{1,0:T(8,128)(2,1)S(1)} collective-permute-done((bf16[1024,128]{1,0:T(8,128)(2,1)S(1)}, bf16[1024,128]{1,0:T(8,128)(2,1)S(1)}, u32[]{:S(2)}, u32[]{:S(2)}) %collective-permute-start.7) | collective-permute-done | bytes 262176 | tf_op jit(solution)/shard_map/ppermute | solution.py:272
  44.7 0.8 collective-permute-start.11
  45.5 2.4 %collective-permute-done.6.rest_4_ = bf16[1024,128]{1,0:T(8,128)(2,1)S(1)} collective-permute-done((bf16[1024,128]{1,0:T(8,128)(2,1)S(1)}, bf16[1024,128]{1,0:T(8,128)(2,1)S(1)}, u32[]{:S(2)}, u32[]{:S(2)}) %collective-permute-start.6) | collective-permute-done | bytes 262176 | tf_op jit(solution)/shard_map/ppermute | solution.py:272
  47.9 1.1 collective-permute-start.10
  49.0 0.0 collective-permute-done.11.rest_9_
  49.0 1.2 %collective-permute-done.10.rest_8_ = bf16[1024,128]{1,0:T(8,128)(2,1)S(1)} collective-permute-done((bf16[1024,128]{1,0:T(8,128)(2,1)S(1)}, bf16[1024,128]{1,0:T(8,128)(2,1)S(1)}, u32[]{:S(2)}, u32[]{:S(2)}) %collective-permute-start.10) | collective-permute-done | bytes 262176 | tf_op jit(solution)/shard_map/ppermute | solution.py:278
  50.2 0.0 collective-permute-done.8.rest_6_
  50.2 0.0 collective-permute-done.9.rest_7_
  50.2 0.0 copy-done
  50.2 0.0 copy-done.1
  50.2 0.0 copy-done.2
  50.2 24.0 %attend.1 = bf16[4096,256]{1,0:T(8,128)(2,1)S(1)} custom-call(s32[32,24]{1,0:T(8,128)S(1)} %bitcast.6, s32[32]{0:T(128)S(1)} %reshape.230.counts, s32[128]{0:T(128)S(1)} %get-tuple-element.20.sent, s32[128]{0:T(128)S(1)} %select_reduce_fusion.3.start, bf16[2048,256]{1,0:T(8,128)(2,1)S(1)} %copy-done, s32[1,2048]{1,0:T(1,128)S(1)} %bitcast.7, ...), custom_call_target="tpu_custom_call" | custom-call | tf_op jit(solution)/shard_map/attend/pallas_call | solution.py:308
  74.3 37.1 %all_to_all.5 = bf16[128,32,256]{2,1,0:T(8,128)(2,1)S(1)} all-to-all(bf16[128,32,256]{2,1,0:T(8,128)(2,1)S(1)} %bitcast.5), channel_id=1, replica_groups=mesh['ctx'=8,'rows'=16] {'ctx','rows'}, dimensions={0} | all-to-all | bytes 4194304 | tf_op jit(solution)/shard_map/all_to_all | solution.py:325
  111.3 1.6 %arrange.1 = bf16[128,4096]{1,0:T(8,128)(2,1)} custom-call(bf16[8,16,32,256]{3,2,1,0:T(8,128)(2,1)S(1)} %bitcast.4), custom_call_target="tpu_custom_call" | custom-call | tf_op jit(solution)/shard_map/arrange/pallas_call | solution.py:329
  (10 shorter events, 0.1 us)
Async XLA Ops:
  0.0 7.3 %copy-start.3 = (s32[2048]{0:T(1024)S(1)}, s32[2048]{0:T(1024)}, u32[]{:S(2)}) copy-start(s32[2048]{0:T(1024)} %param.11) | copy-start | bytes 24580
  0.0 10.2 %copy-start.4 = (s32[2,16]{1,0:T(2,128)S(1)}, s32[2,16]{1,0:T(2,128)}, u32[]{:S(2)}) copy-start(s32[2,16]{1,0:T(2,128)} %param.10) | copy-start | bytes 388
  0.0 10.2 %copy-start.5 = (s32[2,8]{1,0:T(2,128)S(1)}, s32[2,8]{1,0:T(2,128)}, u32[]{:S(2)}) copy-start(s32[2,8]{1,0:T(2,128)} %param.9) | copy-start | bytes 196
  3.5 16.9 %collective-permute-start.2 = (bf16[2048,128]{1,0:T(8,128)(2,1)}, bf16[2048,128]{1,0:T(8,128)(2,1)S(1)}, u32[]{:S(2)}, u32[]{:S(2)}) collective-permute-start(bf16[2048,128]{1,0:T(8,128)(2,1)} %get-tuple-element.26), channel_id=1, source_target_pairs={{0,16},{16,0},{32,48},{48,32},{64,80},{80,64},{96,112},{112,96},{1... | collective-permute-start | bytes 1572872 | tf_op jit(solution)/shard_map/ppermute | solution.py:275
  6.0 13.9 %collective-permute-start = (bf16[2048,128]{1,0:T(8,128)(2,1)}, bf16[2048,128]{1,0:T(8,128)(2,1)S(1)}, u32[]{:S(2)}, u32[]{:S(2)}) collective-permute-start(bf16[2048,128]{1,0:T(8,128)(2,1)} %get-tuple-element.26), channel_id=1, source_target_pairs={{0,32},{16,48},{32,64},{48,80},{64,96},{80,112},{96,0},{112,16},{1... | collective-permute-start | bytes 1572872 | tf_op jit(solution)/shard_map/ppermute | solution.py:272
  8.5 14.7 %collective-permute-start.1 = (bf16[2048,128]{1,0:T(8,128)(2,1)}, bf16[2048,128]{1,0:T(8,128)(2,1)S(1)}, u32[]{:S(2)}, u32[]{:S(2)}) collective-permute-start(bf16[2048,128]{1,0:T(8,128)(2,1)} %get-tuple-element.26), channel_id=1, source_target_pairs={{0,96},{16,112},{32,0},{48,16},{64,32},{80,48},{96,64},{112,80},{1... | collective-permute-start | bytes 1572872 | tf_op jit(solution)/shard_map/ppermute | solution.py:272
  19.9 13.4 %collective-permute-start.5 = (bf16[2048,128]{1,0:T(8,128)(2,1)S(1)}, bf16[2048,128]{1,0:T(8,128)(2,1)S(1)}, u32[]{:S(2)}, u32[]{:S(2)}) collective-permute-start(bf16[2048,128]{1,0:T(8,128)(2,1)S(1)} %collective-permute-done), channel_id=1, source_target_pairs={{0,16},{16,0},{32,48},{48,32},{64,80},{80,64},{96,112},{112,96},{1... | collective-permute-start | bytes 1572872 | tf_op jit(solution)/shard_map/ppermute | solution.py:275
  20.3 12.8 %collective-permute-start.3 = (bf16[2048,128]{1,0:T(8,128)(2,1)S(1)}, bf16[2048,128]{1,0:T(8,128)(2,1)S(1)}, u32[]{:S(2)}, u32[]{:S(2)}) collective-permute-start(bf16[2048,128]{1,0:T(8,128)(2,1)S(1)} %collective-permute-done), channel_id=1, source_target_pairs={{0,32},{16,48},{32,64},{48,80},{64,96},{80,112},{96,0},{112,16},{1... | collective-permute-start | bytes 1572872 | tf_op jit(solution)/shard_map/ppermute | solution.py:272
  20.4 12.8 %collective-permute-start.4 = (bf16[2048,128]{1,0:T(8,128)(2,1)S(1)}, bf16[2048,128]{1,0:T(8,128)(2,1)S(1)}, u32[]{:S(2)}, u32[]{:S(2)}) collective-permute-start(bf16[2048,128]{1,0:T(8,128)(2,1)S(1)} %collective-permute-done.2), channel_id=1, source_target_pairs={{0,96},{16,112},{32,0},{48,16},{64,32},{80,48},{96,64},{112,80},{1... | collective-permute-start | bytes 1572872 | tf_op jit(solution)/shard_map/ppermute | solution.py:272
  23.3 26.9 %collective-permute-start.8 = (bf16[6144,128]{1,0:T(8,128)(2,1)S(1)}, bf16[6144,128]{1,0:T(8,128)(2,1)S(1)}, u32[]{:S(2)}, u32[]{:S(2)}) collective-permute-start(bf16[6144,128]{1,0:T(8,128)(2,1)S(1)} %constant_dynamic-update-slice_fusion.rest_2_), channel_id=1, source_target_pairs={{0,1},{1,0},{2,3},{3,2},{4,5},{5,4},{6,7},{7,6},{8,9},{9,8},{10,11... | collective-permute-start | bytes 4718600 | tf_op jit(solution)/shard_map/ppermute | solution.py:278
  33.2 17.0 %copy-start = (bf16[2048,256]{1,0:T(8,128)(2,1)S(1)}, bf16[2048,256]{1,0:T(8,128)(2,1)}, u32[]{:S(2)}) copy-start(bf16[2048,256]{1,0:T(8,128)(2,1)} %q_ref.1) | copy-start | bytes 3145732
  33.2 17.0 %copy-start.1 = (bf16[2048,128]{1,0:T(8,128)(2,1)S(1)}, bf16[2048,128]{1,0:T(8,128)(2,1)}, u32[]{:S(2)}) copy-start(bf16[2048,128]{1,0:T(8,128)(2,1)} %get-tuple-element.23.rest_0_) | copy-start | bytes 1572868
  33.2 17.0 %copy-start.2 = (bf16[2048,128]{1,0:T(8,128)(2,1)S(1)}, bf16[2048,128]{1,0:T(8,128)(2,1)}, u32[]{:S(2)}) copy-start(bf16[2048,128]{1,0:T(8,128)(2,1)} %get-tuple-element.24.rest_1_) | copy-start | bytes 1572868
  33.4 16.8 %collective-permute-start.9 = (bf16[6144,128]{1,0:T(8,128)(2,1)S(1)}, bf16[6144,128]{1,0:T(8,128)(2,1)S(1)}, u32[]{:S(2)}, u32[]{:S(2)}) collective-permute-start(bf16[6144,128]{1,0:T(8,128)(2,1)S(1)} %constant_dynamic-update-slice_fusion.3.rest_3_), channel_id=1, source_target_pairs={{0,1},{1,0},{2,3},{3,2},{4,5},{5,4},{6,7},{7,6},{8,9},{9,8},{10,11... | collective-permute-start | bytes 4718600 | tf_op jit(solution)/shard_map/ppermute | solution.py:278
  36.2 8.5 %collective-permute-start.7 = (bf16[1024,128]{1,0:T(8,128)(2,1)S(1)}, bf16[1024,128]{1,0:T(8,128)(2,1)S(1)}, u32[]{:S(2)}, u32[]{:S(2)}) collective-permute-start(bf16[1024,128]{1,0:T(8,128)(2,1)S(1)} %slice.9), channel_id=1, source_target_pairs={{0,96},{16,112},{32,0},{48,16},{64,32},{80,48},{96,64},{112,80},{1... | collective-permute-start | bytes 786440 | tf_op jit(solution)/shard_map/ppermute | solution.py:272
  39.0 8.9 %collective-permute-start.6 = (bf16[1024,128]{1,0:T(8,128)(2,1)S(1)}, bf16[1024,128]{1,0:T(8,128)(2,1)S(1)}, u32[]{:S(2)}, u32[]{:S(2)}) collective-permute-start(bf16[1024,128]{1,0:T(8,128)(2,1)S(1)} %slice.8), channel_id=1, source_target_pairs={{0,32},{16,48},{32,64},{48,80},{64,96},{80,112},{96,0},{112,16},{1... | collective-permute-start | bytes 786440 | tf_op jit(solution)/shard_map/ppermute | solution.py:272
  44.7 4.3 %collective-permute-start.11 = (bf16[1024,128]{1,0:T(8,128)(2,1)S(1)}, bf16[1024,128]{1,0:T(8,128)(2,1)S(1)}, u32[]{:S(2)}, u32[]{:S(2)}) collective-permute-start(bf16[1024,128]{1,0:T(8,128)(2,1)S(1)} %collective-permute-done.7.rest_5_), channel_id=1, source_target_pairs={{0,1},{1,0},{2,3},{3,2},{4,5},{5,4},{6,7},{7,6},{8,9},{9,8},{10,11... | collective-permute-start | bytes 786440 | tf_op jit(solution)/shard_map/ppermute | solution.py:278
  47.9 2.3 %collective-permute-start.10 = (bf16[1024,128]{1,0:T(8,128)(2,1)S(1)}, bf16[1024,128]{1,0:T(8,128)(2,1)S(1)}, u32[]{:S(2)}, u32[]{:S(2)}) collective-permute-start(bf16[1024,128]{1,0:T(8,128)(2,1)S(1)} %collective-permute-done.6.rest_4_), channel_id=1, source_target_pairs={{0,1},{1,0},{2,3},{3,2},{4,5},{5,4},{6,7},{7,6},{8,9},{9,8},{10,11... | collective-permute-start | bytes 786440 | tf_op jit(solution)/shard_map/ppermute | solution.py:278

commit v9 on v7

--- a/solution.py
+++ b/solution.py
@@ -27,26 +27,17 @@
     return lax.dot_general(a, b, (((1,), (1,)), ((), ())), preferred_element_type=jnp.float32)
 
 
-def sent_kernel(meta, keys, values, sent_ref, value_s, sem):
-    column = pl.ds(pl.multiple_of(meta[1] * DH, DH), DH)
-
-    @pl.when(meta[0] == 0)
-    def _():
-        pltpu.make_async_copy(keys.at[:, column], value_s, sem.at[0]).start()
-
-    @pl.when(meta[0] != 0)
-    def _():
-        pltpu.make_async_copy(values.at[:, column], value_s, sem.at[0]).start()
-
-    pltpu.make_async_copy(keys.at[:, column], value_s, sem.at[0]).wait()
-    for start in range(0, value_s.shape[0], BLOCK):
+def turn_kernel(block_ref, out_ref):
+    core = lax.rem(lax.axis_index("rows"), 2)
+    for start in range(0, block_ref.shape[0], BLOCK):
         rows = slice(start, start + BLOCK)
-        block = value_s[rows, :]
-        sent_ref[rows, :] = jnp.where(meta[0] == 0, block, block.T)
-
-
-def own_kernel(meta, keys, values, keys_ref, values_ref, value_s, sem):
-    column = pl.ds(pl.multiple_of(meta[1] * DH, DH), DH)
+        block = block_ref[rows, :]
+        out_ref[rows, :] = jnp.where(core == 0, block, block.T)
+
+
+def own_kernel(keys, values, keys_ref, values_ref, value_s, sem):
+    head = lax.axis_index("rows") * (HEADS // lax.axis_size("rows")) // (HEADS // KV_HEADS)
+    column = pl.ds(pl.multiple_of(head * DH, DH), DH)
     copies = [
         pltpu.make_async_copy(values.at[:, column], value_s, sem.at[0]),
         pltpu.make_async_copy(keys.at[:, column], keys_ref, sem.at[1]),
@@ -60,7 +51,7 @@
         values_ref[rows, :] = value_s[rows, :].T
 
 
-def attend_kernel(sizes, slots, heads, meta, lists, counts, sent, start, q_ref, rank_ref, *rest):
+def attend_kernel(sizes, slots, heads, lists, counts, sent, start, q_ref, rank_ref, *rest):
     rest = list(rest)
     take = lambda n: [rest.pop(0) for _ in range(n)]
     pieces = len(sizes)
@@ -71,7 +62,7 @@
     att, sorted_s, sem = take(3)
     shard = q_ref.shape[0]
     nblk = shard // BLOCK
-    core = meta[0]
+    core = lax.rem(lax.axis_index("rows"), 2)
     key_copies, value_copies = [], []
     for number, (ref, to, held) in enumerate(zip(own, (k_s, v_s), (key_copies, value_copies))):
         copy = pltpu.make_async_copy(ref, to.at[pl.ds(0, shard)], sem.at[number])
@@ -268,21 +259,22 @@
     devices = cycle * groups
     own_rows = rows_here // groups
     group = lax.axis_index("rows")
-    meta = jnp.stack([group % 2, group * heads // (HEADS // KV_HEADS)]).astype(jnp.int32)
+    head = group * heads // (HEADS // KV_HEADS)
     piece = jax.ShapeDtypeStruct((rows_here, DH), jnp.bfloat16)
-
-    def slices(kernel, outs, keys, values):
-        return pl.pallas_call(
-            kernel,
-            out_shape=[piece] * outs,
-            in_specs=[SMEM, ANY, ANY],
-            out_specs=[VMEM] * outs,
-            scratch_shapes=[pltpu.VMEM((rows_here, DH), jnp.bfloat16), pltpu.SemaphoreType.DMA((outs,))],
-            compiler_params=pltpu.CompilerParams(vmem_limit_bytes=60 * 1024 * 1024),
-            name="own",
-        )(meta, keys, values)
-
-    (own,) = slices(sent_kernel, 1, keys, values)
+    own = pl.pallas_call(
+        turn_kernel,
+        out_shape=piece,
+        in_specs=[VMEM],
+        out_specs=VMEM,
+        compiler_params=pltpu.CompilerParams(vmem_limit_bytes=24 * 1024 * 1024),
+        name="turn",
+    )(
+        jnp.where(
+            group % 2 == 0,
+            lax.dynamic_slice_in_dim(keys, head * DH, DH, 1),
+            lax.dynamic_slice_in_dim(values, head * DH, DH, 1),
+        )
+    )
 
     def along_x(x, step):
         return lax.ppermute(x, "ctx", [(c, (c + 2 * step) % cycle) for c in range(cycle)])
@@ -293,7 +285,7 @@
     def swap(x):
         return lax.ppermute(x, "rows", [(r, r ^ 1) for r in range(groups)])
 
-    half = rows_here // 2
+    cut = rows_here * 5 // 8
     owner = destination // own_rows
     member = owner[:, None] == jnp.arange(devices, dtype=jnp.int32)[None, :]
     first_row = jnp.min(jnp.where(member, destination[:, None], ROW_CEILING), axis=0)
@@ -305,18 +297,26 @@
     p3 = along_z(own)
     own, sent, keys, values = lax.optimization_barrier((own, sent, keys, values))
     p2 = along_x(own, -1)
-    here = slices(own_kernel, 2, keys, values)
+    here = pl.pallas_call(
+        own_kernel,
+        out_shape=[piece] * 2,
+        in_specs=[ANY, ANY],
+        out_specs=[VMEM] * 2,
+        scratch_shapes=[pltpu.VMEM((rows_here, DH), jnp.bfloat16), pltpu.SemaphoreType.DMA((2,))],
+        compiler_params=pltpu.CompilerParams(vmem_limit_bytes=60 * 1024 * 1024),
+        name="own",
+    )(keys, values)
     lists, counts = block_lists(verticals, slashes, place, nblk, cycle)
     small = (lists, counts, sent, start, rank.reshape(1, rows_here))
-    p1, p3, small, here = lax.optimization_barrier((p1, p3, small, here))
+    p1, small, here = lax.optimization_barrier((p1, small, here))
 
     p4 = along_x(p1, 1)
     p5 = along_x(p3, -1)
     p6 = along_z(p1)
     mine = [jnp.concatenate([p1, p2, p3], axis=0)]
     other = [swap(mine[0])]
-    p7 = along_x(p6[:half], 1)
-    p8 = along_x(p5[half:], -1)
+    p7 = along_x(p6[:cut], 1)
+    p8 = along_x(p5[cut:], -1)
     mine += [jnp.concatenate([p4, p5, p6], axis=0), p7, p8]
     other += [swap(x) for x in mine[1:]]
 
@@ -325,7 +325,7 @@
     outgoing = pl.pallas_call(
         functools.partial(attend_kernel, [x.shape[0] for x in mine], slots, heads),
         out_shape=jax.ShapeDtypeStruct((devices * SLOT, heads * DH), jnp.bfloat16),
-        in_specs=[SMEM] * 5 + [VMEM] * 2 + [ANY] * (2 + 2 * len(mine)),
+        in_specs=[SMEM] * 4 + [VMEM] * 2 + [ANY] * (2 + 2 * len(mine)),
         out_specs=VMEM,
         scratch_shapes=[pltpu.VMEM((cycle * rows_here, DH), jnp.bfloat16)] * 2
         + [pltpu.VMEM(((slots + 1) * BLOCK, BLOCK), jnp.float32)] * (2 * heads)
@@ -337,7 +337,7 @@
         ],
         compiler_params=pltpu.CompilerParams(vmem_limit_bytes=28 * 1024 * 1024),
         name="attend",
-    )(meta, lists, counts, sent, start, queries, rank, *here, *mine, *other)
+    )(lists, counts, sent, start, queries, rank, *here, *mine, *other)
 
     incoming = lax.all_to_all(
         outgoing.reshape(devices, SLOT, heads * DH), ("ctx", "rows"), split_axis=0, concat_axis=0, tiled=True

time: 114 us -> 113 us (level)
  Pallas kernels: 32.4 us -> 29.7 us
  starting transfers between devices: 18.5 us -> 17.3 us
  blocking collectives: 37.1 us -> 38.3 us
    pallas_call x2, Pallas kernels: 5.73 us -> 2.4 us  [the longest x1 2.21 us: body(): pl.pallas_call(own_kernel, out_shape=[piece] * 2, in_specs=[ANY, ANY], ou...]
    ppermute x6, waiting for transfers between devices: 17.5 us -> 19.5 us  [along_x(): lax.ppermute(x, 'ctx', [(c, (c + 2 * step) % cycle) for c in range(cycle)])]
    ppermute x2, waiting for transfers between devices: 1.82 us -> 0.01 us  [along_z(): return lax.ppermute(x, 'ctx', [(c, c ^ 1) for c in range(cycle)])]
    select_n x0 -> x1, other arithmetic: none -> 1.36 us  [body(): jnp.where(group % 2 == 0, lax.dynamic_slice_in_dim(keys, head * DH, DH, 1...]
    all_to_all x1, blocking collectives: 37.1 us -> 38.3 us  [body(): lax.all_to_all(outgoing.reshape(devices, SLOT, heads * DH), ('ctx', 'rows...]
    ppermute x4, starting transfers between devices: 7.21 us -> 6.06 us  [swap(): return lax.ppermute(x, 'rows', [(r, r ^ 1) for r in range(groups)])]
  transfers between devices with their start and end apart: 12 -> 12, of which waited for: 6 -> 4; matrix products, arithmetic and copies ran while one was open for 4% -> 4% of each run, Pallas kernels for 3% -> 2%
where the time goes in v9:
time: 113 us
  blocking collectives  38.3 us (34%)
  Pallas kernels  29.7 us (26%)
  waiting for transfers between devices  21.1 us (19%)
  starting transfers between devices  17.3 us (15%)
  other arithmetic  5.59 us (5%)
    all_to_all x1, blocking collectives, body(): lax.all_to_all(outgoing.reshape(devices, SLOT, heads * DH), ('ctx', 'rows...  38.3 us
    pallas_call x1, Pallas kernels, body(): pl.pallas_call(functools.partial(attend_kernel, [x.shape[0] for x in mine...  25.7 us
    ppermute x6, waiting for transfers between devices, along_x(): lax.ppermute(x, 'ctx', [(c, (c + 2 * step) % cycle) for c in range(cycle)])  19.5 us
    ppermute x6, starting transfers between devices, along_x(): lax.ppermute(x, 'ctx', [(c, (c + 2 * step) % cycle) for c in range(cycle)])  8.34 us
    ppermute x4, starting transfers between devices, swap(): return lax.ppermute(x, 'rows', [(r, r ^ 1) for r in range(groups)])  6.06 us
    ppermute x2, starting transfers between devices, along_z(): return lax.ppermute(x, 'ctx', [(c, c ^ 1) for c in range(cycle)])  2.95 us
  transfers between devices with their start and end apart: 12, of which 4 were waited for; matrix products, arithmetic and copies ran while one was open for 4% of the time, Pallas kernels for 2%

profile of v9, /device:TPU:1, one launch (start us, length us, event | category | flops | bytes accessed | tf_op | source)
XLA Modules:
  0.0 112.7 jit_solution(2999867493450548843)
XLA Ops:
  0.0 0.0 copy-start.3
  0.0 0.0 copy-start.4
  0.0 0.0 copy-start.5
  0.0 1.4 %dynamic-slice_select_fusion.block_ref = bf16[2048,128]{1,0:T(8,128)(2,1)S(1)} fusion(bf16[2048,1024]{1,0:T(8,128)(2,1)} %values, s32[]{:T(128)S(6)} %select_n.145, bf16[2048,1024]{1,0:T(8,128)(2,1)} %keys, pred[]{:T(512)S(6)} %eq.100), kind=kLoop, calls=%fused_computation.4 | loop fusion | flops 262144 | bytes 1572869 | tf_op jit(solution)/shard_map/jit(_where)/select_n | solution.py:272
  1.4 0.2 turn.1
  1.6 2.5 %collective-permute-start.2 = (bf16[2048,128]{1,0:T(8,128)(2,1)S(1)}, bf16[2048,128]{1,0:T(8,128)(2,1)S(1)}, u32[]{:S(2)}, u32[]{:S(2)}) collective-permute-start(bf16[2048,128]{1,0:T(8,128)(2,1)S(1)} %turn.1), channel_id=1, source_target_pairs={{0,16},{16,0},{32,48},{48,32},{64,80},{80,64},{96,112},{112,96},{1... | collective-permute-start | bytes 1572872 | tf_op jit(solution)/shard_map/ppermute | solution.py:283
  4.2 1.2 %collective-permute-start = (bf16[2048,128]{1,0:T(8,128)(2,1)S(1)}, bf16[2048,128]{1,0:T(8,128)(2,1)S(1)}, u32[]{:S(2)}, u32[]{:S(2)}) collective-permute-start(bf16[2048,128]{1,0:T(8,128)(2,1)S(1)} %turn.1), channel_id=1, source_target_pairs={{0,32},{16,48},{32,64},{48,80},{64,96},{80,112},{96,0},{112,16},{1... | collective-permute-start | bytes 1572872 | tf_op jit(solution)/shard_map/ppermute | solution.py:280
  5.4 0.0 copy-done.3
  5.4 1.2 %select_reduce_fusion.1 = (s32[128]{0:T(128)S(1)}, s32[128]{0:T(128)S(1)}) fusion(s32[2048]{0:T(1024)S(1)} %copy-done.3, s32[2048]{0:T(1024)S(1)} %add_select_fusion.5), kind=kLoop, calls=%fused_computation.1 | loop fusion | flops 1310464 | bytes 17408 | tf_op jit(solution)/shard_map/reduce_min | solution.py:291
  6.6 1.5 %collective-permute-start.1 = (bf16[2048,128]{1,0:T(8,128)(2,1)S(1)}, bf16[2048,128]{1,0:T(8,128)(2,1)S(1)}, u32[]{:S(2)}, u32[]{:S(2)}) collective-permute-start(bf16[2048,128]{1,0:T(8,128)(2,1)S(1)} %turn.1), channel_id=1, source_target_pairs={{0,96},{16,112},{32,0},{48,16},{64,32},{80,48},{96,64},{112,80},{1... | collective-permute-start | bytes 1572872 | tf_op jit(solution)/shard_map/ppermute | solution.py:280
  8.1 0.1 select_reduce_fusion.3.start
  8.3 0.0 copy-done.4
  8.3 0.1 broadcast_subtract_fusion
  8.4 0.0 copy-done.5
  8.4 0.1 pad_add_fusion
  8.4 0.8 and_reduce_fusion
  9.2 0.2 convert_reduce_fusion.2
  9.4 0.6 select_reduce_fusion
  10.1 0.1 reshape.230.counts
  10.2 2.2 %own.1 = (bf16[2048,128]{1,0:T(8,128)(2,1)}, bf16[2048,128]{1,0:T(8,128)(2,1)}) custom-call(bf16[2048,1024]{1,0:T(8,128)(2,1)} %keys, bf16[2048,1024]{1,0:T(8,128)(2,1)} %values), custom_call_target="tpu_custom_call" | custom-call | tf_op jit(solution)/shard_map/own/pallas_call | solution.py:300
  12.4 0.6 convert_reduce_fusion.1
  13.0 0.5 select_reduce_fusion.2
  13.5 4.3 %collective-permute-done = bf16[2048,128]{1,0:T(8,128)(2,1)S(1)} collective-permute-done((bf16[2048,128]{1,0:T(8,128)(2,1)S(1)}, bf16[2048,128]{1,0:T(8,128)(2,1)S(1)}, u32[]{:S(2)}, u32[]{:S(2)}) %collective-permute-start) | collective-permute-done | bytes 524320 | tf_op jit(solution)/shard_map/ppermute | solution.py:280
  17.8 0.4 collective-permute-start.5
  18.2 0.0 collective-permute-start.3
  18.3 0.0 collective-permute-done.2
  18.3 2.7 %collective-permute-start.4 = (bf16[2048,128]{1,0:T(8,128)(2,1)S(1)}, bf16[2048,128]{1,0:T(8,128)(2,1)S(1)}, u32[]{:S(2)}, u32[]{:S(2)}) collective-permute-start(bf16[2048,128]{1,0:T(8,128)(2,1)S(1)} %collective-permute-done.2), channel_id=1, source_target_pairs={{0,96},{16,112},{32,0},{48,16},{64,32},{80,48},{96,64},{112,80},{1... | collective-permute-start | bytes 1572872 | tf_op jit(solution)/shard_map/ppermute | solution.py:280
  21.0 0.0 collective-permute-done.1
  21.0 0.1 constant_dynamic-update-slice_fusion.1
  21.1 0.1 constant_dynamic-update-slice_fusion.rest_2_
  21.2 2.5 %collective-permute-start.8 = (bf16[6144,128]{1,0:T(8,128)(2,1)S(1)}, bf16[6144,128]{1,0:T(8,128)(2,1)S(1)}, u32[]{:S(2)}, u32[]{:S(2)}) collective-permute-start(bf16[6144,128]{1,0:T(8,128)(2,1)S(1)} %constant_dynamic-update-slice_fusion.rest_2_), channel_id=1, source_target_pairs={{0,1},{1,0},{2,3},{3,2},{4,5},{5,4},{6,7},{7,6},{8,9},{9,8},{10,11... | collective-permute-start | bytes 4718600 | tf_op jit(solution)/shard_map/ppermute | solution.py:286
  23.7 7.4 %collective-permute-done.3 = bf16[2048,128]{1,0:T(8,128)(2,1)S(1)} collective-permute-done((bf16[2048,128]{1,0:T(8,128)(2,1)S(1)}, bf16[2048,128]{1,0:T(8,128)(2,1)S(1)}, u32[]{:S(2)}, u32[]{:S(2)}) %collective-permute-start.3) | collective-permute-done | bytes 524320 | tf_op jit(solution)/shard_map/ppermute | solution.py:280
  31.1 0.0 copy-start
  31.1 0.0 copy-start.1
  31.1 0.0 copy-start.2
  31.1 0.0 collective-permute-done.4
  31.1 0.1 constant_dynamic-update-slice_fusion.4
  31.2 0.0 collective-permute-done.5
  31.2 0.1 constant_dynamic-update-slice_fusion.3.rest_3_
  31.3 2.8 %collective-permute-start.9 = (bf16[6144,128]{1,0:T(8,128)(2,1)S(1)}, bf16[6144,128]{1,0:T(8,128)(2,1)S(1)}, u32[]{:S(2)}, u32[]{:S(2)}) collective-permute-start(bf16[6144,128]{1,0:T(8,128)(2,1)S(1)} %constant_dynamic-update-slice_fusion.3.rest_3_), channel_id=1, source_target_pairs={{0,1},{1,0},{2,3},{3,2},{4,5},{5,4},{6,7},{7,6},{8,9},{9,8},{10,11... | collective-permute-start | bytes 4718600 | tf_op jit(solution)/shard_map/ppermute | solution.py:286
  34.1 0.1 collective-permute-start.6
  34.2 2.8 %collective-permute-start.7 = (bf16[768,128]{1,0:T(8,128)(2,1)S(1)}, bf16[768,128]{1,0:T(8,128)(2,1)S(1)}, u32[]{:S(2)}, u32[]{:S(2)}) collective-permute-start(bf16[768,128]{1,0:T(8,128)(2,1)S(1)} %slice.9), channel_id=1, source_target_pairs={{0,96},{16,112},{32,0},{48,16},{64,32},{80,48},{96,64},{112,80},{1... | collective-permute-start | bytes 589832 | tf_op jit(solution)/shard_map/ppermute | solution.py:280
  37.0 7.8 %collective-permute-done.6.rest_4_ = bf16[1280,128]{1,0:T(8,128)(2,1)S(1)} collective-permute-done((bf16[1280,128]{1,0:T(8,128)(2,1)S(1)}, bf16[1280,128]{1,0:T(8,128)(2,1)S(1)}, u32[]{:S(2)}, u32[]{:S(2)}) %collective-permute-start.6) | collective-permute-done | bytes 327712 | tf_op jit(solution)/shard_map/ppermute | solution.py:280
  44.8 0.8 collective-permute-start.10
  45.6 0.0 collective-permute-done.7.rest_5_
  45.6 0.0 collective-permute-start.11
  45.6 1.5 %collective-permute-done.11.rest_9_ = bf16[768,128]{1,0:T(8,128)(2,1)S(1)} collective-permute-done((bf16[768,128]{1,0:T(8,128)(2,1)S(1)}, bf16[768,128]{1,0:T(8,128)(2,1)S(1)}, u32[]{:S(2)}, u32[]{:S(2)}) %collective-permute-start.11) | collective-permute-done | bytes 196640 | tf_op jit(solution)/shard_map/ppermute | solution.py:286
  47.1 0.0 collective-permute-done.10.rest_8_
  47.1 0.0 collective-permute-done.8.rest_6_
  47.1 0.0 collective-permute-done.9.rest_7_
  47.1 0.0 copy-done
  47.1 0.0 copy-done.1
  47.2 0.0 copy-done.2
  47.2 25.7 %attend.1 = bf16[4096,256]{1,0:T(8,128)(2,1)S(1)} custom-call(s32[32,24]{1,0:T(8,128)S(1)} %bitcast.6, s32[32]{0:T(128)S(1)} %reshape.230.counts, s32[128]{0:T(128)S(1)} %get-tuple-element.26.sent, s32[128]{0:T(128)S(1)} %select_reduce_fusion.3.start, bf16[2048,256]{1,0:T(8,128)(2,1)S(1)} %copy-done, s32[1,2048]{1,0:T(1,128)S(1)} %bitcast.7, ...), custom_call_target="tpu_custom_call" | custom-call | tf_op jit(solution)/shard_map/attend/pallas_call | solution.py:325
  72.9 38.3 %all_to_all.5 = bf16[128,32,256]{2,1,0:T(8,128)(2,1)S(1)} all-to-all(bf16[128,32,256]{2,1,0:T(8,128)(2,1)S(1)} %bitcast.5), channel_id=1, replica_groups=mesh['ctx'=8,'rows'=16] {'ctx','rows'}, dimensions={0} | all-to-all | bytes 4194304 | tf_op jit(solution)/shard_map/all_to_all | solution.py:342
  111.1 1.6 %arrange.1 = bf16[128,4096]{1,0:T(8,128)(2,1)} custom-call(bf16[8,16,32,256]{3,2,1,0:T(8,128)(2,1)S(1)} %bitcast.4), custom_call_target="tpu_custom_call" | custom-call | tf_op jit(solution)/shard_map/arrange/pallas_call | solution.py:346
  (10 shorter events, 0.1 us)
Async XLA Ops:
  0.0 5.4 %copy-start.3 = (s32[2048]{0:T(1024)S(1)}, s32[2048]{0:T(1024)}, u32[]{:S(2)}) copy-start(s32[2048]{0:T(1024)} %param.11) | copy-start | bytes 24580
  0.0 8.3 %copy-start.4 = (s32[2,16]{1,0:T(2,128)S(1)}, s32[2,16]{1,0:T(2,128)}, u32[]{:S(2)}) copy-start(s32[2,16]{1,0:T(2,128)} %param.10) | copy-start | bytes 388
  0.0 8.3 %copy-start.5 = (s32[2,8]{1,0:T(2,128)S(1)}, s32[2,8]{1,0:T(2,128)}, u32[]{:S(2)}) copy-start(s32[2,8]{1,0:T(2,128)} %param.9) | copy-start | bytes 196
  1.6 16.7 %collective-permute-start.2 = (bf16[2048,128]{1,0:T(8,128)(2,1)S(1)}, bf16[2048,128]{1,0:T(8,128)(2,1)S(1)}, u32[]{:S(2)}, u32[]{:S(2)}) collective-permute-start(bf16[2048,128]{1,0:T(8,128)(2,1)S(1)} %turn.1), channel_id=1, source_target_pairs={{0,16},{16,0},{32,48},{48,32},{64,80},{80,64},{96,112},{112,96},{1... | collective-permute-start | bytes 1572872 | tf_op jit(solution)/shard_map/ppermute | solution.py:283
  4.2 13.7 %collective-permute-start = (bf16[2048,128]{1,0:T(8,128)(2,1)S(1)}, bf16[2048,128]{1,0:T(8,128)(2,1)S(1)}, u32[]{:S(2)}, u32[]{:S(2)}) collective-permute-start(bf16[2048,128]{1,0:T(8,128)(2,1)S(1)} %turn.1), channel_id=1, source_target_pairs={{0,32},{16,48},{32,64},{48,80},{64,96},{80,112},{96,0},{112,16},{1... | collective-permute-start | bytes 1572872 | tf_op jit(solution)/shard_map/ppermute | solution.py:280
  6.6 14.4 %collective-permute-start.1 = (bf16[2048,128]{1,0:T(8,128)(2,1)S(1)}, bf16[2048,128]{1,0:T(8,128)(2,1)S(1)}, u32[]{:S(2)}, u32[]{:S(2)}) collective-permute-start(bf16[2048,128]{1,0:T(8,128)(2,1)S(1)} %turn.1), channel_id=1, source_target_pairs={{0,96},{16,112},{32,0},{48,16},{64,32},{80,48},{96,64},{112,80},{1... | collective-permute-start | bytes 1572872 | tf_op jit(solution)/shard_map/ppermute | solution.py:280
  17.8 13.4 %collective-permute-start.5 = (bf16[2048,128]{1,0:T(8,128)(2,1)S(1)}, bf16[2048,128]{1,0:T(8,128)(2,1)S(1)}, u32[]{:S(2)}, u32[]{:S(2)}) collective-permute-start(bf16[2048,128]{1,0:T(8,128)(2,1)S(1)} %collective-permute-done), channel_id=1, source_target_pairs={{0,16},{16,0},{32,48},{48,32},{64,80},{80,64},{96,112},{112,96},{1... | collective-permute-start | bytes 1572872 | tf_op jit(solution)/shard_map/ppermute | solution.py:283
  18.2 12.8 %collective-permute-start.3 = (bf16[2048,128]{1,0:T(8,128)(2,1)S(1)}, bf16[2048,128]{1,0:T(8,128)(2,1)S(1)}, u32[]{:S(2)}, u32[]{:S(2)}) collective-permute-start(bf16[2048,128]{1,0:T(8,128)(2,1)S(1)} %collective-permute-done), channel_id=1, source_target_pairs={{0,32},{16,48},{32,64},{48,80},{64,96},{80,112},{96,0},{112,16},{1... | collective-permute-start | bytes 1572872 | tf_op jit(solution)/shard_map/ppermute | solution.py:280
  18.3 12.8 %collective-permute-start.4 = (bf16[2048,128]{1,0:T(8,128)(2,1)S(1)}, bf16[2048,128]{1,0:T(8,128)(2,1)S(1)}, u32[]{:S(2)}, u32[]{:S(2)}) collective-permute-start(bf16[2048,128]{1,0:T(8,128)(2,1)S(1)} %collective-permute-done.2), channel_id=1, source_target_pairs={{0,96},{16,112},{32,0},{48,16},{64,32},{80,48},{96,64},{112,80},{1... | collective-permute-start | bytes 1572872 | tf_op jit(solution)/shard_map/ppermute | solution.py:280
  21.2 25.9 %collective-permute-start.8 = (bf16[6144,128]{1,0:T(8,128)(2,1)S(1)}, bf16[6144,128]{1,0:T(8,128)(2,1)S(1)}, u32[]{:S(2)}, u32[]{:S(2)}) collective-permute-start(bf16[6144,128]{1,0:T(8,128)(2,1)S(1)} %constant_dynamic-update-slice_fusion.rest_2_), channel_id=1, source_target_pairs={{0,1},{1,0},{2,3},{3,2},{4,5},{5,4},{6,7},{7,6},{8,9},{9,8},{10,11... | collective-permute-start | bytes 4718600 | tf_op jit(solution)/shard_map/ppermute | solution.py:286
  31.1 16.1 %copy-start = (bf16[2048,256]{1,0:T(8,128)(2,1)S(1)}, bf16[2048,256]{1,0:T(8,128)(2,1)}, u32[]{:S(2)}) copy-start(bf16[2048,256]{1,0:T(8,128)(2,1)} %q_ref.1) | copy-start | bytes 3145732
  31.1 16.1 %copy-start.1 = (bf16[2048,128]{1,0:T(8,128)(2,1)S(1)}, bf16[2048,128]{1,0:T(8,128)(2,1)}, u32[]{:S(2)}) copy-start(bf16[2048,128]{1,0:T(8,128)(2,1)} %get-tuple-element.29.rest_0_) | copy-start | bytes 1572868
  31.1 16.1 %copy-start.2 = (bf16[2048,128]{1,0:T(8,128)(2,1)S(1)}, bf16[2048,128]{1,0:T(8,128)(2,1)}, u32[]{:S(2)}) copy-start(bf16[2048,128]{1,0:T(8,128)(2,1)} %get-tuple-element.30.rest_1_) | copy-start | bytes 1572868
  31.3 15.8 %collective-permute-start.9 = (bf16[6144,128]{1,0:T(8,128)(2,1)S(1)}, bf16[6144,128]{1,0:T(8,128)(2,1)S(1)}, u32[]{:S(2)}, u32[]{:S(2)}) collective-permute-start(bf16[6144,128]{1,0:T(8,128)(2,1)S(1)} %constant_dynamic-update-slice_fusion.3.rest_3_), channel_id=1, source_target_pairs={{0,1},{1,0},{2,3},{3,2},{4,5},{5,4},{6,7},{7,6},{8,9},{9,8},{10,11... | collective-permute-start | bytes 4718600 | tf_op jit(solution)/shard_map/ppermute | solution.py:286
  34.1 10.7 %collective-permute-start.6 = (bf16[1280,128]{1,0:T(8,128)(2,1)S(1)}, bf16[1280,128]{1,0:T(8,128)(2,1)S(1)}, u32[]{:S(2)}, u32[]{:S(2)}) collective-permute-start(bf16[1280,128]{1,0:T(8,128)(2,1)S(1)} %slice.8), channel_id=1, source_target_pairs={{0,32},{16,48},{32,64},{48,80},{64,96},{80,112},{96,0},{112,16},{1... | collective-permute-start | bytes 983048 | tf_op jit(solution)/shard_map/ppermute | solution.py:280
  34.2 11.3 %collective-permute-start.7 = (bf16[768,128]{1,0:T(8,128)(2,1)S(1)}, bf16[768,128]{1,0:T(8,128)(2,1)S(1)}, u32[]{:S(2)}, u32[]{:S(2)}) collective-permute-start(bf16[768,128]{1,0:T(8,128)(2,1)S(1)} %slice.9), channel_id=1, source_target_pairs={{0,96},{16,112},{32,0},{48,16},{64,32},{80,48},{96,64},{112,80},{1... | collective-permute-start | bytes 589832 | tf_op jit(solution)/shard_map/ppermute | solution.py:280
  44.8 2.3 %collective-permute-start.10 = (bf16[1280,128]{1,0:T(8,128)(2,1)S(1)}, bf16[1280,128]{1,0:T(8,128)(2,1)S(1)}, u32[]{:S(2)}, u32[]{:S(2)}) collective-permute-start(bf16[1280,128]{1,0:T(8,128)(2,1)S(1)} %collective-permute-done.6.rest_4_), channel_id=1, source_target_pairs={{0,1},{1,0},{2,3},{3,2},{4,5},{5,4},{6,7},{7,6},{8,9},{9,8},{10,11... | collective-permute-start | bytes 983048 | tf_op jit(solution)/shard_map/ppermute | solution.py:286
  45.6 1.5 %collective-permute-start.11 = (bf16[768,128]{1,0:T(8,128)(2,1)S(1)}, bf16[768,128]{1,0:T(8,128)(2,1)S(1)}, u32[]{:S(2)}, u32[]{:S(2)}) collective-permute-start(bf16[768,128]{1,0:T(8,128)(2,1)S(1)} %collective-permute-done.7.rest_5_), channel_id=1, source_target_pairs={{0,1},{1,0},{2,3},{3,2},{4,5},{5,4},{6,7},{7,6},{8,9},{9,8},{10,11... | collective-permute-start | bytes 589832 | tf_op jit(solution)/shard_map/ppermute | solution.py:286

commit v10 on v9

--- a/solution.py
+++ b/solution.py
@@ -285,7 +285,7 @@
     def swap(x):
         return lax.ppermute(x, "rows", [(r, r ^ 1) for r in range(groups)])
 
-    cut = rows_here * 5 // 8
+    cut = rows_here // 2
     owner = destination // own_rows
     member = owner[:, None] == jnp.arange(devices, dtype=jnp.int32)[None, :]
     first_row = jnp.min(jnp.where(member, destination[:, None], ROW_CEILING), axis=0)
@@ -335,7 +335,7 @@
             pltpu.VMEM((rows_here + SLOT + 8, heads * DH), jnp.float32),
             pltpu.SemaphoreType.DMA((2 + 2 * len(mine),)),
         ],
-        compiler_params=pltpu.CompilerParams(vmem_limit_bytes=28 * 1024 * 1024),
+        compiler_params=pltpu.CompilerParams(vmem_limit_bytes=32 * 1024 * 1024),
         name="attend",
     )(lists, counts, sent, start, queries, rank, *here, *mine, *other)
 

time: 113 us -> 112 us (level)
  starting transfers between devices: 17.3 us -> 18.5 us
  blocking collectives: 38.3 us -> 37.1 us
    all_to_all x1, blocking collectives: 38.3 us -> 37.1 us  [body(): lax.all_to_all(outgoing.reshape(devices, SLOT, heads * DH), ('ctx', 'rows...]
    ppermute x4, starting transfers between devices: 6.06 us -> 7.21 us  [swap(): return lax.ppermute(x, 'rows', [(r, r ^ 1) for r in range(groups)])]
  transfers between devices with their start and end apart: 12 -> 12, of which waited for: 4 -> 5; matrix products, arithmetic and copies ran while one was open for 4% -> 4% of each run, Pallas kernels for 2% -> 2%
where the time goes in v10:
time: 112 us
  blocking collectives  37.1 us (33%)
  Pallas kernels  29 us (26%)
  waiting for transfers between devices  20.9 us (19%)
  starting transfers between devices  18.5 us (17%)
  other arithmetic  5.59 us (5%)
    all_to_all x1, blocking collectives, body(): lax.all_to_all(outgoing.reshape(devices, SLOT, heads * DH), ('ctx', 'rows...  37.1 us
    pallas_call x1, Pallas kernels, body(): pl.pallas_call(functools.partial(attend_kernel, [x.shape[0] for x in mine...  25.1 us
    ppermute x6, waiting for transfers between devices, along_x(): lax.ppermute(x, 'ctx', [(c, (c + 2 * step) % cycle) for c in range(cycle)])  19.7 us
    ppermute x6, starting transfers between devices, along_x(): lax.ppermute(x, 'ctx', [(c, (c + 2 * step) % cycle) for c in range(cycle)])  8.34 us
    ppermute x4, starting transfers between devices, swap(): return lax.ppermute(x, 'rows', [(r, r ^ 1) for r in range(groups)])  7.21 us
    ppermute x2, starting transfers between devices, along_z(): return lax.ppermute(x, 'ctx', [(c, c ^ 1) for c in range(cycle)])  2.95 us
  transfers between devices with their start and end apart: 12, of which 5 were waited for; matrix products, arithmetic and copies ran while one was open for 4% of the time, Pallas kernels for 2%

profile of v10, /device:TPU:1, one launch (start us, length us, event | category | flops | bytes accessed | tf_op | source)
XLA Modules:
  0.0 111.9 jit_solution(15933560126311135874)
XLA Ops:
  0.0 0.0 copy-start.3
  0.0 0.0 copy-start.4
  0.0 0.0 copy-start.5
  0.0 1.4 %dynamic-slice_select_fusion.block_ref = bf16[2048,128]{1,0:T(8,128)(2,1)S(1)} fusion(bf16[2048,1024]{1,0:T(8,128)(2,1)} %values, s32[]{:T(128)S(6)} %select_n.145, bf16[2048,1024]{1,0:T(8,128)(2,1)} %keys, pred[]{:T(512)S(6)} %eq.100), kind=kLoop, calls=%fused_computation.4 | loop fusion | flops 262144 | bytes 1572869 | tf_op jit(solution)/shard_map/jit(_where)/select_n | solution.py:272
  1.4 0.2 turn.1
  1.6 2.5 %collective-permute-start.2 = (bf16[2048,128]{1,0:T(8,128)(2,1)S(1)}, bf16[2048,128]{1,0:T(8,128)(2,1)S(1)}, u32[]{:S(2)}, u32[]{:S(2)}) collective-permute-start(bf16[2048,128]{1,0:T(8,128)(2,1)S(1)} %turn.1), channel_id=1, source_target_pairs={{0,16},{16,0},{32,48},{48,32},{64,80},{80,64},{96,112},{112,96},{1... | collective-permute-start | bytes 1572872 | tf_op jit(solution)/shard_map/ppermute | solution.py:283
  4.2 1.2 %collective-permute-start = (bf16[2048,128]{1,0:T(8,128)(2,1)S(1)}, bf16[2048,128]{1,0:T(8,128)(2,1)S(1)}, u32[]{:S(2)}, u32[]{:S(2)}) collective-permute-start(bf16[2048,128]{1,0:T(8,128)(2,1)S(1)} %turn.1), channel_id=1, source_target_pairs={{0,32},{16,48},{32,64},{48,80},{64,96},{80,112},{96,0},{112,16},{1... | collective-permute-start | bytes 1572872 | tf_op jit(solution)/shard_map/ppermute | solution.py:280
  5.4 0.0 copy-done.3
  5.4 1.2 %select_reduce_fusion.1 = (s32[128]{0:T(128)S(1)}, s32[128]{0:T(128)S(1)}) fusion(s32[2048]{0:T(1024)S(1)} %copy-done.3, s32[2048]{0:T(1024)S(1)} %add_select_fusion.5), kind=kLoop, calls=%fused_computation.1 | loop fusion | flops 1310464 | bytes 17408 | tf_op jit(solution)/shard_map/reduce_min | solution.py:291
  6.6 1.5 %collective-permute-start.1 = (bf16[2048,128]{1,0:T(8,128)(2,1)S(1)}, bf16[2048,128]{1,0:T(8,128)(2,1)S(1)}, u32[]{:S(2)}, u32[]{:S(2)}) collective-permute-start(bf16[2048,128]{1,0:T(8,128)(2,1)S(1)} %turn.1), channel_id=1, source_target_pairs={{0,96},{16,112},{32,0},{48,16},{64,32},{80,48},{96,64},{112,80},{1... | collective-permute-start | bytes 1572872 | tf_op jit(solution)/shard_map/ppermute | solution.py:280
  8.1 0.1 select_reduce_fusion.3.start
  8.3 0.0 copy-done.4
  8.3 0.1 broadcast_subtract_fusion
  8.4 0.0 copy-done.5
  8.4 0.1 pad_add_fusion
  8.4 0.8 and_reduce_fusion
  9.2 0.2 convert_reduce_fusion.2
  9.4 0.6 select_reduce_fusion
  10.1 0.1 reshape.230.counts
  10.2 2.2 %own.1 = (bf16[2048,128]{1,0:T(8,128)(2,1)}, bf16[2048,128]{1,0:T(8,128)(2,1)}) custom-call(bf16[2048,1024]{1,0:T(8,128)(2,1)} %keys, bf16[2048,1024]{1,0:T(8,128)(2,1)} %values), custom_call_target="tpu_custom_call" | custom-call | tf_op jit(solution)/shard_map/own/pallas_call | solution.py:300
  12.4 0.6 convert_reduce_fusion.1
  13.0 0.5 select_reduce_fusion.2
  13.5 4.3 %collective-permute-done = bf16[2048,128]{1,0:T(8,128)(2,1)S(1)} collective-permute-done((bf16[2048,128]{1,0:T(8,128)(2,1)S(1)}, bf16[2048,128]{1,0:T(8,128)(2,1)S(1)}, u32[]{:S(2)}, u32[]{:S(2)}) %collective-permute-start) | collective-permute-done | bytes 524320 | tf_op jit(solution)/shard_map/ppermute | solution.py:280
  17.8 0.4 collective-permute-start.5
  18.2 0.0 collective-permute-start.3
  18.3 0.0 collective-permute-done.2
  18.3 2.7 %collective-permute-start.4 = (bf16[2048,128]{1,0:T(8,128)(2,1)S(1)}, bf16[2048,128]{1,0:T(8,128)(2,1)S(1)}, u32[]{:S(2)}, u32[]{:S(2)}) collective-permute-start(bf16[2048,128]{1,0:T(8,128)(2,1)S(1)} %collective-permute-done.2), channel_id=1, source_target_pairs={{0,96},{16,112},{32,0},{48,16},{64,32},{80,48},{96,64},{112,80},{1... | collective-permute-start | bytes 1572872 | tf_op jit(solution)/shard_map/ppermute | solution.py:280
  21.0 0.0 collective-permute-done.1
  21.0 0.1 constant_dynamic-update-slice_fusion.1
  21.1 0.1 constant_dynamic-update-slice_fusion.rest_2_
  21.2 2.5 %collective-permute-start.8 = (bf16[6144,128]{1,0:T(8,128)(2,1)S(1)}, bf16[6144,128]{1,0:T(8,128)(2,1)S(1)}, u32[]{:S(2)}, u32[]{:S(2)}) collective-permute-start(bf16[6144,128]{1,0:T(8,128)(2,1)S(1)} %constant_dynamic-update-slice_fusion.rest_2_), channel_id=1, source_target_pairs={{0,1},{1,0},{2,3},{3,2},{4,5},{5,4},{6,7},{7,6},{8,9},{9,8},{10,11... | collective-permute-start | bytes 4718600 | tf_op jit(solution)/shard_map/ppermute | solution.py:286
  23.7 7.4 %collective-permute-done.3 = bf16[2048,128]{1,0:T(8,128)(2,1)S(1)} collective-permute-done((bf16[2048,128]{1,0:T(8,128)(2,1)S(1)}, bf16[2048,128]{1,0:T(8,128)(2,1)S(1)}, u32[]{:S(2)}, u32[]{:S(2)}) %collective-permute-start.3) | collective-permute-done | bytes 524320 | tf_op jit(solution)/shard_map/ppermute | solution.py:280
  31.1 0.0 copy-start
  31.1 0.0 copy-start.1
  31.1 0.0 copy-start.2
  31.1 0.0 collective-permute-done.4
  31.1 0.1 constant_dynamic-update-slice_fusion.4
  31.2 0.0 collective-permute-done.5
  31.2 0.1 constant_dynamic-update-slice_fusion.3.rest_3_
  31.3 2.8 %collective-permute-start.9 = (bf16[6144,128]{1,0:T(8,128)(2,1)S(1)}, bf16[6144,128]{1,0:T(8,128)(2,1)S(1)}, u32[]{:S(2)}, u32[]{:S(2)}) collective-permute-start(bf16[6144,128]{1,0:T(8,128)(2,1)S(1)} %constant_dynamic-update-slice_fusion.3.rest_3_), channel_id=1, source_target_pairs={{0,1},{1,0},{2,3},{3,2},{4,5},{5,4},{6,7},{7,6},{8,9},{9,8},{10,11... | collective-permute-start | bytes 4718600 | tf_op jit(solution)/shard_map/ppermute | solution.py:286
  34.1 2.8 %collective-permute-start.7 = (bf16[1024,128]{1,0:T(8,128)(2,1)S(1)}, bf16[1024,128]{1,0:T(8,128)(2,1)S(1)}, u32[]{:S(2)}, u32[]{:S(2)}) collective-permute-start(bf16[1024,128]{1,0:T(8,128)(2,1)S(1)} %slice.9), channel_id=1, source_target_pairs={{0,96},{16,112},{32,0},{48,16},{64,32},{80,48},{96,64},{112,80},{1... | collective-permute-start | bytes 786440 | tf_op jit(solution)/shard_map/ppermute | solution.py:280
  36.9 0.1 collective-permute-start.6
  37.0 5.6 %collective-permute-done.7.rest_5_ = bf16[1024,128]{1,0:T(8,128)(2,1)S(1)} collective-permute-done((bf16[1024,128]{1,0:T(8,128)(2,1)S(1)}, bf16[1024,128]{1,0:T(8,128)(2,1)S(1)}, u32[]{:S(2)}, u32[]{:S(2)}) %collective-permute-start.7) | collective-permute-done | bytes 262176 | tf_op jit(solution)/shard_map/ppermute | solution.py:280
  42.6 0.8 collective-permute-start.11
  43.4 2.4 %collective-permute-done.6.rest_4_ = bf16[1024,128]{1,0:T(8,128)(2,1)S(1)} collective-permute-done((bf16[1024,128]{1,0:T(8,128)(2,1)S(1)}, bf16[1024,128]{1,0:T(8,128)(2,1)S(1)}, u32[]{:S(2)}, u32[]{:S(2)}) %collective-permute-start.6) | collective-permute-done | bytes 262176 | tf_op jit(solution)/shard_map/ppermute | solution.py:280
  45.8 1.1 %collective-permute-start.10 = (bf16[1024,128]{1,0:T(8,128)(2,1)S(1)}, bf16[1024,128]{1,0:T(8,128)(2,1)S(1)}, u32[]{:S(2)}, u32[]{:S(2)}) collective-permute-start(bf16[1024,128]{1,0:T(8,128)(2,1)S(1)} %collective-permute-done.6.rest_4_), channel_id=1, source_target_pairs={{0,1},{1,0},{2,3},{3,2},{4,5},{5,4},{6,7},{7,6},{8,9},{9,8},{10,11... | collective-permute-start | bytes 786440 | tf_op jit(solution)/shard_map/ppermute | solution.py:286
  46.9 0.0 collective-permute-done.11.rest_9_
  46.9 1.2 %collective-permute-done.10.rest_8_ = bf16[1024,128]{1,0:T(8,128)(2,1)S(1)} collective-permute-done((bf16[1024,128]{1,0:T(8,128)(2,1)S(1)}, bf16[1024,128]{1,0:T(8,128)(2,1)S(1)}, u32[]{:S(2)}, u32[]{:S(2)}) %collective-permute-start.10) | collective-permute-done | bytes 262176 | tf_op jit(solution)/shard_map/ppermute | solution.py:286
  48.1 0.0 collective-permute-done.8.rest_6_
  48.1 0.0 collective-permute-done.9.rest_7_
  48.1 0.0 copy-done
  48.1 0.0 copy-done.1
  48.1 0.0 copy-done.2
  48.1 25.1 %attend.1 = bf16[4096,256]{1,0:T(8,128)(2,1)S(1)} custom-call(s32[32,24]{1,0:T(8,128)S(1)} %bitcast.6, s32[32]{0:T(128)S(1)} %reshape.230.counts, s32[128]{0:T(128)S(1)} %get-tuple-element.26.sent, s32[128]{0:T(128)S(1)} %select_reduce_fusion.3.start, bf16[2048,256]{1,0:T(8,128)(2,1)S(1)} %copy-done, s32[1,2048]{1,0:T(1,128)S(1)} %bitcast.7, ...), custom_call_target="tpu_custom_call" | custom-call | tf_op jit(solution)/shard_map/attend/pallas_call | solution.py:325
  73.2 37.1 %all_to_all.5 = bf16[128,32,256]{2,1,0:T(8,128)(2,1)S(1)} all-to-all(bf16[128,32,256]{2,1,0:T(8,128)(2,1)S(1)} %bitcast.5), channel_id=1, replica_groups=mesh['ctx'=8,'rows'=16] {'ctx','rows'}, dimensions={0} | all-to-all | bytes 4194304 | tf_op jit(solution)/shard_map/all_to_all | solution.py:342
  110.3 1.6 %arrange.1 = bf16[128,4096]{1,0:T(8,128)(2,1)} custom-call(bf16[8,16,32,256]{3,2,1,0:T(8,128)(2,1)S(1)} %bitcast.4), custom_call_target="tpu_custom_call" | custom-call | tf_op jit(solution)/shard_map/arrange/pallas_call | solution.py:346
  (10 shorter events, 0.1 us)
Async XLA Ops:
  0.0 5.4 %copy-start.3 = (s32[2048]{0:T(1024)S(1)}, s32[2048]{0:T(1024)}, u32[]{:S(2)}) copy-start(s32[2048]{0:T(1024)} %param.11) | copy-start | bytes 24580
  0.0 8.3 %copy-start.4 = (s32[2,16]{1,0:T(2,128)S(1)}, s32[2,16]{1,0:T(2,128)}, u32[]{:S(2)}) copy-start(s32[2,16]{1,0:T(2,128)} %param.10) | copy-start | bytes 388
  0.0 8.3 %copy-start.5 = (s32[2,8]{1,0:T(2,128)S(1)}, s32[2,8]{1,0:T(2,128)}, u32[]{:S(2)}) copy-start(s32[2,8]{1,0:T(2,128)} %param.9) | copy-start | bytes 196
  1.6 16.7 %collective-permute-start.2 = (bf16[2048,128]{1,0:T(8,128)(2,1)S(1)}, bf16[2048,128]{1,0:T(8,128)(2,1)S(1)}, u32[]{:S(2)}, u32[]{:S(2)}) collective-permute-start(bf16[2048,128]{1,0:T(8,128)(2,1)S(1)} %turn.1), channel_id=1, source_target_pairs={{0,16},{16,0},{32,48},{48,32},{64,80},{80,64},{96,112},{112,96},{1... | collective-permute-start | bytes 1572872 | tf_op jit(solution)/shard_map/ppermute | solution.py:283
  4.2 13.7 %collective-permute-start = (bf16[2048,128]{1,0:T(8,128)(2,1)S(1)}, bf16[2048,128]{1,0:T(8,128)(2,1)S(1)}, u32[]{:S(2)}, u32[]{:S(2)}) collective-permute-start(bf16[2048,128]{1,0:T(8,128)(2,1)S(1)} %turn.1), channel_id=1, source_target_pairs={{0,32},{16,48},{32,64},{48,80},{64,96},{80,112},{96,0},{112,16},{1... | collective-permute-start | bytes 1572872 | tf_op jit(solution)/shard_map/ppermute | solution.py:280
  6.6 14.4 %collective-permute-start.1 = (bf16[2048,128]{1,0:T(8,128)(2,1)S(1)}, bf16[2048,128]{1,0:T(8,128)(2,1)S(1)}, u32[]{:S(2)}, u32[]{:S(2)}) collective-permute-start(bf16[2048,128]{1,0:T(8,128)(2,1)S(1)} %turn.1), channel_id=1, source_target_pairs={{0,96},{16,112},{32,0},{48,16},{64,32},{80,48},{96,64},{112,80},{1... | collective-permute-start | bytes 1572872 | tf_op jit(solution)/shard_map/ppermute | solution.py:280
  17.8 13.4 %collective-permute-start.5 = (bf16[2048,128]{1,0:T(8,128)(2,1)S(1)}, bf16[2048,128]{1,0:T(8,128)(2,1)S(1)}, u32[]{:S(2)}, u32[]{:S(2)}) collective-permute-start(bf16[2048,128]{1,0:T(8,128)(2,1)S(1)} %collective-permute-done), channel_id=1, source_target_pairs={{0,16},{16,0},{32,48},{48,32},{64,80},{80,64},{96,112},{112,96},{1... | collective-permute-start | bytes 1572872 | tf_op jit(solution)/shard_map/ppermute | solution.py:283
  18.2 12.8 %collective-permute-start.3 = (bf16[2048,128]{1,0:T(8,128)(2,1)S(1)}, bf16[2048,128]{1,0:T(8,128)(2,1)S(1)}, u32[]{:S(2)}, u32[]{:S(2)}) collective-permute-start(bf16[2048,128]{1,0:T(8,128)(2,1)S(1)} %collective-permute-done), channel_id=1, source_target_pairs={{0,32},{16,48},{32,64},{48,80},{64,96},{80,112},{96,0},{112,16},{1... | collective-permute-start | bytes 1572872 | tf_op jit(solution)/shard_map/ppermute | solution.py:280
  18.3 12.8 %collective-permute-start.4 = (bf16[2048,128]{1,0:T(8,128)(2,1)S(1)}, bf16[2048,128]{1,0:T(8,128)(2,1)S(1)}, u32[]{:S(2)}, u32[]{:S(2)}) collective-permute-start(bf16[2048,128]{1,0:T(8,128)(2,1)S(1)} %collective-permute-done.2), channel_id=1, source_target_pairs={{0,96},{16,112},{32,0},{48,16},{64,32},{80,48},{96,64},{112,80},{1... | collective-permute-start | bytes 1572872 | tf_op jit(solution)/shard_map/ppermute | solution.py:280
  21.2 26.9 %collective-permute-start.8 = (bf16[6144,128]{1,0:T(8,128)(2,1)S(1)}, bf16[6144,128]{1,0:T(8,128)(2,1)S(1)}, u32[]{:S(2)}, u32[]{:S(2)}) collective-permute-start(bf16[6144,128]{1,0:T(8,128)(2,1)S(1)} %constant_dynamic-update-slice_fusion.rest_2_), channel_id=1, source_target_pairs={{0,1},{1,0},{2,3},{3,2},{4,5},{5,4},{6,7},{7,6},{8,9},{9,8},{10,11... | collective-permute-start | bytes 4718600 | tf_op jit(solution)/shard_map/ppermute | solution.py:286
  31.1 17.0 %copy-start = (bf16[2048,256]{1,0:T(8,128)(2,1)S(1)}, bf16[2048,256]{1,0:T(8,128)(2,1)}, u32[]{:S(2)}) copy-start(bf16[2048,256]{1,0:T(8,128)(2,1)} %q_ref.1) | copy-start | bytes 3145732
  31.1 17.0 %copy-start.1 = (bf16[2048,128]{1,0:T(8,128)(2,1)S(1)}, bf16[2048,128]{1,0:T(8,128)(2,1)}, u32[]{:S(2)}) copy-start(bf16[2048,128]{1,0:T(8,128)(2,1)} %get-tuple-element.29.rest_0_) | copy-start | bytes 1572868
  31.1 17.0 %copy-start.2 = (bf16[2048,128]{1,0:T(8,128)(2,1)S(1)}, bf16[2048,128]{1,0:T(8,128)(2,1)}, u32[]{:S(2)}) copy-start(bf16[2048,128]{1,0:T(8,128)(2,1)} %get-tuple-element.30.rest_1_) | copy-start | bytes 1572868
  31.3 16.8 %collective-permute-start.9 = (bf16[6144,128]{1,0:T(8,128)(2,1)S(1)}, bf16[6144,128]{1,0:T(8,128)(2,1)S(1)}, u32[]{:S(2)}, u32[]{:S(2)}) collective-permute-start(bf16[6144,128]{1,0:T(8,128)(2,1)S(1)} %constant_dynamic-update-slice_fusion.3.rest_3_), channel_id=1, source_target_pairs={{0,1},{1,0},{2,3},{3,2},{4,5},{5,4},{6,7},{7,6},{8,9},{9,8},{10,11... | collective-permute-start | bytes 4718600 | tf_op jit(solution)/shard_map/ppermute | solution.py:286
  34.1 8.5 %collective-permute-start.7 = (bf16[1024,128]{1,0:T(8,128)(2,1)S(1)}, bf16[1024,128]{1,0:T(8,128)(2,1)S(1)}, u32[]{:S(2)}, u32[]{:S(2)}) collective-permute-start(bf16[1024,128]{1,0:T(8,128)(2,1)S(1)} %slice.9), channel_id=1, source_target_pairs={{0,96},{16,112},{32,0},{48,16},{64,32},{80,48},{96,64},{112,80},{1... | collective-permute-start | bytes 786440 | tf_op jit(solution)/shard_map/ppermute | solution.py:280
  36.9 8.9 %collective-permute-start.6 = (bf16[1024,128]{1,0:T(8,128)(2,1)S(1)}, bf16[1024,128]{1,0:T(8,128)(2,1)S(1)}, u32[]{:S(2)}, u32[]{:S(2)}) collective-permute-start(bf16[1024,128]{1,0:T(8,128)(2,1)S(1)} %slice.8), channel_id=1, source_target_pairs={{0,32},{16,48},{32,64},{48,80},{64,96},{80,112},{96,0},{112,16},{1... | collective-permute-start | bytes 786440 | tf_op jit(solution)/shard_map/ppermute | solution.py:280
  42.6 4.3 %collective-permute-start.11 = (bf16[1024,128]{1,0:T(8,128)(2,1)S(1)}, bf16[1024,128]{1,0:T(8,128)(2,1)S(1)}, u32[]{:S(2)}, u32[]{:S(2)}) collective-permute-start(bf16[1024,128]{1,0:T(8,128)(2,1)S(1)} %collective-permute-done.7.rest_5_), channel_id=1, source_target_pairs={{0,1},{1,0},{2,3},{3,2},{4,5},{5,4},{6,7},{7,6},{8,9},{9,8},{10,11... | collective-permute-start | bytes 786440 | tf_op jit(solution)/shard_map/ppermute | solution.py:286
  45.8 2.3 %collective-permute-start.10 = (bf16[1024,128]{1,0:T(8,128)(2,1)S(1)}, bf16[1024,128]{1,0:T(8,128)(2,1)S(1)}, u32[]{:S(2)}, u32[]{:S(2)}) collective-permute-start(bf16[1024,128]{1,0:T(8,128)(2,1)S(1)} %collective-permute-done.6.rest_4_), channel_id=1, source_target_pairs={{0,1},{1,0},{2,3},{3,2},{4,5},{5,4},{6,7},{7,6},{8,9},{9,8},{10,11... | collective-permute-start | bytes 786440 | tf_op jit(solution)/shard_map/ppermute | solution.py:286

commit v11 on v10

--- a/solution.py
+++ b/solution.py
@@ -285,7 +285,7 @@
     def swap(x):
         return lax.ppermute(x, "rows", [(r, r ^ 1) for r in range(groups)])
 
-    cut = rows_here // 2
+    cut = rows_here * 9 // 16
     owner = destination // own_rows
     member = owner[:, None] == jnp.arange(devices, dtype=jnp.int32)[None, :]
     first_row = jnp.min(jnp.where(member, destination[:, None], ROW_CEILING), axis=0)

time: 112 us -> 112 us (level)
  starting transfers between devices: 18.5 us -> 17.3 us
  blocking collectives: 37.1 us -> 38.3 us
    all_to_all x1, blocking collectives: 37.1 us -> 38.3 us  [body(): lax.all_to_all(outgoing.reshape(devices, SLOT, heads * DH), ('ctx', 'rows...]
    ppermute x4, starting transfers between devices: 7.21 us -> 6.06 us  [swap(): return lax.ppermute(x, 'rows', [(r, r ^ 1) for r in range(groups)])]
  transfers between devices with their start and end apart: 12 -> 12, of which waited for: 5 -> 4; matrix products, arithmetic and copies ran while one was open for 4% -> 4% of each run, Pallas kernels for 2% -> 2%
where the time goes in v11:
time: 112 us
  blocking collectives  38.3 us (34%)
  Pallas kernels  29.7 us (27%)
  waiting for transfers between devices  20.4 us (18%)
  starting transfers between devices  17.3 us (15%)
  other arithmetic  5.59 us (5%)
    all_to_all x1, blocking collectives, body(): lax.all_to_all(outgoing.reshape(devices, SLOT, heads * DH), ('ctx', 'rows...  38.3 us
    pallas_call x1, Pallas kernels, body(): pl.pallas_call(functools.partial(attend_kernel, [x.shape[0] for x in mine...  25.7 us
    ppermute x6, waiting for transfers between devices, along_x(): lax.ppermute(x, 'ctx', [(c, (c + 2 * step) % cycle) for c in range(cycle)])  18.8 us
    ppermute x6, starting transfers between devices, along_x(): lax.ppermute(x, 'ctx', [(c, (c + 2 * step) % cycle) for c in range(cycle)])  8.34 us
    ppermute x4, starting transfers between devices, swap(): return lax.ppermute(x, 'rows', [(r, r ^ 1) for r in range(groups)])  6.06 us
    ppermute x2, starting transfers between devices, along_z(): return lax.ppermute(x, 'ctx', [(c, c ^ 1) for c in range(cycle)])  2.95 us
  transfers between devices with their start and end apart: 12, of which 4 were waited for; matrix products, arithmetic and copies ran while one was open for 4% of the time, Pallas kernels for 2%

profile of v11, /device:TPU:1, one launch (start us, length us, event | category | flops | bytes accessed | tf_op | source)
XLA Modules:
  0.0 112.0 jit_solution(5247552870667858894)
XLA Ops:
  0.0 0.0 copy-start.3
  0.0 0.0 copy-start.4
  0.0 0.0 copy-start.5
  0.0 1.4 %dynamic-slice_select_fusion.block_ref = bf16[2048,128]{1,0:T(8,128)(2,1)S(1)} fusion(bf16[2048,1024]{1,0:T(8,128)(2,1)} %values, s32[]{:T(128)S(6)} %select_n.145, bf16[2048,1024]{1,0:T(8,128)(2,1)} %keys, pred[]{:T(512)S(6)} %eq.100), kind=kLoop, calls=%fused_computation.4 | loop fusion | flops 262144 | bytes 1572869 | tf_op jit(solution)/shard_map/jit(_where)/select_n | solution.py:272
  1.4 0.2 turn.1
  1.6 2.5 %collective-permute-start.2 = (bf16[2048,128]{1,0:T(8,128)(2,1)S(1)}, bf16[2048,128]{1,0:T(8,128)(2,1)S(1)}, u32[]{:S(2)}, u32[]{:S(2)}) collective-permute-start(bf16[2048,128]{1,0:T(8,128)(2,1)S(1)} %turn.1), channel_id=1, source_target_pairs={{0,16},{16,0},{32,48},{48,32},{64,80},{80,64},{96,112},{112,96},{1... | collective-permute-start | bytes 1572872 | tf_op jit(solution)/shard_map/ppermute | solution.py:283
  4.2 1.2 %collective-permute-start = (bf16[2048,128]{1,0:T(8,128)(2,1)S(1)}, bf16[2048,128]{1,0:T(8,128)(2,1)S(1)}, u32[]{:S(2)}, u32[]{:S(2)}) collective-permute-start(bf16[2048,128]{1,0:T(8,128)(2,1)S(1)} %turn.1), channel_id=1, source_target_pairs={{0,32},{16,48},{32,64},{48,80},{64,96},{80,112},{96,0},{112,16},{1... | collective-permute-start | bytes 1572872 | tf_op jit(solution)/shard_map/ppermute | solution.py:280
  5.4 0.0 copy-done.3
  5.4 1.2 %select_reduce_fusion.1 = (s32[128]{0:T(128)S(1)}, s32[128]{0:T(128)S(1)}) fusion(s32[2048]{0:T(1024)S(1)} %copy-done.3, s32[2048]{0:T(1024)S(1)} %add_select_fusion.5), kind=kLoop, calls=%fused_computation.1 | loop fusion | flops 1310464 | bytes 17408 | tf_op jit(solution)/shard_map/reduce_min | solution.py:291
  6.6 1.5 %collective-permute-start.1 = (bf16[2048,128]{1,0:T(8,128)(2,1)S(1)}, bf16[2048,128]{1,0:T(8,128)(2,1)S(1)}, u32[]{:S(2)}, u32[]{:S(2)}) collective-permute-start(bf16[2048,128]{1,0:T(8,128)(2,1)S(1)} %turn.1), channel_id=1, source_target_pairs={{0,96},{16,112},{32,0},{48,16},{64,32},{80,48},{96,64},{112,80},{1... | collective-permute-start | bytes 1572872 | tf_op jit(solution)/shard_map/ppermute | solution.py:280
  8.1 0.1 select_reduce_fusion.3.start
  8.3 0.0 copy-done.4
  8.3 0.1 broadcast_subtract_fusion
  8.4 0.0 copy-done.5
  8.4 0.1 pad_add_fusion
  8.4 0.8 and_reduce_fusion
  9.2 0.2 convert_reduce_fusion.2
  9.4 0.6 select_reduce_fusion
  10.1 0.1 reshape.230.counts
  10.2 2.2 %own.1 = (bf16[2048,128]{1,0:T(8,128)(2,1)}, bf16[2048,128]{1,0:T(8,128)(2,1)}) custom-call(bf16[2048,1024]{1,0:T(8,128)(2,1)} %keys, bf16[2048,1024]{1,0:T(8,128)(2,1)} %values), custom_call_target="tpu_custom_call" | custom-call | tf_op jit(solution)/shard_map/own/pallas_call | solution.py:300
  12.4 0.6 convert_reduce_fusion.1
  13.0 0.5 select_reduce_fusion.2
  13.5 4.3 %collective-permute-done = bf16[2048,128]{1,0:T(8,128)(2,1)S(1)} collective-permute-done((bf16[2048,128]{1,0:T(8,128)(2,1)S(1)}, bf16[2048,128]{1,0:T(8,128)(2,1)S(1)}, u32[]{:S(2)}, u32[]{:S(2)}) %collective-permute-start) | collective-permute-done | bytes 524320 | tf_op jit(solution)/shard_map/ppermute | solution.py:280
  17.8 0.4 collective-permute-start.5
  18.2 0.0 collective-permute-start.3
  18.3 0.0 collective-permute-done.2
  18.3 2.7 %collective-permute-start.4 = (bf16[2048,128]{1,0:T(8,128)(2,1)S(1)}, bf16[2048,128]{1,0:T(8,128)(2,1)S(1)}, u32[]{:S(2)}, u32[]{:S(2)}) collective-permute-start(bf16[2048,128]{1,0:T(8,128)(2,1)S(1)} %collective-permute-done.2), channel_id=1, source_target_pairs={{0,96},{16,112},{32,0},{48,16},{64,32},{80,48},{96,64},{112,80},{1... | collective-permute-start | bytes 1572872 | tf_op jit(solution)/shard_map/ppermute | solution.py:280
  21.0 0.0 collective-permute-done.1
  21.0 0.1 constant_dynamic-update-slice_fusion.1
  21.1 0.1 constant_dynamic-update-slice_fusion.rest_2_
  21.2 2.5 %collective-permute-start.8 = (bf16[6144,128]{1,0:T(8,128)(2,1)S(1)}, bf16[6144,128]{1,0:T(8,128)(2,1)S(1)}, u32[]{:S(2)}, u32[]{:S(2)}) collective-permute-start(bf16[6144,128]{1,0:T(8,128)(2,1)S(1)} %constant_dynamic-update-slice_fusion.rest_2_), channel_id=1, source_target_pairs={{0,1},{1,0},{2,3},{3,2},{4,5},{5,4},{6,7},{7,6},{8,9},{9,8},{10,11... | collective-permute-start | bytes 4718600 | tf_op jit(solution)/shard_map/ppermute | solution.py:286
  23.7 7.4 %collective-permute-done.3 = bf16[2048,128]{1,0:T(8,128)(2,1)S(1)} collective-permute-done((bf16[2048,128]{1,0:T(8,128)(2,1)S(1)}, bf16[2048,128]{1,0:T(8,128)(2,1)S(1)}, u32[]{:S(2)}, u32[]{:S(2)}) %collective-permute-start.3) | collective-permute-done | bytes 524320 | tf_op jit(solution)/shard_map/ppermute | solution.py:280
  31.1 0.0 copy-start
  31.1 0.0 copy-start.1
  31.1 0.0 copy-start.2
  31.1 0.0 collective-permute-done.4
  31.1 0.1 constant_dynamic-update-slice_fusion.4
  31.2 0.0 collective-permute-done.5
  31.2 0.1 constant_dynamic-update-slice_fusion.3.rest_3_
  31.3 2.8 %collective-permute-start.9 = (bf16[6144,128]{1,0:T(8,128)(2,1)S(1)}, bf16[6144,128]{1,0:T(8,128)(2,1)S(1)}, u32[]{:S(2)}, u32[]{:S(2)}) collective-permute-start(bf16[6144,128]{1,0:T(8,128)(2,1)S(1)} %constant_dynamic-update-slice_fusion.3.rest_3_), channel_id=1, source_target_pairs={{0,1},{1,0},{2,3},{3,2},{4,5},{5,4},{6,7},{7,6},{8,9},{9,8},{10,11... | collective-permute-start | bytes 4718600 | tf_op jit(solution)/shard_map/ppermute | solution.py:286
  34.1 0.1 collective-permute-start.6
  34.2 2.8 %collective-permute-start.7 = (bf16[896,128]{1,0:T(8,128)(2,1)S(1)}, bf16[896,128]{1,0:T(8,128)(2,1)S(1)}, u32[]{:S(2)}, u32[]{:S(2)}) collective-permute-start(bf16[896,128]{1,0:T(8,128)(2,1)S(1)} %slice.9), channel_id=1, source_target_pairs={{0,96},{16,112},{32,0},{48,16},{64,32},{80,48},{96,64},{112,80},{1... | collective-permute-start | bytes 688136 | tf_op jit(solution)/shard_map/ppermute | solution.py:280
  37.0 7.1 %collective-permute-done.6.rest_4_ = bf16[1152,128]{1,0:T(8,128)(2,1)S(1)} collective-permute-done((bf16[1152,128]{1,0:T(8,128)(2,1)S(1)}, bf16[1152,128]{1,0:T(8,128)(2,1)S(1)}, u32[]{:S(2)}, u32[]{:S(2)}) %collective-permute-start.6) | collective-permute-done | bytes 294944 | tf_op jit(solution)/shard_map/ppermute | solution.py:280
  44.1 0.8 collective-permute-start.10
  44.9 0.0 collective-permute-done.7.rest_5_
  44.9 0.0 collective-permute-start.11
  44.9 1.5 %collective-permute-done.11.rest_9_ = bf16[896,128]{1,0:T(8,128)(2,1)S(1)} collective-permute-done((bf16[896,128]{1,0:T(8,128)(2,1)S(1)}, bf16[896,128]{1,0:T(8,128)(2,1)S(1)}, u32[]{:S(2)}, u32[]{:S(2)}) %collective-permute-start.11) | collective-permute-done | bytes 229408 | tf_op jit(solution)/shard_map/ppermute | solution.py:286
  46.4 0.0 collective-permute-done.10.rest_8_
  46.4 0.0 collective-permute-done.8.rest_6_
  46.4 0.0 collective-permute-done.9.rest_7_
  46.4 0.0 copy-done
  46.4 0.0 copy-done.1
  46.4 0.0 copy-done.2
  46.5 25.7 %attend.1 = bf16[4096,256]{1,0:T(8,128)(2,1)S(1)} custom-call(s32[32,24]{1,0:T(8,128)S(1)} %bitcast.6, s32[32]{0:T(128)S(1)} %reshape.230.counts, s32[128]{0:T(128)S(1)} %get-tuple-element.26.sent, s32[128]{0:T(128)S(1)} %select_reduce_fusion.3.start, bf16[2048,256]{1,0:T(8,128)(2,1)S(1)} %copy-done, s32[1,2048]{1,0:T(1,128)S(1)} %bitcast.7, ...), custom_call_target="tpu_custom_call" | custom-call | tf_op jit(solution)/shard_map/attend/pallas_call | solution.py:325
  72.2 38.3 %all_to_all.5 = bf16[128,32,256]{2,1,0:T(8,128)(2,1)S(1)} all-to-all(bf16[128,32,256]{2,1,0:T(8,128)(2,1)S(1)} %bitcast.5), channel_id=1, replica_groups=mesh['ctx'=8,'rows'=16] {'ctx','rows'}, dimensions={0} | all-to-all | bytes 4194304 | tf_op jit(solution)/shard_map/all_to_all | solution.py:342
  110.4 1.6 %arrange.1 = bf16[128,4096]{1,0:T(8,128)(2,1)} custom-call(bf16[8,16,32,256]{3,2,1,0:T(8,128)(2,1)S(1)} %bitcast.4), custom_call_target="tpu_custom_call" | custom-call | tf_op jit(solution)/shard_map/arrange/pallas_call | solution.py:346
  (10 shorter events, 0.1 us)
Async XLA Ops:
  0.0 5.4 %copy-start.3 = (s32[2048]{0:T(1024)S(1)}, s32[2048]{0:T(1024)}, u32[]{:S(2)}) copy-start(s32[2048]{0:T(1024)} %param.11) | copy-start | bytes 24580
  0.0 8.3 %copy-start.4 = (s32[2,16]{1,0:T(2,128)S(1)}, s32[2,16]{1,0:T(2,128)}, u32[]{:S(2)}) copy-start(s32[2,16]{1,0:T(2,128)} %param.10) | copy-start | bytes 388
  0.0 8.3 %copy-start.5 = (s32[2,8]{1,0:T(2,128)S(1)}, s32[2,8]{1,0:T(2,128)}, u32[]{:S(2)}) copy-start(s32[2,8]{1,0:T(2,128)} %param.9) | copy-start | bytes 196
  1.6 16.7 %collective-permute-start.2 = (bf16[2048,128]{1,0:T(8,128)(2,1)S(1)}, bf16[2048,128]{1,0:T(8,128)(2,1)S(1)}, u32[]{:S(2)}, u32[]{:S(2)}) collective-permute-start(bf16[2048,128]{1,0:T(8,128)(2,1)S(1)} %turn.1), channel_id=1, source_target_pairs={{0,16},{16,0},{32,48},{48,32},{64,80},{80,64},{96,112},{112,96},{1... | collective-permute-start | bytes 1572872 | tf_op jit(solution)/shard_map/ppermute | solution.py:283
  4.2 13.7 %collective-permute-start = (bf16[2048,128]{1,0:T(8,128)(2,1)S(1)}, bf16[2048,128]{1,0:T(8,128)(2,1)S(1)}, u32[]{:S(2)}, u32[]{:S(2)}) collective-permute-start(bf16[2048,128]{1,0:T(8,128)(2,1)S(1)} %turn.1), channel_id=1, source_target_pairs={{0,32},{16,48},{32,64},{48,80},{64,96},{80,112},{96,0},{112,16},{1... | collective-permute-start | bytes 1572872 | tf_op jit(solution)/shard_map/ppermute | solution.py:280
  6.6 14.4 %collective-permute-start.1 = (bf16[2048,128]{1,0:T(8,128)(2,1)S(1)}, bf16[2048,128]{1,0:T(8,128)(2,1)S(1)}, u32[]{:S(2)}, u32[]{:S(2)}) collective-permute-start(bf16[2048,128]{1,0:T(8,128)(2,1)S(1)} %turn.1), channel_id=1, source_target_pairs={{0,96},{16,112},{32,0},{48,16},{64,32},{80,48},{96,64},{112,80},{1... | collective-permute-start | bytes 1572872 | tf_op jit(solution)/shard_map/ppermute | solution.py:280
  17.8 13.4 %collective-permute-start.5 = (bf16[2048,128]{1,0:T(8,128)(2,1)S(1)}, bf16[2048,128]{1,0:T(8,128)(2,1)S(1)}, u32[]{:S(2)}, u32[]{:S(2)}) collective-permute-start(bf16[2048,128]{1,0:T(8,128)(2,1)S(1)} %collective-permute-done), channel_id=1, source_target_pairs={{0,16},{16,0},{32,48},{48,32},{64,80},{80,64},{96,112},{112,96},{1... | collective-permute-start | bytes 1572872 | tf_op jit(solution)/shard_map/ppermute | solution.py:283
  18.2 12.8 %collective-permute-start.3 = (bf16[2048,128]{1,0:T(8,128)(2,1)S(1)}, bf16[2048,128]{1,0:T(8,128)(2,1)S(1)}, u32[]{:S(2)}, u32[]{:S(2)}) collective-permute-start(bf16[2048,128]{1,0:T(8,128)(2,1)S(1)} %collective-permute-done), channel_id=1, source_target_pairs={{0,32},{16,48},{32,64},{48,80},{64,96},{80,112},{96,0},{112,16},{1... | collective-permute-start | bytes 1572872 | tf_op jit(solution)/shard_map/ppermute | solution.py:280
  18.3 12.8 %collective-permute-start.4 = (bf16[2048,128]{1,0:T(8,128)(2,1)S(1)}, bf16[2048,128]{1,0:T(8,128)(2,1)S(1)}, u32[]{:S(2)}, u32[]{:S(2)}) collective-permute-start(bf16[2048,128]{1,0:T(8,128)(2,1)S(1)} %collective-permute-done.2), channel_id=1, source_target_pairs={{0,96},{16,112},{32,0},{48,16},{64,32},{80,48},{96,64},{112,80},{1... | collective-permute-start | bytes 1572872 | tf_op jit(solution)/shard_map/ppermute | solution.py:280
  21.2 25.2 %collective-permute-start.8 = (bf16[6144,128]{1,0:T(8,128)(2,1)S(1)}, bf16[6144,128]{1,0:T(8,128)(2,1)S(1)}, u32[]{:S(2)}, u32[]{:S(2)}) collective-permute-start(bf16[6144,128]{1,0:T(8,128)(2,1)S(1)} %constant_dynamic-update-slice_fusion.rest_2_), channel_id=1, source_target_pairs={{0,1},{1,0},{2,3},{3,2},{4,5},{5,4},{6,7},{7,6},{8,9},{9,8},{10,11... | collective-permute-start | bytes 4718600 | tf_op jit(solution)/shard_map/ppermute | solution.py:286
  31.1 15.4 %copy-start = (bf16[2048,256]{1,0:T(8,128)(2,1)S(1)}, bf16[2048,256]{1,0:T(8,128)(2,1)}, u32[]{:S(2)}) copy-start(bf16[2048,256]{1,0:T(8,128)(2,1)} %q_ref.1) | copy-start | bytes 3145732
  31.1 15.4 %copy-start.1 = (bf16[2048,128]{1,0:T(8,128)(2,1)S(1)}, bf16[2048,128]{1,0:T(8,128)(2,1)}, u32[]{:S(2)}) copy-start(bf16[2048,128]{1,0:T(8,128)(2,1)} %get-tuple-element.29.rest_0_) | copy-start | bytes 1572868
  31.1 15.3 %copy-start.2 = (bf16[2048,128]{1,0:T(8,128)(2,1)S(1)}, bf16[2048,128]{1,0:T(8,128)(2,1)}, u32[]{:S(2)}) copy-start(bf16[2048,128]{1,0:T(8,128)(2,1)} %get-tuple-element.30.rest_1_) | copy-start | bytes 1572868
  31.3 15.1 %collective-permute-start.9 = (bf16[6144,128]{1,0:T(8,128)(2,1)S(1)}, bf16[6144,128]{1,0:T(8,128)(2,1)S(1)}, u32[]{:S(2)}, u32[]{:S(2)}) collective-permute-start(bf16[6144,128]{1,0:T(8,128)(2,1)S(1)} %constant_dynamic-update-slice_fusion.3.rest_3_), channel_id=1, source_target_pairs={{0,1},{1,0},{2,3},{3,2},{4,5},{5,4},{6,7},{7,6},{8,9},{9,8},{10,11... | collective-permute-start | bytes 4718600 | tf_op jit(solution)/shard_map/ppermute | solution.py:286
  34.1 10.0 %collective-permute-start.6 = (bf16[1152,128]{1,0:T(8,128)(2,1)S(1)}, bf16[1152,128]{1,0:T(8,128)(2,1)S(1)}, u32[]{:S(2)}, u32[]{:S(2)}) collective-permute-start(bf16[1152,128]{1,0:T(8,128)(2,1)S(1)} %slice.8), channel_id=1, source_target_pairs={{0,32},{16,48},{32,64},{48,80},{64,96},{80,112},{96,0},{112,16},{1... | collective-permute-start | bytes 884744 | tf_op jit(solution)/shard_map/ppermute | solution.py:280
  34.2 10.6 %collective-permute-start.7 = (bf16[896,128]{1,0:T(8,128)(2,1)S(1)}, bf16[896,128]{1,0:T(8,128)(2,1)S(1)}, u32[]{:S(2)}, u32[]{:S(2)}) collective-permute-start(bf16[896,128]{1,0:T(8,128)(2,1)S(1)} %slice.9), channel_id=1, source_target_pairs={{0,96},{16,112},{32,0},{48,16},{64,32},{80,48},{96,64},{112,80},{1... | collective-permute-start | bytes 688136 | tf_op jit(solution)/shard_map/ppermute | solution.py:280
  44.1 2.3 %collective-permute-start.10 = (bf16[1152,128]{1,0:T(8,128)(2,1)S(1)}, bf16[1152,128]{1,0:T(8,128)(2,1)S(1)}, u32[]{:S(2)}, u32[]{:S(2)}) collective-permute-start(bf16[1152,128]{1,0:T(8,128)(2,1)S(1)} %collective-permute-done.6.rest_4_), channel_id=1, source_target_pairs={{0,1},{1,0},{2,3},{3,2},{4,5},{5,4},{6,7},{7,6},{8,9},{9,8},{10,11... | collective-permute-start | bytes 884744 | tf_op jit(solution)/shard_map/ppermute | solution.py:286
  44.9 1.5 %collective-permute-start.11 = (bf16[896,128]{1,0:T(8,128)(2,1)S(1)}, bf16[896,128]{1,0:T(8,128)(2,1)S(1)}, u32[]{:S(2)}, u32[]{:S(2)}) collective-permute-start(bf16[896,128]{1,0:T(8,128)(2,1)S(1)} %collective-permute-done.7.rest_5_), channel_id=1, source_target_pairs={{0,1},{1,0},{2,3},{3,2},{4,5},{5,4},{6,7},{7,6},{8,9},{9,8},{10,11... | collective-permute-start | bytes 688136 | tf_op jit(solution)/shard_map/ppermute | solution.py:286
